TPU v7x, 256 devices: a whole 4x4x8 slice. The times are simulated.
256 devices in a mesh: seq: 128 (over y_lo, z, x, core), ch: 2 (over y_hi).
Axes of the slice: x: 4, y: 4 (y_hi: 2, y_lo: 2; y = y_hi * 2 + y_lo), z: 8, core: 2. Of those that a mesh axis runs over, the one named last changes fastest.
Arguments:
- inputs: bfloat16 [2, 384, 262144], P(None, 'ch', 'seq'), may hold values from -6 to 6
- convolution_weight: bfloat16 [3, 384, 384], P(None, 'ch'), may hold values from -0.1875 to 0.1875
- conv_bias: float32 [384], P('ch'), may hold values from -3 to 3
- mix_weight: bfloat16 [384, 384], P('ch'), may hold values from -0.3125 to 0.3125
- cotangent: bfloat16 [2, 384, 262144], P(None, 'ch', 'seq'), may hold values from -6 to 6
Outputs:
- outputs: bfloat16 [2, 384, 262144], P(None, 'ch', 'seq')
- input_grad: bfloat16 [2, 384, 262144], P(None, 'ch', 'seq')
- conv_weight_grad: float32 [3, 384, 384], P(None, 'ch')
- conv_bias_grad: float32 [384], P('ch')
- mix_weight_grad: float32 [384, 384], P('ch')
All inputs are finite; a program needn't handle non-finite values.
Results may differ from a plain program's by a relative error of at most 0.007.
Values may be sent and summed in bfloat16 or wider, within the bound.
No kernel may reach another device: no remote copies, remote signals or barrier semaphores. Data moves between devices by JAX's collectives and lax.ppermute only.
A program may use at most 128 MiB of HBM per device.

v0:
```python
import math

import jax
import jax.numpy as jnp
from jax import lax
from jax.sharding import PartitionSpec as P


def shifted(block, axis, distance):
    devices = range(lax.axis_size(axis))
    route = [(i - distance, i) for i in devices if i - distance in devices]
    return lax.ppermute(block, axis, route)


def shift_inputs(receptive_field):
    later = shifted(receptive_field, "seq", 2)
    earlier = shifted(receptive_field, "seq", -2)
    return (later, earlier)


def shift_grads(receptive_field):
    later = shifted(receptive_field, "seq", 2)
    earlier = shifted(receptive_field, "seq", -2)
    return (later, earlier)


def tap_product(weight, receptive_field):
    return jnp.einsum("oi,bil->bol", weight, receptive_field, preferred_element_type=jnp.float32)


def tap_back(weight, receptive_field):
    return jnp.einsum("oi,bol->bil", weight, receptive_field, preferred_element_type=jnp.float32)


def gelu_grad(pre, upstream):
    return jax.vjp(jax.nn.gelu, pre)[1](upstream)[0]


def per_device(inputs, convolution_weight, conv_bias, mix_weight, cotangent):
    factor = 1.0 / math.sqrt(inputs.shape[0] * inputs.shape[2] * lax.axis_size("seq"))
    whole = lax.all_gather(inputs, "ch", axis=1, tiled=True)
    trailing_tap_slice, forward_tap_slice = shift_inputs(whole)
    pre = tap_product(convolution_weight[0], trailing_tap_slice) + tap_product(
        convolution_weight[1], whole
    )
    pre = pre + tap_product(convolution_weight[2], forward_tap_slice) + conv_bias[None, :, None]
    activated = jax.nn.gelu(pre).astype(jnp.bfloat16)
    act_whole = lax.all_gather(activated, "ch", axis=1, tiled=True)
    mix_out = jnp.einsum("om,bml->bol", mix_weight, act_whole, preferred_element_type=jnp.float32)
    outputs = (inputs.astype(jnp.float32) + mix_out).astype(jnp.bfloat16)
    mix_grad = jnp.einsum("bol,bml->om", cotangent, act_whole, preferred_element_type=jnp.float32)
    act_terms = jnp.einsum("om,bol->bml", mix_weight, cotangent, preferred_element_type=jnp.float32)
    grad_act = lax.psum_scatter(act_terms, "ch", scatter_dimension=1, tiled=True)
    preactivation_gradient = gelu_grad(pre, grad_act).astype(jnp.bfloat16)
    grad_behind, grad_ahead = shift_grads(preactivation_gradient)
    back_terms = tap_back(convolution_weight[0], grad_ahead) + tap_back(
        convolution_weight[1], preactivation_gradient
    )
    back_terms = back_terms + tap_back(convolution_weight[2], grad_behind)
    back_sum = lax.psum_scatter(back_terms, "ch", scatter_dimension=1, tiled=True)
    input_grad = (cotangent.astype(jnp.float32) + back_sum).astype(jnp.bfloat16)
    weight_grad = jnp.stack(
        [
            jnp.einsum(
                "bol,bil->oi",
                preactivation_gradient,
                trailing_tap_slice,
                preferred_element_type=jnp.float32,
            ),
            jnp.einsum(
                "bol,bil->oi", preactivation_gradient, whole, preferred_element_type=jnp.float32
            ),
            jnp.einsum(
                "bol,bil->oi",
                preactivation_gradient,
                forward_tap_slice,
                preferred_element_type=jnp.float32,
            ),
        ]
    )
    bias_grad = jnp.sum(preactivation_gradient.astype(jnp.float32), axis=(0, 2))
    weight_grad, mix_grad, bias_grad = lax.psum((weight_grad, mix_grad, bias_grad), "seq")
    return (outputs, input_grad, weight_grad * factor, bias_grad * factor, mix_grad * factor)


def solution(mesh):
    in_specs = (
        P(None, "ch", "seq"),
        P(None, "ch", None),
        P("ch"),
        P("ch", None),
        P(None, "ch", "seq"),
    )
    out_specs = (
        P(None, "ch", "seq"),
        P(None, "ch", "seq"),
        P(None, "ch", None),
        P("ch"),
        P("ch", None),
    )
    return jax.shard_map(
        per_device, mesh=mesh, in_specs=in_specs, out_specs=out_specs, check_vma=False
    )
```

profile of v0, /device:TPU:1, one launch (start us, length us, event | category | flops | bytes accessed | tf_op | source)
XLA Modules:
  0.0 1500.6 jit_solution(5448428080988921829)
XLA Ops:
  7.2 0.0 copy-start
  7.2 0.0 all-gather.3.cloned.1.call-start
  7.2 0.7 all-gather.3.cloned.1.call-update
  7.9 0.0 reduce-scatter.2.cloned.1.call-start
  8.0 0.1 copy-done
  8.1 5.1 convolution_bitcast_fusion
  13.2 0.0 copy-start.6
  13.2 0.0 reduce-scatter.2.cloned.1.call-update
  13.2 0.0 all-gather.5.cloned.1.call-start
  13.3 51.9 %all-gather.3.cloned.1.call-done = bf16[2,384,2048]{2,1,0:T(8,128)(2,1)} async-done(((bf16[2,192,2048]{2,1,0:T(8,128)(2,1)}), bf16[2,384,2048]{2,1,0:T(8,128)(2,1)}) %all-gather.3.cloned.1.call-update) | async-done | bytes 3145744 | tf_op jit(solution)/shard_map/all_gather | solution.py:41
  65.2 3.3 collective-permute-start
  68.5 1.3 collective-permute-start.1
  69.8 0.0 copy-done.6
  69.8 4.5 fusion.24
  74.3 0.0 copy-start.8
  74.3 61.0 %collective-permute-done = bf16[2,384,2048]{2,1,0:T(8,128)(2,1)S(1)} collective-permute-done((bf16[2,384,2048]{2,1,0:T(8,128)(2,1)}, bf16[2,384,2048]{2,1,0:T(8,128)(2,1)S(1)}, u32[]{:S(2)}, u32[]{:S(2)}) %collective-permute-start) | collective-permute-done | bytes 3145760 | tf_op jit(solution)/shard_map/ppermute | solution.py:12
  135.3 0.0 copy-start.2
  135.4 2.7 fusion.28
  138.0 0.0 copy-done.2
  138.0 1.3 collective-permute-done.1
  139.3 105.6 %reduce-scatter.2.cloned.1.call-done = f32[2,192,2048]{2,1,0:T(8,128)} async-done(((f32[2,384,2048]{2,1,0:T(8,128)}), f32[2,192,2048]{2,1,0:T(8,128)}) %reduce-scatter.2.cloned.1.call-update) | async-done | bytes 3145744 | tf_op jit(solution)/shard_map/reduce_scatter | solution.py:53
  245.0 0.0 copy-done.8
  245.0 9.0 convert_reduce_fusion
  254.0 0.0 all-gather.5.cloned.1.call-update
  254.0 0.0 all-reduce.7.cloned.1.call-start
  254.1 0.0 copy-start.3
  254.1 1.6 collective-permute-start.2
  255.6 5.2 collective-permute-start.3
  260.8 3.1 convolution_bitcast_fusion.2
  263.9 0.0 copy-done.3
  263.9 0.0 copy-start.1
  263.9 1.2 convolution_bitcast_fusion.4
  265.1 1.0 copy-done.1
  266.1 0.0 copy-start.5
  266.1 1.2 convolution_bitcast_fusion.3
  267.3 1.0 pad_maximum_fusion
  268.3 36.8 %all-gather.5.cloned.1.call-done = bf16[2,384,2048]{2,1,0:T(8,128)(2,1)} async-done(((bf16[2,192,2048]{2,1,0:T(8,128)(2,1)}), bf16[2,384,2048]{2,1,0:T(8,128)(2,1)}) %all-gather.5.cloned.1.call-update) | async-done | bytes 3145744 | tf_op jit(solution)/shard_map/all_gather | solution.py:48
  305.1 0.0 copy-done.5
  305.1 3.8 convolution_bitcast_fusion.1
  308.9 0.0 all-reduce.7.cloned.1.call-update
  308.9 0.2 all-reduce.5.cloned.1.call-start
  309.1 0.0 copy-start.7
  309.1 2.3 fusion.22
  311.4 0.0 collective-permute-done.2
  311.4 0.0 copy-done.7
  311.5 2.7 fusion.26
  314.2 0.0 collective-permute-done.3
  314.2 5.5 add_bitcast_fusion
  319.6 10.4 copy.15
  330.1 0.0 copy-start.9
  330.1 0.0 copy-start.4
  330.1 0.0 all-reduce.5.cloned.1.call-update
  330.1 0.6 copy-done.9
  330.8 0.6 dynamic-slice
  332.0 275.7 %psum.22 = f32[192]{0:T(256)S(1)} all-reduce(f32[192]{0:T(256)S(1)} %get-tuple-element.17), channel_id=1, replica_groups=mesh['seq'=128,'ch'=2] {'seq'}, use_global_device_ids=true, to_apply=%region_4.0 | all-reduce | flops 192 | bytes 1536 | tf_op jit(solution)/shard_map/psum | solution.py:82
  607.6 0.6 broadcast_multiply_fusion.2
  608.2 0.0 copy-done.4
  608.2 4.0 fusion.8
  612.3 709.9 %all-reduce.7.cloned.1.call-done = (f32[3,192,384]{2,1,0:T(8,128)}, f32[192,384]{1,0:T(8,128)}) async-done(((f32[3,192,384]{2,1,0:T(8,128)}, f32[192,384]{1,0:T(8,128)}), (f32[3,192,384]{2,1,0:T(8,128)}, f32[192,384]{1,0:T(8,128)})) %all-reduce.7.cloned.1.call-update) | async-done | bytes 1179664 | tf_op jit(solution)/shard_map/psum | solution.py:82
  1322.1 1.7 broadcast_multiply_fusion.1
  1323.8 2.2 broadcast_multiply_fusion
  1326.0 162.2 %all-reduce.5.cloned.1.call-done = f32[2,384,2048]{2,0,1:T(2,128)} async-done(((f32[2,384,2048]{2,0,1:T(2,128)}), f32[2,384,2048]{2,0,1:T(2,128)}) %all-reduce.5.cloned.1.call-update) | async-done | bytes 6291472
  1488.2 4.1 fusion.7
  1492.3 1.8 copy.16
Async XLA Ops:
  7.2 0.9 copy-start
  7.2 58.0 %all-gather.3.cloned.1.call-start = ((), (), s32[]{:S(2)}) async-start(), calls=%async_computation.1 | async-start | bytes 4718592 | tf_op jit(solution)/shard_map/all_gather | solution.py:41
  7.9 237.0 %reduce-scatter.2.cloned.1.call-start = ((), (), s32[]{:S(2)}) async-start(), calls=%async_computation.3 | async-start | bytes 9437184 | tf_op jit(solution)/shard_map/reduce_scatter | solution.py:53
  13.2 56.6 %copy-start.6 = (bf16[3,192,384]{2,1,0:T(8,128)(2,1)S(1)}, bf16[3,192,384]{2,1,0:T(8,128)(2,1)}, u32[]{:S(2)}) copy-start(bf16[3,192,384]{2,1,0:T(8,128)(2,1)} %param.6) | copy-start | bytes 1327108
  13.2 291.9 %all-gather.5.cloned.1.call-start = ((), (), s32[]{:S(2)}) async-start(), calls=%async_computation.2 | async-start | bytes 4718592 | tf_op jit(solution)/shard_map/all_gather | solution.py:48
  65.2 70.2 %collective-permute-start = (bf16[2,384,2048]{2,1,0:T(8,128)(2,1)}, bf16[2,384,2048]{2,1,0:T(8,128)(2,1)S(1)}, u32[]{:S(2)}, u32[]{:S(2)}) collective-permute-start(bf16[2,384,2048]{2,1,0:T(8,128)(2,1)} %all-gather.3.cloned.1.call-done), channel_id=1, source_target_pairs={{0,4},{2,6},{4,8},{6,10},{8,12},{10,14},{12,16},{14,18},{16,20},{1... | collective-permute-start | bytes 9437192 | tf_op jit(solution)/shard_map/ppermute | solution.py:12
  68.5 70.9 %collective-permute-start.1 = (bf16[2,384,2048]{2,1,0:T(8,128)(2,1)}, bf16[2,384,2048]{2,1,0:T(8,128)(2,1)}, u32[]{:S(2)}, u32[]{:S(2)}) collective-permute-start(bf16[2,384,2048]{2,1,0:T(8,128)(2,1)} %all-gather.3.cloned.1.call-done), channel_id=1, source_target_pairs={{4,0},{6,2},{8,4},{10,6},{12,8},{14,10},{16,12},{18,14},{20,16},{2... | collective-permute-start | bytes 9437192 | tf_op jit(solution)/shard_map/ppermute | solution.py:12
  74.3 170.6 %copy-start.8 = (f32[192]{0:T(256)S(1)}, f32[192]{0:T(256)}, u32[]{:S(2)}) copy-start(f32[192]{0:T(256)} %param.7) | copy-start | bytes 2308
  135.3 2.7 copy-start.2
  254.0 1068.1 %all-reduce.7.cloned.1.call-start = ((), (), s32[]{:S(2)}) async-start(), calls=%async_computation.5 | async-start | bytes 2359296 | tf_op jit(solution)/shard_map/psum | solution.py:82
  254.1 9.8 copy-start.3
  254.1 57.4 %collective-permute-start.2 = (bf16[2,192,2048]{2,1,0:T(8,128)(2,1)S(1)}, bf16[2,192,2048]{2,1,0:T(8,128)(2,1)}, u32[]{:S(2)}, u32[]{:S(2)}) collective-permute-start(bf16[2,192,2048]{2,1,0:T(8,128)(2,1)S(1)} %get-tuple-element.18), channel_id=1, source_target_pairs={{4,0},{6,2},{8,4},{10,6},{12,8},{14,10},{16,12},{18,14},{20,16},{2... | collective-permute-start | bytes 4718600 | tf_op jit(solution)/shard_map/ppermute | solution.py:12
  255.6 58.6 %collective-permute-start.3 = (bf16[2,192,2048]{2,1,0:T(8,128)(2,1)S(1)}, bf16[2,192,2048]{2,1,0:T(8,128)(2,1)}, u32[]{:S(2)}, u32[]{:S(2)}) collective-permute-start(bf16[2,192,2048]{2,1,0:T(8,128)(2,1)S(1)} %get-tuple-element.18), channel_id=1, source_target_pairs={{0,4},{2,6},{4,8},{6,10},{8,12},{10,14},{12,16},{14,18},{16,20},{1... | collective-permute-start | bytes 4718600 | tf_op jit(solution)/shard_map/ppermute | solution.py:12
  263.9 2.2 copy-start.1
  266.1 39.0 %copy-start.5 = (bf16[2,192,2048]{2,1,0:T(8,128)(2,1)S(1)}, bf16[2,192,2048]{2,1,0:T(8,128)(2,1)}, u32[]{:S(2)}) copy-start(bf16[2,192,2048]{2,1,0:T(8,128)(2,1)} %param.9) | copy-start | bytes 4718596
  308.9 1179.3 %all-reduce.5.cloned.1.call-start = ((), (), s32[]{:S(2)}) async-start(), calls=%async_computation.4 | async-start | bytes 12582912
  309.1 2.3 copy-start.7
  330.1 0.7 copy-start.9
  330.1 278.1 %copy-start.4 = (bf16[2,192,2048]{2,1,0:T(8,128)(2,1)S(1)}, bf16[2,192,2048]{2,1,0:T(8,128)(2,1)}, u32[]{:S(2)}) copy-start(bf16[2,192,2048]{2,1,0:T(8,128)(2,1)} %param.5) | copy-start | bytes 4718596
Sparse Core Ops, SparseCore 0:
  9.8 55.3 all-gather.2
  67.7 177.1 reduce-scatter.1
  254.1 50.9 all-gather.4
  309.0 1013.0 all-reduce.6
  1324.7 163.4 all-reduce.4
where the time goes:
time: 1500 us
  waiting for transfers between devices  1130 us (75%)
  blocking collectives  276 us (18%)
  matrix products  45.1 us (3%)
    psum x1, waiting for transfers between devices, per_device(): lax.psum((weight_grad, mix_grad, bias_grad), 'seq')  710 us
    psum x1, blocking collectives, per_device(): lax.psum((weight_grad, mix_grad, bias_grad), 'seq')  276 us
    unnamed x6, waiting for transfers between devices  163 us
    reduce_scatter x1, waiting for transfers between devices, per_device(): lax.psum_scatter(act_terms, 'ch', scatter_dimension=1, tiled=True)  106 us
    ppermute x4, waiting for transfers between devices, shifted(): return lax.ppermute(block, axis, route)  62.3 us
    all_gather x1, waiting for transfers between devices, per_device(): whole = lax.all_gather(inputs, 'ch', axis=1, tiled=True)  51.9 us
    all_gather x1, waiting for transfers between devices, per_device(): act_whole = lax.all_gather(activated, 'ch', axis=1, tiled=True)  36.8 us
  transfers between devices with their start and end apart: 9, of which 7 were waited for; matrix products, arithmetic and copies ran while one was open for 3% of the time, Pallas kernels for 0%

commit v1 on v0

v1 whole, which is shorter than its diff:
```python
import math

import jax
import jax.numpy as jnp
from jax import lax
from jax.experimental import pallas as pl
from jax.experimental.pallas import tpu as pltpu
from jax.sharding import PartitionSpec as P

BF16, F32 = jnp.bfloat16, jnp.float32
AXES = ("seq", "ch")
CHUNKS = 2
SIZE = 1024 // CHUNKS
TILE = 512
ROOT = math.sqrt(2.0 / math.pi)
CUBE = 0.044715


def route(target):
    pairs = []
    for s in range(128):
        for h in range(2):
            to = target(s, h)
            pairs.append((2 * s + h, 2 * to[0] + to[1]))
    return pairs


def send(block, target):
    return lax.ppermute(block, AXES, route(target))


def other_ch(s, h):
    return s, 1 - h


def other_core(s, h):
    return s ^ 1, h


def along_x(step):
    return lambda s, h: ((s & ~6) | ((((s >> 1) + step) & 3) << 1), h)


def flip(bits):
    return lambda s, h: (s ^ bits, h)


def chips_on(step):
    return lambda s, h: ((s & 64) | ((s + 2 * step) & 63), h)


def column_groups():
    return [[2 * (64 * (y & 1) + place) + (y >> 1) for y in range(4)] for place in range(64)]


def exchange(block):
    return lax.all_to_all(block, AXES, 0, 0, axis_index_groups=column_groups())


def dot(a, b, dims=((1,), (0,))):
    return lax.dot_general(a, b, (dims, ((), ())), preferred_element_type=F32)


def params(megabytes=28):
    return pltpu.CompilerParams(vmem_limit_bytes=megabytes * 2**20)


def copy_kernel(source, target):
    target[...] = source[...]


def pack(array, k):
    block = (1, 192, SIZE)
    return pl.pallas_call(
        copy_kernel,
        grid=(4,),
        in_specs=[pl.BlockSpec(block, lambda d: (d // 2, 0, (d % 2) * CHUNKS + k))],
        out_specs=pl.BlockSpec(block, lambda d: (d, 0, 0)),
        out_shape=jax.ShapeDtypeStruct((4, 192, SIZE), BF16),
        compiler_params=params(),
        cost_estimate=pl.CostEstimate(flops=0, bytes_accessed=16 * 192 * SIZE, transcendentals=0),
    )(array)


def unpack_kernel(*refs):
    for k, source in enumerate(refs[:-1]):
        width = source.shape[2]
        refs[-1][:, :, k * width : (k + 1) * width] = source[...]


def unpack(pieces):
    width = pieces[0].shape[2]
    return pl.pallas_call(
        unpack_kernel,
        grid=(4,),
        in_specs=[pl.BlockSpec((1, 192, width), lambda d: (d, 0, 0))] * len(pieces),
        out_specs=pl.BlockSpec((1, 192, 1024), lambda d: (d // 2, 0, d % 2)),
        out_shape=jax.ShapeDtypeStruct((2, 192, 2048), BF16),
        compiler_params=params(),
        cost_estimate=pl.CostEstimate(flops=0, bytes_accessed=16 * 192 * 1024, transcendentals=0),
    )(*pieces)


def weights_kernel(taps, mix, bias, out):
    for k in range(3):
        out[:, 384 * k : 384 * (k + 1)] = taps[k]
    out[:, 1152:1536] = mix[...]
    value = jnp.broadcast_to(bias[...], (192, 128))
    high = value.astype(BF16).astype(F32)
    middle = (value - high).astype(BF16).astype(F32)
    low = value - high - middle
    lane = lax.broadcasted_iota(jnp.int32, (192, 128), 1)
    split = jnp.where(lane == 0, high, jnp.where(lane == 1, middle, jnp.where(lane == 2, low, 0.0)))
    out[:, 1536:1664] = split.astype(BF16)


def pack_weights(taps, mix, bias):
    return pl.pallas_call(
        weights_kernel,
        out_shape=jax.ShapeDtypeStruct((192, 1664), BF16),
        compiler_params=params(),
    )(taps, mix, bias.reshape(192, 1))


def rows(ref):
    return ref[...].reshape(384, TILE)


def masked(ref, keep):
    return jnp.where(keep == 1, rows(ref), jnp.zeros((384, TILE), BF16))


def middle_kernel(edge, behind, here, ahead, cot, weights, *refs):
    so_far, (out, grad_pre, sums) = refs[:-3], refs[-3:]
    group = pl.program_id(0)

    @pl.when((group == 0) & (pl.program_id(1) == 0))
    def _():
        sums[...] = so_far[0][...] if so_far else jnp.zeros((384, 1664), F32)

    center = rows(here)
    field = jnp.concatenate(
        [masked(behind, edge[2 + group]), center, masked(ahead, edge[6 + group])], axis=0
    )
    bias = weights[:, 1536:1664].astype(F32)
    bias = bias[:, 0:1] + bias[:, 1:2] + bias[:, 2:3]
    pre = dot(weights[:, 0:1152], field) + bias
    square = pre * pre
    bent = jnp.tanh(ROOT * pre * (1.0 + CUBE * square))
    half = 0.5 * (1.0 + bent)
    act = (pre * half).astype(BF16)
    slope = half + 0.5 * pre * (1.0 - bent * bent) * (ROOT * (1.0 + 3.0 * CUBE * square))
    mix = weights[:, 1152:1536]
    out[...] = (center.astype(F32) + dot(mix, act)).astype(BF16).reshape(out.shape)
    upstream = rows(cot)
    grad = (dot(mix, upstream, ((0,), (0,))) * slope).astype(BF16)
    grad_pre[...] = grad.reshape(grad_pre.shape)
    last = ((1,), (1,))
    sums[:, 0:1152] += dot(grad, field, last)
    sums[:, 1152:1536] += dot(upstream, act, last)
    sums[:, 1536:1664] += jnp.broadcast_to(
        jnp.sum(grad.astype(F32), axis=1, keepdims=True), (384, 128)
    )


def tile_specs():
    block = (2, 1, 192, TILE)
    plain = pl.BlockSpec(block, lambda g, i, edge: (0, g, 0, i))
    behind = pl.BlockSpec(block, lambda g, i, edge: (0, edge[g], 0, i))
    ahead = pl.BlockSpec(block, lambda g, i, edge: (0, edge[4 + g], 0, i))
    return plain, behind, ahead


def whole(array):
    return pl.BlockSpec(array.shape, lambda g, i, edge: (0,) * array.ndim)


def middle(edge, behind, here, ahead, cot, weights, *so_far):
    plain, before, after = tile_specs()
    sums = jax.ShapeDtypeStruct((384, 1664), F32)
    field = jax.ShapeDtypeStruct((2, 2, 192, SIZE), BF16)
    return pl.pallas_call(
        middle_kernel,
        grid_spec=pltpu.PrefetchScalarGridSpec(
            num_scalar_prefetch=1,
            grid=(2, SIZE // TILE),
            in_specs=[before, plain, after, plain, whole(weights)] + [whole(a) for a in so_far],
            out_specs=[plain, plain, whole(sums)],
        ),
        out_shape=[field, field, sums],
        compiler_params=params(),
        cost_estimate=pl.CostEstimate(
            flops=36 * 384 * 384 * SIZE, bytes_accessed=24 * 384 * SIZE, transcendentals=768 * SIZE
        ),
    )(edge, behind, here, ahead, cot, weights, *so_far)


def back_kernel(edge, behind, here, ahead, cot, weights, out, taps):
    group = pl.program_id(0)

    @pl.when((group == 0) & (pl.program_id(1) == 0))
    def _():
        for k in range(3):
            tap = weights[:, 384 * (2 - k) : 384 * (3 - k)]
            taps[:, 384 * k : 384 * (k + 1)] = tap.T

    field = jnp.concatenate(
        [masked(behind, edge[2 + group]), rows(here), masked(ahead, edge[6 + group])], axis=0
    )
    result = (rows(cot).astype(F32) + dot(taps[...], field)).astype(BF16)
    out[...] = result.reshape(out.shape)


def back(edge, behind, here, ahead, cot, weights):
    plain, before, after = tile_specs()
    return pl.pallas_call(
        back_kernel,
        grid_spec=pltpu.PrefetchScalarGridSpec(
            num_scalar_prefetch=1,
            grid=(2, SIZE // TILE),
            in_specs=[before, plain, after, plain, whole(weights)],
            out_specs=plain,
            scratch_shapes=[pltpu.VMEM((384, 1152), BF16)],
        ),
        out_shape=jax.ShapeDtypeStruct((2, 2, 192, SIZE), BF16),
        compiler_params=params(),
        cost_estimate=pl.CostEstimate(
            flops=12 * 384 * 384 * SIZE, bytes_accessed=20 * 384 * SIZE, transcendentals=0
        ),
    )(edge, behind, here, ahead, cot, weights)


def pick(array, index, axis):
    return lax.dynamic_index_in_dim(array, index, axis, keepdims=False)


def choose(choices, index):
    found = choices[0]
    for k in range(1, len(choices)):
        found = jnp.where(index == k, choices[k], found)
    return found


def sum_over_devices(sums, factor):
    place, half = lax.axis_index("seq"), lax.axis_index("ch")
    core, x = place & 1, (place >> 1) & 3
    parts = sums.reshape(2, 2, 4, 24, 1664)
    both = pick(parts, core, 1) + send(pick(parts, 1 - core, 1), other_core)
    mine = pick(both, half, 0) + send(pick(both, 1 - half, 0).astype(BF16), other_ch).astype(F32)
    total = pick(mine, x, 0)
    for step in (1, 2, 3):
        part = pick(mine, (x + step) & 3, 0).astype(BF16)
        total = total + send(part, along_x(step)).astype(F32)
    for a, b in ((64, 8), (16, 32)):
        own = total.astype(BF16)
        first, second, third = (send(own, flip(m)).astype(F32) for m in (a, b, a ^ b))
        total = (own.astype(F32) + first) + (second + third)
    total = (total * factor).astype(BF16)
    found = [total] + [send(total, along_x(step)) for step in (1, 2, 3)]
    gathered = jnp.stack([choose(found, (x - to) & 3) for to in range(4)])
    across = send(gathered, other_core)
    first = jnp.where(core == 0, gathered, across)
    second = jnp.where(core == 0, across, gathered)
    return jnp.concatenate([first, second]).reshape(192, 1664).astype(F32)


def edges(chip):
    first, final = (chip == 0).astype(jnp.int32), (chip == 31).astype(jnp.int32)
    one, zero = jnp.int32(1), jnp.int32(0)
    return jnp.stack([zero, 1 - first, 1 - first, one, final, one, one, 1 - final])


def per_device(inputs, convolution_weight, conv_bias, mix_weight, cotangent):
    factor = 1.0 / math.sqrt(inputs.shape[0] * inputs.shape[2] * lax.axis_size("seq"))
    edge = edges((lax.axis_index("seq") >> 1) & 31)
    field = (2, 2, 192, SIZE)
    here = [exchange(pack(inputs, k)).reshape(field) for k in range(CHUNKS)]
    weights = pack_weights(convolution_weight, mix_weight, conv_bias)
    weights = lax.all_gather(weights, "ch", axis=0, tiled=True)
    cot = [exchange(pack(cotangent, k)).reshape(field) for k in range(CHUNKS)]
    sides = [(send(a, chips_on(1)), send(a, chips_on(-1))) for a in here]
    sums, outs, grads, grad_sides = (), [], [], []
    for k in range(CHUNKS):
        out, grad, *sums = middle(edge, sides[k][0], here[k], sides[k][1], cot[k], weights, *sums)
        outs.append(out)
        grads.append(grad)
        grad_sides.append((send(grad, chips_on(1)), send(grad, chips_on(-1))))

    def spread(pieces):
        return unpack([exchange(p.reshape(4, 192, p.shape[3])) for p in pieces])

    outputs = spread(outs)
    input_grad = spread(
        [
            back(edge, grad_sides[k][0], grads[k], grad_sides[k][1], cot[k], weights)
            for k in range(CHUNKS)
        ]
    )
    found = sum_over_devices(sums[0], factor)
    weight_grad = jnp.stack([found[:, 0:384], found[:, 384:768], found[:, 768:1152]])
    return outputs, input_grad, weight_grad, found[:, 1536], found[:, 1152:1536]


def solution(mesh):
    in_specs = (
        P(None, "ch", "seq"),
        P(None, "ch", None),
        P("ch"),
        P("ch", None),
        P(None, "ch", "seq"),
    )
    out_specs = (
        P(None, "ch", "seq"),
        P(None, "ch", "seq"),
        P(None, "ch", None),
        P("ch"),
        P("ch", None),
    )
    return jax.shard_map(
        per_device, mesh=mesh, in_specs=in_specs, out_specs=out_specs, check_vma=False
    )
```

time: 1500 us -> 213 us (0.14)
  the two profiles are of different devices: /device:TPU:1 before, /device:TPU:34 now
where the time goes in v1:
time: 213 us; the launch traced here: 212 us
  starting transfers between devices  82.2 us (39%)
  waiting for transfers between devices  58.7 us (28%)
  Pallas kernels  32.7 us (15%)
  local copies, waits for them, and re-layouts  19.7 us (9%)
  between operations  14.4 us (7%)
  other arithmetic  4.47 us (2%)
    ppermute x23, starting transfers between devices, send(): return lax.ppermute(block, AXES, route(target))  50.1 us
    all_to_all x8, waiting for transfers between devices, exchange(): return lax.all_to_all(block, AXES, 0, 0, axis_index_groups=column_groups())  37.2 us
    all_to_all x8, starting transfers between devices, exchange(): return lax.all_to_all(block, AXES, 0, 0, axis_index_groups=column_groups())  32 us
    unnamed x50, local copies, waits for them, and re-layouts  17.8 us
    pallas_call x2, Pallas kernels, middle(): pl.pallas_call(middle_kernel, grid_spec=pltpu.PrefetchScalarGridSpec(num_...  13.4 us
    ppermute x23, waiting for transfers between devices, send(): return lax.ppermute(block, AXES, route(target))  13.1 us
    all_gather x1, waiting for transfers between devices, per_device(): weights = lax.all_gather(weights, 'ch', axis=0, tiled=True)  8.4 us
    pallas_call x2, Pallas kernels, back(): pl.pallas_call(back_kernel, grid_spec=pltpu.PrefetchScalarGridSpec(num_sc...  7.01 us
  transfers between devices with their start and end apart: 32, of which 9 were waited for; matrix products, arithmetic and copies ran while one was open for 1% of the time, Pallas kernels for 12%

profile of v1, /device:TPU:34, one launch (start us, length us, event | category | flops | bytes accessed | tf_op | source)
XLA Modules:
  0.0 212.1 jit_solution(15236043582945930630)
XLA Ops:
  7.2 1.4 copy-done
  8.6 1.5 shard_map.96
  10.1 4.6 %all-to-all-start.3 = ((bf16[4,192,512]{2,1,0:T(8,128)(2,1)}), bf16[4,192,512]{2,1,0:T(8,128)(2,1)S(1)}, u32[]{:S(2)}, u32[]{:S(2)}) async-start(bf16[4,192,512]{2,1,0:T(8,128)(2,1)} %shard_map.96), calls=%async_computation.3 | async-start | bytes 1572864 | tf_op jit(solution)/shard_map/all_to_all | solution.py:57
  14.7 1.5 shard_map.92
  16.2 10.8 %all-to-all-done.3 = bf16[4,192,512]{2,1,0:T(8,128)(2,1)S(1)} async-done(((bf16[4,192,512]{2,1,0:T(8,128)(2,1)}), bf16[4,192,512]{2,1,0:T(8,128)(2,1)S(1)}, u32[]{:S(2)}, u32[]{:S(2)}) %all-to-all-start.3) | async-done | bytes 786464 | tf_op jit(solution)/shard_map/all_to_all | solution.py:57
  27.0 3.5 %all-to-all-start = ((bf16[4,192,512]{2,1,0:T(8,128)(2,1)}), bf16[4,192,512]{2,1,0:T(8,128)(2,1)S(1)}, u32[]{:S(2)}, u32[]{:S(2)}) async-start(bf16[4,192,512]{2,1,0:T(8,128)(2,1)} %shard_map.92), calls=%async_computation | async-start | bytes 1572864 | tf_op jit(solution)/shard_map/all_to_all | solution.py:57
  30.7 1.1 copy-done.19
  31.8 0.9 shard_map.94
  32.8 1.5 shard_map.93
  34.3 7.5 %all-to-all-done = bf16[4,192,512]{2,1,0:T(8,128)(2,1)S(1)} async-done(((bf16[4,192,512]{2,1,0:T(8,128)(2,1)}), bf16[4,192,512]{2,1,0:T(8,128)(2,1)S(1)}, u32[]{:S(2)}, u32[]{:S(2)}) %all-to-all-start) | async-done | bytes 786464 | tf_op jit(solution)/shard_map/all_to_all | solution.py:57
  41.8 0.9 copy-done.15
  42.7 3.5 %all-to-all-start.1 = ((bf16[4,192,512]{2,1,0:T(8,128)(2,1)}), bf16[4,192,512]{2,1,0:T(8,128)(2,1)S(1)}, u32[]{:S(2)}, u32[]{:S(2)}) async-start(bf16[4,192,512]{2,1,0:T(8,128)(2,1)} %shard_map.93), calls=%async_computation.1 | async-start | bytes 1572864 | tf_op jit(solution)/shard_map/all_to_all | solution.py:57
  46.2 0.6 collective-permute-start.1
  46.8 1.5 collective-permute-start
  48.3 0.8 collective-permute-start.3
  49.1 1.2 collective-permute-start.2
  50.3 1.6 shard_map.97
  51.9 11.4 %all-to-all-done.1 = bf16[4,192,512]{2,1,0:T(8,128)(2,1)S(1)} async-done(((bf16[4,192,512]{2,1,0:T(8,128)(2,1)}), bf16[4,192,512]{2,1,0:T(8,128)(2,1)S(1)}, u32[]{:S(2)}, u32[]{:S(2)}) %all-to-all-start.1) | async-done | bytes 786464 | tf_op jit(solution)/shard_map/all_to_all | solution.py:57
  63.3 3.5 %all-to-all-start.4 = ((bf16[4,192,512]{2,1,0:T(8,128)(2,1)}), bf16[4,192,512]{2,1,0:T(8,128)(2,1)S(1)}, u32[]{:S(2)}, u32[]{:S(2)}) async-start(bf16[4,192,512]{2,1,0:T(8,128)(2,1)} %shard_map.97), calls=%async_computation.4 | async-start | bytes 1572864 | tf_op jit(solution)/shard_map/all_to_all | solution.py:57
  66.9 8.4 %all-gather.2.cloned.1.call-done.weights = bf16[384,1664]{1,0:T(8,128)(2,1)} async-done(((bf16[192,1664]{1,0:T(8,128)(2,1)}), bf16[384,1664]{1,0:T(8,128)(2,1)}) %all-gather.2.cloned.1.call-update) | async-done | bytes 1277968 | tf_op jit(solution)/shard_map/all_gather | solution.py:279
  75.3 1.3 copy-done.3
  76.6 1.1 copy-done.16
  77.8 7.1 %shard_map.95 = (bf16[2,2,192,512]{3,2,1,0:T(8,128)(2,1)}, bf16[2,2,192,512]{3,2,1,0:T(8,128)(2,1)}, f32[384,1664]{1,0:T(8,128)S(1)}) custom-call(s32[8]{0:T(128)S(1)} %stack.43.edge, bf16[2,2,192,512]{3,2,1,0:T(8,128)(2,1)} %collective-permute-done.behind, bf16[2,2,192,512]{3,2,1,0:T(8,128)(2,1)S(1)} %bitcast.66, ...), custom_call_target="tpu_custom_call" | custom-call | flops 2717908992 | bytes 4718592 | tf_op jit(solution)/shard_map/pallas_call | solution.py:182
  84.9 1.4 copy-done.21
  86.4 1.4 copy-done.14
  87.8 1.7 copy-done.22
  89.5 6.3 %shard_map.98 = (bf16[2,2,192,512]{3,2,1,0:T(8,128)(2,1)S(1)}, bf16[2,2,192,512]{3,2,1,0:T(8,128)(2,1)S(1)}, f32[384,1664]{1,0:T(8,128)S(1)}) custom-call(s32[8]{0:T(128)S(1)} %stack.43.edge, bf16[2,2,192,512]{3,2,1,0:T(8,128)(2,1)} %collective-permute-done.2.behind, bf16[2,2,192,512]{3,2,1,0:T(8,128)(2,1)S(1)} %bitcast.63, ...), custom_call_target="tpu_custom_call" | custom-call | flops 2717908992 | bytes 4718592 | tf_op jit(solution)/shard_map/pallas_call | solution.py:182
  95.8 1.4 copy-done.11
  97.8 3.1 %collective-permute-done.8 = f32[2,4,24,1664]{3,2,1,0:T(8,128)} collective-permute-done((f32[2,4,24,1664]{3,2,1,0:T(8,128)S(1)}, f32[2,4,24,1664]{3,2,1,0:T(8,128)}, u32[]{:S(2)}, u32[]{:S(2)}) %collective-permute-start.8) | collective-permute-done | bytes 1277984 | tf_op jit(solution)/shard_map/ppermute | solution.py:29
  100.9 1.8 bitcast_add_fusion
  103.7 3.9 %all-to-all-start.2 = ((bf16[4,192,512]{2,1,0:T(8,128)(2,1)}), bf16[4,192,512]{2,1,0:T(8,128)(2,1)S(1)}, u32[]{:S(2)}, u32[]{:S(2)}) async-start(bf16[4,192,512]{2,1,0:T(8,128)(2,1)} %bitcast.6), calls=%async_computation.2 | async-start | bytes 1572864 | tf_op jit(solution)/shard_map/all_to_all | solution.py:57
  107.6 7.1 %collective-permute-done.9 = bf16[4,24,1664]{2,1,0:T(8,128)(2,1)S(1)} collective-permute-done((bf16[4,24,1664]{2,1,0:T(8,128)(2,1)S(1)}, bf16[4,24,1664]{2,1,0:T(8,128)(2,1)S(1)}, u32[]{:S(2)}, u32[]{:S(2)}) %collective-permute-start.9) | collective-permute-done | bytes 319520 | tf_op jit(solution)/shard_map/ppermute | solution.py:29
  114.7 1.1 bitcast_add_fusion.1
  115.9 1.5 collective-permute-start.10
  117.5 0.6 collective-permute-start.12
  118.0 2.1 collective-permute-start.11
  120.1 1.5 collective-permute-start.5
  121.6 0.6 collective-permute-start.4
  122.1 0.6 collective-permute-done.12
  122.7 2.3 %collective-permute-done.11 = bf16[24,1664]{1,0:T(8,128)(2,1)S(1)} collective-permute-done((bf16[24,1664]{1,0:T(8,128)(2,1)S(1)}, bf16[24,1664]{1,0:T(8,128)(2,1)S(1)}, u32[]{:S(2)}, u32[]{:S(2)}) %collective-permute-start.11) | collective-permute-done | bytes 79904 | tf_op jit(solution)/shard_map/ppermute | solution.py:29
  125.0 4.4 %collective-permute-start.15 = (bf16[24,1664]{1,0:T(8,128)(2,1)S(1)}, bf16[24,1664]{1,0:T(8,128)(2,1)S(1)}, u32[]{:S(2)}, u32[]{:S(2)}) collective-permute-start(bf16[24,1664]{1,0:T(8,128)(2,1)S(1)} %fusion.3), channel_id=1, source_target_pairs={{0,144},{1,145},{2,146},{3,147},{4,148},{5,149},{6,150},{7,151},{8... | collective-permute-start | bytes 239624 | tf_op jit(solution)/shard_map/ppermute | solution.py:29
  129.4 0.7 collective-permute-start.13
  130.1 4.2 %all-to-all-start.5 = ((bf16[4,192,512]{2,1,0:T(8,128)(2,1)}), bf16[4,192,512]{2,1,0:T(8,128)(2,1)S(1)}, u32[]{:S(2)}, u32[]{:S(2)}) async-start(bf16[4,192,512]{2,1,0:T(8,128)(2,1)} %bitcast.60), calls=%async_computation.5 | async-start | bytes 1572864 | tf_op jit(solution)/shard_map/all_to_all | solution.py:57
  134.3 13.8 %collective-permute-start.7 = (bf16[2,2,192,512]{3,2,1,0:T(8,128)(2,1)}, bf16[2,2,192,512]{3,2,1,0:T(8,128)(2,1)}, u32[]{:S(2)}, u32[]{:S(2)}) collective-permute-start(bf16[2,2,192,512]{3,2,1,0:T(8,128)(2,1)} %copy-done.17), channel_id=1, source_target_pairs={{0,124},{1,125},{2,126},{3,127},{4,0},{5,1},{6,2},{7,3},{8,4},{9,5... | collective-permute-start | bytes 2359304 | tf_op jit(solution)/shard_map/ppermute | solution.py:29
  148.5 4.0 %collective-permute-start.17 = (bf16[24,1664]{1,0:T(8,128)(2,1)S(1)}, bf16[24,1664]{1,0:T(8,128)(2,1)S(1)}, u32[]{:S(2)}, u32[]{:S(2)}) collective-permute-start(bf16[24,1664]{1,0:T(8,128)(2,1)S(1)} %add_convert_fusion), channel_id=1, source_target_pairs={{0,64},{1,65},{2,66},{3,67},{4,68},{5,69},{6,70},{7,71},{8,72},{9,... | collective-permute-start | bytes 239624 | tf_op jit(solution)/shard_map/ppermute | solution.py:29
  152.4 2.3 %collective-permute-start.16 = (bf16[24,1664]{1,0:T(8,128)(2,1)S(1)}, bf16[24,1664]{1,0:T(8,128)(2,1)S(1)}, u32[]{:S(2)}, u32[]{:S(2)}) collective-permute-start(bf16[24,1664]{1,0:T(8,128)(2,1)S(1)} %add_convert_fusion), channel_id=1, source_target_pairs={{0,32},{1,33},{2,34},{3,35},{4,36},{5,37},{6,38},{7,39},{8,40},{9,... | collective-permute-start | bytes 239624 | tf_op jit(solution)/shard_map/ppermute | solution.py:29
  154.7 1.1 copy-done.8
  155.9 3.6 %shard_map.100 = bf16[2,2,192,512]{3,2,1,0:T(8,128)(2,1)S(1)} custom-call(s32[8]{0:T(128)S(1)} %stack.43.edge, bf16[2,2,192,512]{3,2,1,0:T(8,128)(2,1)} %collective-permute-done.4.behind, bf16[2,2,192,512]{3,2,1,0:T(8,128)(2,1)} %get-tuple-element.14.here, bf16[2,2,192,512]{3,2,1,0:T(8,128)(2,1)} %collective-permute-done.5.ahead, ...), custom_call_target="tpu_custom_call" | custom-call | flops 905969664 | bytes 3932160 | tf_op jit(solution)/shard_map/pallas_call | solution.py:216
  159.4 0.9 copy-done.9
  160.3 4.8 %all-to-all-start.6 = ((bf16[4,192,512]{2,1,0:T(8,128)(2,1)}), bf16[4,192,512]{2,1,0:T(8,128)(2,1)}, u32[]{:S(2)}, u32[]{:S(2)}) async-start(bf16[4,192,512]{2,1,0:T(8,128)(2,1)} %bitcast.56), calls=%async_computation.6 | async-start | bytes 1572864 | tf_op jit(solution)/shard_map/all_to_all | solution.py:57
  165.2 3.4 %collective-permute-start.21 = (bf16[24,1664]{1,0:T(8,128)(2,1)S(1)}, bf16[24,1664]{1,0:T(8,128)(2,1)S(1)}, u32[]{:S(2)}, u32[]{:S(2)}) collective-permute-start(bf16[24,1664]{1,0:T(8,128)(2,1)S(1)} %multiply_convert_fusion), channel_id=1, source_target_pairs={{0,4},{1,5},{2,6},{3,7},{4,8},{5,9},{6,10},{7,11},{8,12},{9,13},{1... | collective-permute-start | bytes 239624 | tf_op jit(solution)/shard_map/ppermute | solution.py:29
  168.6 7.8 %collective-permute-start.20 = (bf16[24,1664]{1,0:T(8,128)(2,1)S(1)}, bf16[24,1664]{1,0:T(8,128)(2,1)S(1)}, u32[]{:S(2)}, u32[]{:S(2)}) collective-permute-start(bf16[24,1664]{1,0:T(8,128)(2,1)S(1)} %multiply_convert_fusion), channel_id=1, source_target_pairs={{0,8},{1,9},{2,10},{3,11},{4,12},{5,13},{6,14},{7,15},{8,0},{9,1},... | collective-permute-start | bytes 239624 | tf_op jit(solution)/shard_map/ppermute | solution.py:29
  176.4 2.5 %collective-permute-start.19 = (bf16[24,1664]{1,0:T(8,128)(2,1)S(1)}, bf16[24,1664]{1,0:T(8,128)(2,1)S(1)}, u32[]{:S(2)}, u32[]{:S(2)}) collective-permute-start(bf16[24,1664]{1,0:T(8,128)(2,1)S(1)} %multiply_convert_fusion), channel_id=1, source_target_pairs={{0,12},{1,13},{2,14},{3,15},{4,0},{5,1},{6,2},{7,3},{8,4},{9,5},{1... | collective-permute-start | bytes 239624 | tf_op jit(solution)/shard_map/ppermute | solution.py:29
  178.9 1.1 copy-done.6
  180.0 1.1 copy-done.18
  181.2 3.4 %shard_map.101 = bf16[2,2,192,512]{3,2,1,0:T(8,128)(2,1)S(1)} custom-call(s32[8]{0:T(128)S(1)} %stack.43.edge, bf16[2,2,192,512]{3,2,1,0:T(8,128)(2,1)} %collective-permute-done.6.behind, bf16[2,2,192,512]{3,2,1,0:T(8,128)(2,1)S(1)} %copy-done.18, bf16[2,2,192,512]{3,2,1,0:T(8,128)(2,1)} %collective-permute-done.7.ahead, ...), custom_call_target="tpu_custom_call" | custom-call | flops 905969664 | bytes 3932160 | tf_op jit(solution)/shard_map/pallas_call | solution.py:216
  184.6 0.9 copy-done.10
  185.5 4.0 %all-to-all-start.7 = ((bf16[4,192,512]{2,1,0:T(8,128)(2,1)}), bf16[4,192,512]{2,1,0:T(8,128)(2,1)S(1)}, u32[]{:S(2)}, u32[]{:S(2)}) async-start(bf16[4,192,512]{2,1,0:T(8,128)(2,1)} %bitcast.57), calls=%async_computation.7 | async-start | bytes 1572864 | tf_op jit(solution)/shard_map/all_to_all | solution.py:57
  189.8 1.7 shard_map.99
  191.5 7.5 %all-to-all-done.7.refs_1_ = bf16[4,192,512]{2,1,0:T(8,128)(2,1)S(1)} async-done(((bf16[4,192,512]{2,1,0:T(8,128)(2,1)}), bf16[4,192,512]{2,1,0:T(8,128)(2,1)S(1)}, u32[]{:S(2)}, u32[]{:S(2)}) %all-to-all-start.7) | async-done | bytes 786464 | tf_op jit(solution)/shard_map/all_to_all | solution.py:57
  199.0 3.4 %shard_map.102 = bf16[2,192,2048]{2,1,0:T(8,128)(2,1)} custom-call(bf16[4,192,512]{2,1,0:T(8,128)(2,1)} %all-to-all-done.6.refs_0_, bf16[4,192,512]{2,1,0:T(8,128)(2,1)S(1)} %all-to-all-done.7.refs_1_), custom_call_target="tpu_custom_call" | custom-call | bytes 3145728 | tf_op jit(solution)/shard_map/pallas_call | solution.py:93
  202.8 0.7 slice_reduce_fusion
  203.4 0.8 fusion.7
  204.2 1.0 pad_maximum_fusion
  (81 shorter events, 3.0 us)
Async XLA Ops:
  7.2 1.4 copy-start
  10.1 4.6 %copy-start.1 = (bf16[2,192,2048]{2,1,0:T(8,128)(2,1)S(1)}, bf16[2,192,2048]{2,1,0:T(8,128)(2,1)}, u32[]{:S(2)}) copy-start(bf16[2,192,2048]{2,1,0:T(8,128)(2,1)} %source.6) | copy-start | bytes 4718596
  10.1 16.9 %all-to-all-start.3 = ((bf16[4,192,512]{2,1,0:T(8,128)(2,1)}), bf16[4,192,512]{2,1,0:T(8,128)(2,1)S(1)}, u32[]{:S(2)}, u32[]{:S(2)}) async-start(bf16[4,192,512]{2,1,0:T(8,128)(2,1)} %shard_map.96), calls=%async_computation.3 | async-start | bytes 1572864 | tf_op jit(solution)/shard_map/all_to_all | solution.py:57
  16.2 14.3 %copy-start.24 = (f32[192]{0:T(256)S(1)}, f32[192]{0:T(256)}, u32[]{:S(2)}) copy-start(f32[192]{0:T(256)} %param.7) | copy-start | bytes 2308
  16.2 14.5 %copy-start.20 = (bf16[192,384]{1,0:T(8,128)(2,1)S(1)}, bf16[192,384]{1,0:T(8,128)(2,1)}, u32[]{:S(2)}) copy-start(bf16[192,384]{1,0:T(8,128)(2,1)} %mix.1) | copy-start | bytes 442372
  27.0 5.8 %copy-start.13 = (bf16[4,192,512]{2,1,0:T(8,128)(2,1)}, bf16[4,192,512]{2,1,0:T(8,128)(2,1)S(1)}, u32[]{:S(2)}) copy-start(bf16[4,192,512]{2,1,0:T(8,128)(2,1)S(1)} %all-to-all-done.3) | copy-start | bytes 2359300
  27.0 14.8 %all-to-all-start = ((bf16[4,192,512]{2,1,0:T(8,128)(2,1)}), bf16[4,192,512]{2,1,0:T(8,128)(2,1)S(1)}, u32[]{:S(2)}, u32[]{:S(2)}) async-start(bf16[4,192,512]{2,1,0:T(8,128)(2,1)} %shard_map.92), calls=%async_computation | async-start | bytes 1572864 | tf_op jit(solution)/shard_map/all_to_all | solution.py:57
  30.5 2.3 %copy-start.2 = (bf16[2,192,2048]{2,1,0:T(8,128)(2,1)S(1)}, bf16[2,192,2048]{2,1,0:T(8,128)(2,1)}, u32[]{:S(2)}) copy-start(bf16[2,192,2048]{2,1,0:T(8,128)(2,1)} %source.7) | copy-start | bytes 4718596
  30.5 44.8 %all-gather.2.cloned.1.call-start = ((), (), s32[]{:S(2)}) async-start(), calls=%async_computation.8 | async-start | bytes 1916928 | tf_op jit(solution)/shard_map/all_gather | solution.py:279
  30.7 1.1 copy-start.19
  41.8 0.9 copy-start.15
  42.7 20.6 %all-to-all-start.1 = ((bf16[4,192,512]{2,1,0:T(8,128)(2,1)}), bf16[4,192,512]{2,1,0:T(8,128)(2,1)S(1)}, u32[]{:S(2)}, u32[]{:S(2)}) async-start(bf16[4,192,512]{2,1,0:T(8,128)(2,1)} %shard_map.93), calls=%async_computation.1 | async-start | bytes 1572864 | tf_op jit(solution)/shard_map/all_to_all | solution.py:57
  46.2 29.1 %collective-permute-start.1 = (bf16[2,2,192,512]{3,2,1,0:T(8,128)(2,1)}, bf16[2,2,192,512]{3,2,1,0:T(8,128)(2,1)}, u32[]{:S(2)}, u32[]{:S(2)}) collective-permute-start(bf16[2,2,192,512]{3,2,1,0:T(8,128)(2,1)} %bitcast.64), channel_id=1, source_target_pairs={{0,124},{1,125},{2,126},{3,127},{4,0},{5,1},{6,2},{7,3},{8,4},{9,5... | collective-permute-start | bytes 2359304 | tf_op jit(solution)/shard_map/ppermute | solution.py:29
  46.8 28.5 %collective-permute-start = (bf16[2,2,192,512]{3,2,1,0:T(8,128)(2,1)}, bf16[2,2,192,512]{3,2,1,0:T(8,128)(2,1)}, u32[]{:S(2)}, u32[]{:S(2)}) collective-permute-start(bf16[2,2,192,512]{3,2,1,0:T(8,128)(2,1)} %bitcast.65), channel_id=1, source_target_pairs={{0,4},{1,5},{2,6},{3,7},{4,8},{5,9},{6,10},{7,11},{8,12},{9,13},{1... | collective-permute-start | bytes 2359304 | tf_op jit(solution)/shard_map/ppermute | solution.py:29
  48.3 38.0 %collective-permute-start.3 = (bf16[2,2,192,512]{3,2,1,0:T(8,128)(2,1)}, bf16[2,2,192,512]{3,2,1,0:T(8,128)(2,1)}, u32[]{:S(2)}, u32[]{:S(2)}) collective-permute-start(bf16[2,2,192,512]{3,2,1,0:T(8,128)(2,1)} %bitcast.61), channel_id=1, source_target_pairs={{0,124},{1,125},{2,126},{3,127},{4,0},{5,1},{6,2},{7,3},{8,4},{9,5... | collective-permute-start | bytes 2359304 | tf_op jit(solution)/shard_map/ppermute | solution.py:29
  49.1 37.2 %collective-permute-start.2 = (bf16[2,2,192,512]{3,2,1,0:T(8,128)(2,1)}, bf16[2,2,192,512]{3,2,1,0:T(8,128)(2,1)}, u32[]{:S(2)}, u32[]{:S(2)}) collective-permute-start(bf16[2,2,192,512]{3,2,1,0:T(8,128)(2,1)} %bitcast.62), channel_id=1, source_target_pairs={{0,4},{1,5},{2,6},{3,7},{4,8},{5,9},{6,10},{7,11},{8,12},{9,13},{1... | collective-permute-start | bytes 2359304 | tf_op jit(solution)/shard_map/ppermute | solution.py:29
  63.3 21.6 %copy-start.7 = (bf16[4,192,512]{2,1,0:T(8,128)(2,1)}, bf16[4,192,512]{2,1,0:T(8,128)(2,1)S(1)}, u32[]{:S(2)}) copy-start(bf16[4,192,512]{2,1,0:T(8,128)(2,1)S(1)} %all-to-all-done.1) | copy-start | bytes 2359300
  63.3 23.0 %all-to-all-start.4 = ((bf16[4,192,512]{2,1,0:T(8,128)(2,1)}), bf16[4,192,512]{2,1,0:T(8,128)(2,1)S(1)}, u32[]{:S(2)}, u32[]{:S(2)}) async-start(bf16[4,192,512]{2,1,0:T(8,128)(2,1)} %shard_map.97), calls=%async_computation.4 | async-start | bytes 1572864 | tf_op jit(solution)/shard_map/all_to_all | solution.py:57
  75.3 1.3 copy-start.3
  76.6 1.1 copy-start.16
  77.8 8.6 %copy-start.4 = (bf16[384,1664]{1,0:T(8,128)(2,1)S(1)}, bf16[384,1664]{1,0:T(8,128)(2,1)}, u32[]{:S(2)}) copy-start(bf16[384,1664]{1,0:T(8,128)(2,1)} %all-gather.2.cloned.1.call-done.weights) | copy-start | bytes 3833860
  84.9 1.4 copy-start.21
  86.3 9.4 %copy-start.5 = (bf16[4,192,512]{2,1,0:T(8,128)(2,1)}, bf16[4,192,512]{2,1,0:T(8,128)(2,1)S(1)}, u32[]{:S(2)}) copy-start(bf16[4,192,512]{2,1,0:T(8,128)(2,1)S(1)} %all-to-all-done.4) | copy-start | bytes 2359300
  86.4 1.4 copy-start.14
  87.8 1.7 copy-start.22
  95.8 1.4 copy-start.11
  95.8 1.7 copy-start.12
  95.8 1.9 copy-start.17
  97.7 3.1 %collective-permute-start.8 = (f32[2,4,24,1664]{3,2,1,0:T(8,128)S(1)}, f32[2,4,24,1664]{3,2,1,0:T(8,128)}, u32[]{:S(2)}, u32[]{:S(2)}) collective-permute-start(f32[2,4,24,1664]{3,2,1,0:T(8,128)S(1)} %dynamic-slice_bitcast_fusion), channel_id=1, source_target_pairs={{0,2},{1,3},{2,0},{3,1},{4,6},{5,7},{6,4},{7,5},{8,10},{9,11},{10,... | collective-permute-start | bytes 3833864 | tf_op jit(solution)/shard_map/ppermute | solution.py:29
  102.7 1.0 copy-start.23
  102.7 12.0 %collective-permute-start.9 = (bf16[4,24,1664]{2,1,0:T(8,128)(2,1)S(1)}, bf16[4,24,1664]{2,1,0:T(8,128)(2,1)S(1)}, u32[]{:S(2)}, u32[]{:S(2)}) collective-permute-start(bf16[4,24,1664]{2,1,0:T(8,128)(2,1)S(1)} %fusion), channel_id=1, source_target_pairs={{0,1},{1,0},{2,3},{3,2},{4,5},{5,4},{6,7},{7,6},{8,9},{9,8},{10,11... | collective-permute-start | bytes 958472 | tf_op jit(solution)/shard_map/ppermute | solution.py:29
  103.7 26.4 %all-to-all-start.2 = ((bf16[4,192,512]{2,1,0:T(8,128)(2,1)}), bf16[4,192,512]{2,1,0:T(8,128)(2,1)S(1)}, u32[]{:S(2)}, u32[]{:S(2)}) async-start(bf16[4,192,512]{2,1,0:T(8,128)(2,1)} %bitcast.6), calls=%async_computation.2 | async-start | bytes 1572864 | tf_op jit(solution)/shard_map/all_to_all | solution.py:57
  115.9 6.2 %collective-permute-start.10 = (bf16[24,1664]{1,0:T(8,128)(2,1)S(1)}, bf16[24,1664]{1,0:T(8,128)(2,1)S(1)}, u32[]{:S(2)}, u32[]{:S(2)}) collective-permute-start(bf16[24,1664]{1,0:T(8,128)(2,1)S(1)} %get-tuple-element.23), channel_id=1, source_target_pairs={{0,4},{1,5},{2,6},{3,7},{4,8},{5,9},{6,10},{7,11},{8,12},{9,13},{1... | collective-permute-start | bytes 239624 | tf_op jit(solution)/shard_map/ppermute | solution.py:29
  117.5 5.3 %collective-permute-start.12 = (bf16[24,1664]{1,0:T(8,128)(2,1)S(1)}, bf16[24,1664]{1,0:T(8,128)(2,1)S(1)}, u32[]{:S(2)}, u32[]{:S(2)}) collective-permute-start(bf16[24,1664]{1,0:T(8,128)(2,1)S(1)} %get-tuple-element.24), channel_id=1, source_target_pairs={{0,12},{1,13},{2,14},{3,15},{4,0},{5,1},{6,2},{7,3},{8,4},{9,5},{1... | collective-permute-start | bytes 239624 | tf_op jit(solution)/shard_map/ppermute | solution.py:29
  118.0 7.0 %collective-permute-start.11 = (bf16[24,1664]{1,0:T(8,128)(2,1)S(1)}, bf16[24,1664]{1,0:T(8,128)(2,1)S(1)}, u32[]{:S(2)}, u32[]{:S(2)}) collective-permute-start(bf16[24,1664]{1,0:T(8,128)(2,1)S(1)} %get-tuple-element.25), channel_id=1, source_target_pairs={{0,8},{1,9},{2,10},{3,11},{4,12},{5,13},{6,14},{7,15},{8,0},{9,1},... | collective-permute-start | bytes 239624 | tf_op jit(solution)/shard_map/ppermute | solution.py:29
  120.1 28.3 %collective-permute-start.5 = (bf16[2,2,192,512]{3,2,1,0:T(8,128)(2,1)}, bf16[2,2,192,512]{3,2,1,0:T(8,128)(2,1)}, u32[]{:S(2)}, u32[]{:S(2)}) collective-permute-start(bf16[2,2,192,512]{3,2,1,0:T(8,128)(2,1)} %get-tuple-element.14.here), channel_id=1, source_target_pairs={{0,124},{1,125},{2,126},{3,127},{4,0},{5,1},{6,2},{7,3},{8,4},{9,5... | collective-permute-start | bytes 2359304 | tf_op jit(solution)/shard_map/ppermute | solution.py:29
  121.6 30.9 %collective-permute-start.4 = (bf16[2,2,192,512]{3,2,1,0:T(8,128)(2,1)}, bf16[2,2,192,512]{3,2,1,0:T(8,128)(2,1)}, u32[]{:S(2)}, u32[]{:S(2)}) collective-permute-start(bf16[2,2,192,512]{3,2,1,0:T(8,128)(2,1)} %get-tuple-element.14.here), channel_id=1, source_target_pairs={{0,4},{1,5},{2,6},{3,7},{4,8},{5,9},{6,10},{7,11},{8,12},{9,13},{1... | collective-permute-start | bytes 2359304 | tf_op jit(solution)/shard_map/ppermute | solution.py:29
  125.0 9.2 %collective-permute-start.15 = (bf16[24,1664]{1,0:T(8,128)(2,1)S(1)}, bf16[24,1664]{1,0:T(8,128)(2,1)S(1)}, u32[]{:S(2)}, u32[]{:S(2)}) collective-permute-start(bf16[24,1664]{1,0:T(8,128)(2,1)S(1)} %fusion.3), channel_id=1, source_target_pairs={{0,144},{1,145},{2,146},{3,147},{4,148},{5,149},{6,150},{7,151},{8... | collective-permute-start | bytes 239624 | tf_op jit(solution)/shard_map/ppermute | solution.py:29
  129.4 18.7 %collective-permute-start.14 = (bf16[24,1664]{1,0:T(8,128)(2,1)S(1)}, bf16[24,1664]{1,0:T(8,128)(2,1)S(1)}, u32[]{:S(2)}, u32[]{:S(2)}) collective-permute-start(bf16[24,1664]{1,0:T(8,128)(2,1)S(1)} %fusion.3), channel_id=1, source_target_pairs={{0,16},{1,17},{2,18},{3,19},{4,20},{5,21},{6,22},{7,23},{8,24},{9,... | collective-permute-start | bytes 239624 | tf_op jit(solution)/shard_map/ppermute | solution.py:29
  129.4 18.7 %collective-permute-start.13 = (bf16[24,1664]{1,0:T(8,128)(2,1)S(1)}, bf16[24,1664]{1,0:T(8,128)(2,1)S(1)}, u32[]{:S(2)}, u32[]{:S(2)}) collective-permute-start(bf16[24,1664]{1,0:T(8,128)(2,1)S(1)} %fusion.3), channel_id=1, source_target_pairs={{0,128},{1,129},{2,130},{3,131},{4,132},{5,133},{6,134},{7,135},{8... | collective-permute-start | bytes 239624 | tf_op jit(solution)/shard_map/ppermute | solution.py:29
  130.1 30.2 %all-to-all-start.5 = ((bf16[4,192,512]{2,1,0:T(8,128)(2,1)}), bf16[4,192,512]{2,1,0:T(8,128)(2,1)S(1)}, u32[]{:S(2)}, u32[]{:S(2)}) async-start(bf16[4,192,512]{2,1,0:T(8,128)(2,1)} %bitcast.60), calls=%async_computation.5 | async-start | bytes 1572864 | tf_op jit(solution)/shard_map/all_to_all | solution.py:57
  134.3 44.6 %collective-permute-start.7 = (bf16[2,2,192,512]{3,2,1,0:T(8,128)(2,1)}, bf16[2,2,192,512]{3,2,1,0:T(8,128)(2,1)}, u32[]{:S(2)}, u32[]{:S(2)}) collective-permute-start(bf16[2,2,192,512]{3,2,1,0:T(8,128)(2,1)} %copy-done.17), channel_id=1, source_target_pairs={{0,124},{1,125},{2,126},{3,127},{4,0},{5,1},{6,2},{7,3},{8,4},{9,5... | collective-permute-start | bytes 2359304 | tf_op jit(solution)/shard_map/ppermute | solution.py:29
  148.1 30.8 %collective-permute-start.6 = (bf16[2,2,192,512]{3,2,1,0:T(8,128)(2,1)}, bf16[2,2,192,512]{3,2,1,0:T(8,128)(2,1)}, u32[]{:S(2)}, u32[]{:S(2)}) collective-permute-start(bf16[2,2,192,512]{3,2,1,0:T(8,128)(2,1)} %copy-done.17), channel_id=1, source_target_pairs={{0,4},{1,5},{2,6},{3,7},{4,8},{5,9},{6,10},{7,11},{8,12},{9,13},{1... | collective-permute-start | bytes 2359304 | tf_op jit(solution)/shard_map/ppermute | solution.py:29
  148.1 17.0 %collective-permute-start.18 = (bf16[24,1664]{1,0:T(8,128)(2,1)S(1)}, bf16[24,1664]{1,0:T(8,128)(2,1)S(1)}, u32[]{:S(2)}, u32[]{:S(2)}) collective-permute-start(bf16[24,1664]{1,0:T(8,128)(2,1)S(1)} %add_convert_fusion), channel_id=1, source_target_pairs={{0,96},{1,97},{2,98},{3,99},{4,100},{5,101},{6,102},{7,103},{8,104... | collective-permute-start | bytes 239624 | tf_op jit(solution)/shard_map/ppermute | solution.py:29
  148.5 16.7 %collective-permute-start.17 = (bf16[24,1664]{1,0:T(8,128)(2,1)S(1)}, bf16[24,1664]{1,0:T(8,128)(2,1)S(1)}, u32[]{:S(2)}, u32[]{:S(2)}) collective-permute-start(bf16[24,1664]{1,0:T(8,128)(2,1)S(1)} %add_convert_fusion), channel_id=1, source_target_pairs={{0,64},{1,65},{2,66},{3,67},{4,68},{5,69},{6,70},{7,71},{8,72},{9,... | collective-permute-start | bytes 239624 | tf_op jit(solution)/shard_map/ppermute | solution.py:29
  152.4 12.7 %collective-permute-start.16 = (bf16[24,1664]{1,0:T(8,128)(2,1)S(1)}, bf16[24,1664]{1,0:T(8,128)(2,1)S(1)}, u32[]{:S(2)}, u32[]{:S(2)}) collective-permute-start(bf16[24,1664]{1,0:T(8,128)(2,1)S(1)} %add_convert_fusion), channel_id=1, source_target_pairs={{0,32},{1,33},{2,34},{3,35},{4,36},{5,37},{6,38},{7,39},{8,40},{9,... | collective-permute-start | bytes 239624 | tf_op jit(solution)/shard_map/ppermute | solution.py:29
  154.7 1.1 copy-start.8
  159.4 0.9 copy-start.9
  160.3 25.2 %all-to-all-start.6 = ((bf16[4,192,512]{2,1,0:T(8,128)(2,1)}), bf16[4,192,512]{2,1,0:T(8,128)(2,1)}, u32[]{:S(2)}, u32[]{:S(2)}) async-start(bf16[4,192,512]{2,1,0:T(8,128)(2,1)} %bitcast.56), calls=%async_computation.6 | async-start | bytes 1572864 | tf_op jit(solution)/shard_map/all_to_all | solution.py:57
  165.2 24.4 %collective-permute-start.21 = (bf16[24,1664]{1,0:T(8,128)(2,1)S(1)}, bf16[24,1664]{1,0:T(8,128)(2,1)S(1)}, u32[]{:S(2)}, u32[]{:S(2)}) collective-permute-start(bf16[24,1664]{1,0:T(8,128)(2,1)S(1)} %multiply_convert_fusion), channel_id=1, source_target_pairs={{0,4},{1,5},{2,6},{3,7},{4,8},{5,9},{6,10},{7,11},{8,12},{9,13},{1... | collective-permute-start | bytes 239624 | tf_op jit(solution)/shard_map/ppermute | solution.py:29
  168.6 21.0 %collective-permute-start.20 = (bf16[24,1664]{1,0:T(8,128)(2,1)S(1)}, bf16[24,1664]{1,0:T(8,128)(2,1)S(1)}, u32[]{:S(2)}, u32[]{:S(2)}) collective-permute-start(bf16[24,1664]{1,0:T(8,128)(2,1)S(1)} %multiply_convert_fusion), channel_id=1, source_target_pairs={{0,8},{1,9},{2,10},{3,11},{4,12},{5,13},{6,14},{7,15},{8,0},{9,1},... | collective-permute-start | bytes 239624 | tf_op jit(solution)/shard_map/ppermute | solution.py:29
  176.4 13.2 %collective-permute-start.19 = (bf16[24,1664]{1,0:T(8,128)(2,1)S(1)}, bf16[24,1664]{1,0:T(8,128)(2,1)S(1)}, u32[]{:S(2)}, u32[]{:S(2)}) collective-permute-start(bf16[24,1664]{1,0:T(8,128)(2,1)S(1)} %multiply_convert_fusion), channel_id=1, source_target_pairs={{0,12},{1,13},{2,14},{3,15},{4,0},{5,1},{6,2},{7,3},{8,4},{9,5},{1... | collective-permute-start | bytes 239624 | tf_op jit(solution)/shard_map/ppermute | solution.py:29
  178.9 1.1 copy-start.6
  180.0 1.1 copy-start.18
  184.6 0.9 copy-start.10
  185.5 13.5 %all-to-all-start.7 = ((bf16[4,192,512]{2,1,0:T(8,128)(2,1)}), bf16[4,192,512]{2,1,0:T(8,128)(2,1)S(1)}, u32[]{:S(2)}, u32[]{:S(2)}) async-start(bf16[4,192,512]{2,1,0:T(8,128)(2,1)} %bitcast.57), calls=%async_computation.7 | async-start | bytes 1572864 | tf_op jit(solution)/shard_map/all_to_all | solution.py:57
  189.7 12.8 %collective-permute-start.22 = (bf16[4,24,1664]{2,1,0:T(8,128)(2,1)S(1)}, bf16[4,24,1664]{2,1,0:T(8,128)(2,1)S(1)}, u32[]{:S(2)}, u32[]{:S(2)}) collective-permute-start(bf16[4,24,1664]{2,1,0:T(8,128)(2,1)S(1)} %pad_maximum_fusion.2), channel_id=1, source_target_pairs={{0,2},{1,3},{2,0},{3,1},{4,6},{5,7},{6,4},{7,5},{8,10},{9,11},{10,... | collective-permute-start | bytes 958472 | tf_op jit(solution)/shard_map/ppermute | solution.py:29
Sparse Core Ops, SparseCore 0:
  33.7 41.5 all-gather.1

commit v2 on v1

v2 whole, which is shorter than its diff:
```python
import math

import jax
import jax.numpy as jnp
from jax import lax
from jax.experimental import pallas as pl
from jax.experimental.pallas import tpu as pltpu
from jax.sharding import PartitionSpec as P

BF16, F32 = jnp.bfloat16, jnp.float32
AXES = ("seq", "ch")
CHUNKS = 1
SIZE = 1024 // CHUNKS
TILE = 512
ROOT = math.sqrt(2.0 / math.pi)
CUBE = 0.044715


def route(target):
    pairs = []
    for s in range(128):
        for h in range(2):
            to = target(s, h)
            pairs.append((2 * s + h, 2 * to[0] + to[1]))
    return pairs


def send(block, target):
    return lax.ppermute(block, AXES, route(target))


def other_ch(s, h):
    return s, 1 - h


def other_core(s, h):
    return s ^ 1, h


def flip(bits):
    return lambda s, h: (s ^ bits, h)


def chips_on(step):
    return lambda s, h: ((s & 64) | ((s + 2 * step) & 63), h)


def column_groups():
    return [[2 * (64 * (y & 1) + place) + (y >> 1) for y in range(4)] for place in range(64)]


def exchange(block):
    return lax.all_to_all(block, AXES, 0, 0, axis_index_groups=column_groups())


def dot(a, b, dims=((1,), (0,))):
    return lax.dot_general(a, b, (dims, ((), ())), preferred_element_type=F32)


def params(megabytes=28):
    return pltpu.CompilerParams(vmem_limit_bytes=megabytes * 2**20)


def copy_kernel(source, *refs):
    refs[-1][...] = source[...]


def pack(array, k, *after):
    block = (1, 192, SIZE)
    return pl.pallas_call(
        copy_kernel,
        grid=(4,),
        in_specs=[pl.BlockSpec(block, lambda d: (d // 2, 0, (d % 2) * CHUNKS + k))]
        + [pl.BlockSpec(memory_space=pl.ANY)] * len(after),
        out_specs=pl.BlockSpec(block, lambda d: (d, 0, 0)),
        out_shape=jax.ShapeDtypeStruct((4, 192, SIZE), BF16),
        compiler_params=params(),
        cost_estimate=pl.CostEstimate(flops=0, bytes_accessed=16 * 192 * SIZE, transcendentals=0),
    )(array, *after)


def split_kernel(place, *refs):
    for source, target in zip(refs[:4], refs[4:]):
        target[...] = source[0]


def split(array, place, k):
    def source(other_half, other_low):
        def index(i, place):
            half, low = place[0] ^ other_half, place[1] ^ other_low
            return half, 0, low * CHUNKS + k

        return pl.BlockSpec((1, 192, SIZE), index)

    plain = pl.BlockSpec((192, SIZE), lambda i, place: (0, 0))
    return pl.pallas_call(
        split_kernel,
        grid_spec=pltpu.PrefetchScalarGridSpec(
            num_scalar_prefetch=1,
            grid=(1,),
            in_specs=[source(0, 0), source(0, 1), source(1, 0), source(1, 1)],
            out_specs=[plain] * 4,
        ),
        out_shape=[jax.ShapeDtypeStruct((192, SIZE), BF16)] * 4,
        compiler_params=params(),
    )(place, array, array, array, array)


def join_kernel(place, own, low, half, both, out):
    for source, a, b in ((own, 0, 0), (low, 0, 1), (half, 1, 0), (both, 1, 1)):
        out[pl.ds(place[0] ^ a, 1), pl.ds(place[1] ^ b, 1)] = source[...][None, None]


def join(place, *parts):
    vmem = pl.BlockSpec(memory_space=pltpu.VMEM)
    return pl.pallas_call(
        join_kernel,
        in_specs=[pl.BlockSpec(memory_space=pltpu.SMEM)] + [vmem] * 4,
        out_specs=vmem,
        out_shape=jax.ShapeDtypeStruct((2, 2, 192, SIZE), BF16),
        compiler_params=params(),
    )(place, *parts)


def other_low(s, h):
    return s ^ 64, h


def other_both(s, h):
    return s ^ 64, 1 - h


def gather_column(array, place, k):
    own, low, half, both = split(array, place, k)
    return join(place, own, send(low, other_low), send(half, other_ch), send(both, other_both))


def unpack_kernel(source, target):
    target[0, :, 0:1024] = source[0]
    target[0, :, 1024:2048] = source[1]


def unpack(pieces):
    return pl.pallas_call(
        unpack_kernel,
        grid=(2,),
        in_specs=[pl.BlockSpec((2, 192, 1024), lambda d: (d, 0, 0))],
        out_specs=pl.BlockSpec((1, 192, 2048), lambda d: (d, 0, 0)),
        out_shape=jax.ShapeDtypeStruct((2, 192, 2048), BF16),
        compiler_params=params(),
        cost_estimate=pl.CostEstimate(flops=0, bytes_accessed=16 * 192 * 1024, transcendentals=0),
    )(pieces[0])


def weights_kernel(taps, mix, bias, *refs):
    out = refs[-1]
    for k in range(3):
        out[:, 384 * k : 384 * (k + 1)] = taps[k]
    out[:, 1152:1536] = mix[...]
    value = jnp.broadcast_to(bias[...], (192, 128))
    high = value.astype(BF16).astype(F32)
    middle = (value - high).astype(BF16).astype(F32)
    low = value - high - middle
    lane = lax.broadcasted_iota(jnp.int32, (192, 128), 1)
    split = jnp.where(lane == 0, high, jnp.where(lane == 1, middle, jnp.where(lane == 2, low, 0.0)))
    out[:, 1536:1664] = split.astype(BF16)


def pack_weights(taps, mix, bias, *after):
    return pl.pallas_call(
        weights_kernel,
        in_specs=[pl.BlockSpec(memory_space=pltpu.VMEM)] * 3
        + [pl.BlockSpec(memory_space=pl.ANY)] * len(after),
        out_shape=jax.ShapeDtypeStruct((192, 1664), BF16),
        compiler_params=params(),
    )(taps, mix, bias.reshape(192, 1), *after)


def assemble_kernel(place, own, straight, crossed, out):
    half, core = place[0], place[1]
    out[pl.ds(pl.multiple_of(192 * half, 192), 192), :] = own[...]
    base = 192 * (1 - half)
    out[pl.ds(pl.multiple_of(base + 96 * core, 96), 96), :] = straight[...]
    out[pl.ds(pl.multiple_of(base + 96 * (1 - core), 96), 96), :] = crossed[...]


def gather_weights(own, half, core):
    straight = send(pick(own.reshape(2, 96, 1664), core, 0), other_ch)
    crossed = send(straight, other_core)
    return pl.pallas_call(
        assemble_kernel,
        in_specs=[pl.BlockSpec(memory_space=pltpu.SMEM)]
        + [pl.BlockSpec(memory_space=pltpu.VMEM)] * 3,
        out_shape=jax.ShapeDtypeStruct((384, 1664), BF16),
        compiler_params=params(),
    )(jnp.stack([half, core]).astype(jnp.int32), own, straight, crossed)


def rows(ref):
    return ref[...].reshape(384, TILE)


def masked(ref, keep):
    return jnp.where(keep == 1, rows(ref), jnp.zeros((384, TILE), BF16))


def middle_kernel(edge, behind, here, ahead, cot, weights, *refs):
    act_out, grad_pre, own, theirs, sums = refs
    group = pl.program_id(0)

    @pl.when((group == 0) & (pl.program_id(1) == 0))
    def _():
        sums[...] = jnp.zeros((384, 1664), F32)

    center = rows(here)
    field = jnp.concatenate(
        [masked(behind, edge[2 + group]), center, masked(ahead, edge[6 + group])], axis=0
    )
    bias = weights[:, 1536:1664].astype(F32)
    bias = bias[:, 0:1] + bias[:, 1:2] + bias[:, 2:3]
    pre = dot(weights[:, 0:1152], field) + bias
    square = pre * pre
    bent = jnp.tanh(ROOT * pre * (1.0 + CUBE * square))
    half = 0.5 * (1.0 + bent)
    act = (pre * half).astype(BF16)
    slope = half + 0.5 * pre * (1.0 - bent * bent) * (ROOT * (1.0 + 3.0 * CUBE * square))
    mix = weights[:, 1152:1536]
    act_out[...] = act.reshape(act_out.shape)
    upstream = rows(cot)
    grad = (dot(mix, upstream, ((0,), (0,))) * slope).astype(BF16)
    grad_pre[...] = grad.reshape(grad_pre.shape)
    last = ((1,), (1,))
    sums[:, 0:1152] += dot(grad, field, last)
    sums[:, 1152:1536] += dot(upstream, act, last)
    sums[:, 1536:1664] += jnp.broadcast_to(
        jnp.sum(grad.astype(F32), axis=1, keepdims=True), (384, 128)
    )

    @pl.when((group == 1) & (pl.program_id(1) == pl.num_programs(1) - 1))
    def _():
        core = edge[8]
        for h in range(2):
            own[h] = sums[pl.ds(pl.multiple_of(192 * h + 96 * core, 96), 96), :]
            theirs[h] = sums[pl.ds(pl.multiple_of(192 * h + 96 * (1 - core), 96), 96), :]


def tile_specs():
    block = (2, 1, 192, TILE)
    plain = pl.BlockSpec(block, lambda g, i, edge: (0, g, 0, i))
    behind = pl.BlockSpec(block, lambda g, i, edge: (0, edge[g], 0, i))
    ahead = pl.BlockSpec(block, lambda g, i, edge: (0, edge[4 + g], 0, i))
    return plain, behind, ahead


def whole(array):
    return pl.BlockSpec(array.shape, lambda g, i, edge: (0,) * array.ndim)


def middle(edge, behind, here, ahead, cot, weights):
    plain, before, after = tile_specs()
    sums = jax.ShapeDtypeStruct((2, 96, 1664), F32)
    field = jax.ShapeDtypeStruct((2, 2, 192, SIZE), BF16)
    return pl.pallas_call(
        middle_kernel,
        grid_spec=pltpu.PrefetchScalarGridSpec(
            num_scalar_prefetch=1,
            grid=(2, SIZE // TILE),
            in_specs=[before, plain, after, plain, whole(weights)],
            out_specs=[plain, plain, whole(sums), whole(sums)],
            scratch_shapes=[pltpu.VMEM((384, 1664), F32)],
        ),
        out_shape=[field, field, sums, sums],
        compiler_params=params(),
        cost_estimate=pl.CostEstimate(
            flops=36 * 384 * 384 * SIZE, bytes_accessed=24 * 384 * SIZE, transcendentals=768 * SIZE
        ),
    )(edge, behind, here, ahead, cot, weights)


def mix_kernel(edge, here, act, weights, *refs):
    out = refs[-1]
    result = rows(here).astype(F32) + dot(weights[:, 1152:1536], rows(act))
    out[...] = result.astype(BF16).reshape(out.shape)


def mixed(edge, here, act, weights, *after):
    plain, _, _ = tile_specs()
    return pl.pallas_call(
        mix_kernel,
        grid_spec=pltpu.PrefetchScalarGridSpec(
            num_scalar_prefetch=1,
            grid=(2, SIZE // TILE),
            in_specs=[plain, plain, whole(weights)]
            + [pl.BlockSpec(memory_space=pl.ANY)] * len(after),
            out_specs=plain,
        ),
        out_shape=jax.ShapeDtypeStruct((2, 2, 192, SIZE), BF16),
        compiler_params=params(),
        cost_estimate=pl.CostEstimate(
            flops=4 * 384 * 384 * SIZE, bytes_accessed=12 * 384 * SIZE, transcendentals=0
        ),
    )(edge, here, act, weights, *after)


def back_kernel(edge, behind, here, ahead, cot, weights, *refs):
    out, taps = refs[-2:]
    group = pl.program_id(0)

    @pl.when((group == 0) & (pl.program_id(1) == 0))
    def _():
        for k in range(3):
            tap = weights[:, 384 * (2 - k) : 384 * (3 - k)]
            taps[:, 384 * k : 384 * (k + 1)] = tap.T

    field = jnp.concatenate(
        [masked(behind, edge[2 + group]), rows(here), masked(ahead, edge[6 + group])], axis=0
    )
    result = (rows(cot).astype(F32) + dot(taps[...], field)).astype(BF16)
    out[...] = result.reshape(out.shape)


def back(edge, behind, here, ahead, cot, weights, *after):
    plain, before, beyond = tile_specs()
    return pl.pallas_call(
        back_kernel,
        grid_spec=pltpu.PrefetchScalarGridSpec(
            num_scalar_prefetch=1,
            grid=(2, SIZE // TILE),
            in_specs=[before, plain, beyond, plain, whole(weights)]
            + [pl.BlockSpec(memory_space=pl.ANY)] * len(after),
            out_specs=plain,
            scratch_shapes=[pltpu.VMEM((384, 1152), BF16)],
        ),
        out_shape=jax.ShapeDtypeStruct((2, 2, 192, SIZE), BF16),
        compiler_params=params(),
        cost_estimate=pl.CostEstimate(
            flops=12 * 384 * 384 * SIZE, bytes_accessed=20 * 384 * SIZE, transcendentals=0
        ),
    )(edge, behind, here, ahead, cot, weights, *after)


def round_kernel(total, *refs):
    refs[-1][...] = total[...].astype(BF16)


def rounded(total, *after):
    return pl.pallas_call(
        round_kernel,
        in_specs=[pl.BlockSpec(memory_space=pltpu.VMEM)]
        + [pl.BlockSpec(memory_space=pl.ANY)] * len(after),
        out_shape=jax.ShapeDtypeStruct(total.shape, BF16),
        compiler_params=params(),
    )(total, *after)


def pick(array, index, axis):
    return lax.dynamic_index_in_dim(array, index, axis, keepdims=False)


def add_kernel(half, own, received, mine, theirs):
    mine[...] = (own[half[0]] + received[half[0]]).astype(BF16)
    theirs[...] = (own[1 - half[0]] + received[1 - half[0]]).astype(BF16)


def add_cores(half, own, received):
    vmem = pl.BlockSpec(memory_space=pltpu.VMEM)
    return pl.pallas_call(
        add_kernel,
        in_specs=[pl.BlockSpec(memory_space=pltpu.SMEM), vmem, vmem],
        out_specs=[vmem, vmem],
        out_shape=[jax.ShapeDtypeStruct((96, 1664), BF16)] * 2,
        compiler_params=params(),
    )(half.reshape(1), own, received)


def sum_in_column(own, given):
    own, theirs = add_cores(lax.axis_index("ch"), own, send(given, other_core))
    beside = send(own, other_low).astype(F32)
    across = send(theirs, other_ch).astype(F32)
    third = send(theirs, other_both).astype(F32)
    return ((own.astype(F32) + beside) + (across + third)).reshape(4, 24, 1664)


def place_on_z():
    return (lax.axis_index("seq") >> 3) & 3


def scatter_over_z(mine):
    z = place_on_z()
    total = pick(mine, z, 0)
    for k in (1, 2, 3):
        part = pick(mine, z ^ k, 0).astype(BF16)
        total = total + send(part, flip(8 * k)).astype(F32)
    return total


def add_flips(own, a, b):
    first, second, third = (send(own, flip(m)).astype(F32) for m in (a, b, a ^ b))
    return (own.astype(F32) + first) + (second + third)


def place_kernel(z, *refs):
    out = refs[-1]
    for k in range(4):
        out[pl.ds(z[0] ^ k, 1)] = refs[k][...][None]


def gather_over_z(total, *after):
    found = [total] + [send(total, flip(8 * k)) for k in (1, 2, 3)]
    return pl.pallas_call(
        place_kernel,
        in_specs=[pl.BlockSpec(memory_space=pltpu.SMEM)]
        + [pl.BlockSpec(memory_space=pltpu.VMEM)] * 4
        + [pl.BlockSpec(memory_space=pl.ANY)] * len(after),
        out_shape=jax.ShapeDtypeStruct((4, 24, 1664), BF16),
        compiler_params=params(),
    )(place_on_z().reshape(1), *found, *after)


def result_kernel(core, own, across, taps, mix, bias):
    for source, base in ((own, 96 * core[0]), (across, 96 * (1 - core[0]))):
        for j in range(4):
            place = pl.ds(pl.multiple_of(base + 24 * j, 8), 24)
            block = source[j].astype(F32)
            for k in range(3):
                taps[k, place, :] = block[:, 384 * k : 384 * (k + 1)]
            mix[place, :] = block[:, 1152:1536]
            bias[place, :] = block[:, 1536:1664]


def results(gathered):
    core = (lax.axis_index("seq") & 1).reshape(1)
    vmem = pl.BlockSpec(memory_space=pltpu.VMEM)
    taps, mix, bias = pl.pallas_call(
        result_kernel,
        in_specs=[pl.BlockSpec(memory_space=pltpu.SMEM), vmem, vmem],
        out_specs=[vmem] * 3,
        out_shape=[
            jax.ShapeDtypeStruct((3, 192, 384), F32),
            jax.ShapeDtypeStruct((192, 384), F32),
            jax.ShapeDtypeStruct((192, 128), F32),
        ],
        compiler_params=params(),
    )(core, gathered, send(gathered, other_core))
    return taps, bias[:, 0], mix


def edges(chip, core):
    first, final = (chip == 0).astype(jnp.int32), (chip == 31).astype(jnp.int32)
    one, zero = jnp.int32(1), jnp.int32(0)
    return jnp.stack([zero, 1 - first, 1 - first, one, final, one, one, 1 - final, core])


def per_device(inputs, convolution_weight, conv_bias, mix_weight, cotangent):
    factor = 1.0 / math.sqrt(inputs.shape[0] * inputs.shape[2] * lax.axis_size("seq"))
    edge = edges((lax.axis_index("seq") >> 1) & 31, lax.axis_index("seq") & 1)
    field = (2, 2, 192, SIZE)
    column = jnp.stack([lax.axis_index("ch"), lax.axis_index("seq") >> 6]).astype(jnp.int32)
    here = [gather_column(inputs, column, k) for k in range(CHUNKS)]
    weights = pack_weights(convolution_weight, mix_weight, conv_bias, here[-1])
    weights = gather_weights(weights, lax.axis_index("ch"), lax.axis_index("seq") & 1)
    cot = [exchange(pack(cotangent, k, weights)).reshape(field) for k in range(CHUNKS)]
    sides = [(send(a, chips_on(1)), send(a, chips_on(-1))) for a in here]
    sums, acts, grads, grad_sides = (), [], [], []
    for k in range(CHUNKS):
        act, grad, *sums = middle(edge, sides[k][0], here[k], sides[k][1], cot[k], weights)
        acts.append(act)
        grads.append(grad)
        grad_sides.append((send(grad, chips_on(1)), send(grad, chips_on(-1))))

    def flat(piece):
        return piece.reshape(4, 192, SIZE)

    mine = sum_in_column(*sums)
    outs = [exchange(flat(mixed(edge, here[k], acts[k], weights))) for k in range(CHUNKS)]
    total = scatter_over_z(mine).astype(BF16)
    input_grads = [
        back(edge, grad_sides[k][0], grads[k], grad_sides[k][1], cot[k], weights, *outs, total)
        for k in range(CHUNKS)
    ]
    input_parts = [exchange(flat(p)) for p in input_grads]
    outputs, input_grad = unpack(outs), unpack(input_parts)
    total = total.astype(F32) + send(total, flip(32)).astype(F32)
    total = add_flips(rounded(total, *input_grads), 2, 4)
    gathered = gather_over_z((total * factor).astype(BF16))
    weight_grad, bias_grad, mix_grad = results(gathered)
    return outputs, input_grad, weight_grad, bias_grad, mix_grad


def solution(mesh):
    in_specs = (
        P(None, "ch", "seq"),
        P(None, "ch", None),
        P("ch"),
        P("ch", None),
        P(None, "ch", "seq"),
    )
    out_specs = (
        P(None, "ch", "seq"),
        P(None, "ch", "seq"),
        P(None, "ch", None),
        P("ch"),
        P("ch", None),
    )
    return jax.shard_map(
        per_device, mesh=mesh, in_specs=in_specs, out_specs=out_specs, check_vma=False
    )
```

time: 213 us -> 178 us (0.84)
  the two profiles are of different devices: /device:TPU:34 before, /device:TPU:1 now
where the time goes in v2:
time: 178 us
  waiting for transfers between devices  72.4 us (41%)
  starting transfers between devices  63.1 us (35%)
  Pallas kernels  26.8 us (15%)
  local copies, waits for them, and re-layouts  11.2 us (6%)
  other arithmetic  3.32 us (2%)
    ppermute x24, waiting for transfers between devices, send(): return lax.ppermute(block, AXES, route(target))  72.4 us
    ppermute x24, starting transfers between devices, send(): return lax.ppermute(block, AXES, route(target))  50.9 us
    all_to_all x3, starting transfers between devices, exchange(): return lax.all_to_all(block, AXES, 0, 0, axis_index_groups=column_groups())  12.2 us
    pallas_call x1, Pallas kernels, middle(): pl.pallas_call(middle_kernel, grid_spec=pltpu.PrefetchScalarGridSpec(num_...  11.2 us
    unnamed x22, local copies, waits for them, and re-layouts  9.19 us
    pallas_call x1, Pallas kernels, back(): pl.pallas_call(back_kernel, grid_spec=pltpu.PrefetchScalarGridSpec(num_sc...  5.98 us
  transfers between devices with their start and end apart: 27, of which 17 were waited for; matrix products, arithmetic and copies ran while one was open for 3% of the time, Pallas kernels for 7%

profile of v2, /device:TPU:1, one launch (start us, length us, event | category | flops | bytes accessed | tf_op | source)
XLA Modules:
  0.0 177.7 jit_solution(13499452186372606744)
XLA Ops:
  0.7 1.4 copy-done
  2.1 0.6 shard_map.92
  2.8 2.2 %collective-permute-start = (bf16[192,1024]{1,0:T(8,128)(2,1)S(1)}, bf16[192,1024]{1,0:T(8,128)(2,1)S(1)}, u32[]{:S(2)}, u32[]{:S(2)}) collective-permute-start(bf16[192,1024]{1,0:T(8,128)(2,1)S(1)} %get-tuple-element.19), channel_id=1, source_target_pairs={{0,128},{1,129},{2,130},{3,131},{4,132},{5,133},{6,134},{7,135},{8... | collective-permute-start | bytes 1179656 | tf_op jit(solution)/shard_map/ppermute | solution.py:29
  5.0 2.6 %collective-permute-start.1 = (bf16[192,1024]{1,0:T(8,128)(2,1)S(1)}, bf16[192,1024]{1,0:T(8,128)(2,1)S(1)}, u32[]{:S(2)}, u32[]{:S(2)}) collective-permute-start(bf16[192,1024]{1,0:T(8,128)(2,1)S(1)} %get-tuple-element.20), channel_id=1, source_target_pairs={{0,1},{1,0},{2,3},{3,2},{4,5},{5,4},{6,7},{7,6},{8,9},{9,8},{10,11... | collective-permute-start | bytes 1179656 | tf_op jit(solution)/shard_map/ppermute | solution.py:29
  7.6 0.1 copy.10.bias
  7.7 4.8 %collective-permute-done.low = bf16[192,1024]{1,0:T(8,128)(2,1)S(1)} collective-permute-done((bf16[192,1024]{1,0:T(8,128)(2,1)S(1)}, bf16[192,1024]{1,0:T(8,128)(2,1)S(1)}, u32[]{:S(2)}, u32[]{:S(2)}) %collective-permute-start) | collective-permute-done | bytes 393248 | tf_op jit(solution)/shard_map/ppermute | solution.py:29
  12.6 12.0 %collective-permute-done.1.half = bf16[192,1024]{1,0:T(8,128)(2,1)S(1)} collective-permute-done((bf16[192,1024]{1,0:T(8,128)(2,1)S(1)}, bf16[192,1024]{1,0:T(8,128)(2,1)S(1)}, u32[]{:S(2)}, u32[]{:S(2)}) %collective-permute-start.1) | collective-permute-done | bytes 393248 | tf_op jit(solution)/shard_map/ppermute | solution.py:29
  24.6 2.0 %collective-permute-done.2.both = bf16[192,1024]{1,0:T(8,128)(2,1)S(1)} collective-permute-done((bf16[192,1024]{1,0:T(8,128)(2,1)S(1)}, bf16[192,1024]{1,0:T(8,128)(2,1)S(1)}, u32[]{:S(2)}, u32[]{:S(2)}) %collective-permute-start.2) | collective-permute-done | bytes 393248 | tf_op jit(solution)/shard_map/ppermute | solution.py:29
  26.6 0.6 shard_map.93.refs_0_.here
  27.3 0.4 copy-done.8
  27.7 0.1 shard_map.94.own
  27.8 0.1 collective-permute-start.5
  27.9 1.3 collective-permute-start.3
  29.2 6.6 %collective-permute-start.4 = (bf16[2,2,192,1024]{3,2,1,0:T(8,128)(2,1)S(1)}, bf16[2,2,192,1024]{3,2,1,0:T(8,128)(2,1)}, u32[]{:S(2)}, u32[]{:S(2)}) collective-permute-start(bf16[2,2,192,1024]{3,2,1,0:T(8,128)(2,1)S(1)} %shard_map.93.refs_0_.here), channel_id=1, source_target_pairs={{0,124},{1,125},{2,126},{3,127},{4,0},{5,1},{6,2},{7,3},{8,4},{9,5... | collective-permute-start | bytes 4718600 | tf_op jit(solution)/shard_map/ppermute | solution.py:29
  35.9 0.4 collective-permute-done.5.straight
  36.3 3.1 %collective-permute-start.6 = (bf16[96,1664]{1,0:T(8,128)(2,1)S(1)}, bf16[96,1664]{1,0:T(8,128)(2,1)S(1)}, u32[]{:S(2)}, u32[]{:S(2)}) collective-permute-start(bf16[96,1664]{1,0:T(8,128)(2,1)S(1)} %collective-permute-done.5.straight), channel_id=1, source_target_pairs={{0,2},{1,3},{2,0},{3,1},{4,6},{5,7},{6,4},{7,5},{8,10},{9,11},{10,... | collective-permute-start | bytes 958472 | tf_op jit(solution)/shard_map/ppermute | solution.py:29
  39.4 1.2 collective-permute-done.6.crossed
  40.6 0.6 shard_map.95.refs_0_.weights
  41.3 0.4 shard_map.96
  41.7 1.1 copy-done.3
  42.8 4.3 %all-to-all-start = ((bf16[4,192,1024]{2,1,0:T(8,128)(2,1)}), bf16[4,192,1024]{2,1,0:T(8,128)(2,1)}, u32[]{:S(2)}, u32[]{:S(2)}) async-start(bf16[4,192,1024]{2,1,0:T(8,128)(2,1)} %copy-done.3), calls=%async_computation | async-start | bytes 3145728 | tf_op jit(solution)/shard_map/all_to_all | solution.py:53
  47.3 21.2 %collective-permute-done.3.behind = bf16[2,2,192,1024]{3,2,1,0:T(8,128)(2,1)} collective-permute-done((bf16[2,2,192,1024]{3,2,1,0:T(8,128)(2,1)S(1)}, bf16[2,2,192,1024]{3,2,1,0:T(8,128)(2,1)}, u32[]{:S(2)}, u32[]{:S(2)}) %collective-permute-start.3) | collective-permute-done | bytes 1572896 | tf_op jit(solution)/shard_map/ppermute | solution.py:29
  68.4 11.2 %shard_map.97 = (bf16[2,2,192,1024]{3,2,1,0:T(8,128)(2,1)S(1)}, bf16[2,2,192,1024]{3,2,1,0:T(8,128)(2,1)}, f32[2,96,1664]{2,1,0:T(8,128)S(1)}, f32[2,96,1664]{2,1,0:T(8,128)S(1)}) custom-call(s32[9]{0:T(128)S(1)} %stack.34.edge, bf16[2,2,192,1024]{3,2,1,0:T(8,128)(2,1)} %collective-permute-done.3.behind, ...), custom_call_target="tpu_custom_call" | custom-call | flops 5435817984 | bytes 9437184 | tf_op jit(solution)/shard_map/pallas_call | solution.py:263
  79.7 1.1 copy-done.6
  80.8 2.8 %collective-permute-start.9 = (f32[2,96,1664]{2,1,0:T(8,128)S(1)}, f32[2,96,1664]{2,1,0:T(8,128)S(1)}, u32[]{:S(2)}, u32[]{:S(2)}) collective-permute-start(f32[2,96,1664]{2,1,0:T(8,128)S(1)} %get-tuple-element.25), channel_id=1, source_target_pairs={{0,2},{1,3},{2,0},{3,1},{4,6},{5,7},{6,4},{7,5},{8,10},{9,11},{10,... | collective-permute-start | bytes 3833864 | tf_op jit(solution)/shard_map/ppermute | solution.py:29
  83.6 2.6 %collective-permute-done.9.received = f32[2,96,1664]{2,1,0:T(8,128)S(1)} collective-permute-done((f32[2,96,1664]{2,1,0:T(8,128)S(1)}, f32[2,96,1664]{2,1,0:T(8,128)S(1)}, u32[]{:S(2)}, u32[]{:S(2)}) %collective-permute-start.9) | collective-permute-done | bytes 1277984 | tf_op jit(solution)/shard_map/ppermute | solution.py:29
  86.2 0.1 shard_map.100
  86.3 0.6 collective-permute-start.10
  87.0 2.4 %collective-permute-start.11 = (bf16[96,1664]{1,0:T(8,128)(2,1)S(1)}, bf16[96,1664]{1,0:T(8,128)(2,1)}, u32[]{:S(2)}, u32[]{:S(2)}) collective-permute-start(bf16[96,1664]{1,0:T(8,128)(2,1)S(1)} %get-tuple-element.27), channel_id=1, source_target_pairs={{0,1},{1,0},{2,3},{3,2},{4,5},{5,4},{6,7},{7,6},{8,9},{9,8},{10,11... | collective-permute-start | bytes 958472 | tf_op jit(solution)/shard_map/ppermute | solution.py:29
  89.4 0.9 collective-permute-start.12
  90.3 5.4 %collective-permute-start.8 = (bf16[2,2,192,1024]{3,2,1,0:T(8,128)(2,1)}, bf16[2,2,192,1024]{3,2,1,0:T(8,128)(2,1)}, u32[]{:S(2)}, u32[]{:S(2)}) collective-permute-start(bf16[2,2,192,1024]{3,2,1,0:T(8,128)(2,1)} %get-tuple-element.23.here), channel_id=1, source_target_pairs={{0,124},{1,125},{2,126},{3,127},{4,0},{5,1},{6,2},{7,3},{8,4},{9,5... | collective-permute-start | bytes 4718600 | tf_op jit(solution)/shard_map/ppermute | solution.py:29
  95.7 1.4 copy-done.7
  97.1 2.4 %shard_map.98 = bf16[2,2,192,1024]{3,2,1,0:T(8,128)(2,1)S(1)} custom-call(s32[9]{0:T(128)S(1)} %stack.34.edge, bf16[2,2,192,1024]{3,2,1,0:T(8,128)(2,1)S(1)} %shard_map.93.refs_0_.here, bf16[2,2,192,1024]{3,2,1,0:T(8,128)(2,1)S(1)} %copy-done.7, bf16[384,1664]{1,0:T(8,128)(2,1)S(1)} %shard_map.95.refs_0_.weights), custom_call_target="tpu_custom_call" | custom-call | flops 603979776 | bytes 4718592 | tf_op jit(solution)/shard_map/pallas_call | solution.py:288
  99.5 1.1 copy-done.4
  100.7 3.6 %all-to-all-start.1 = ((bf16[4,192,1024]{2,1,0:T(8,128)(2,1)}), bf16[4,192,1024]{2,1,0:T(8,128)(2,1)S(1)}, u32[]{:S(2)}, u32[]{:S(2)}) async-start(bf16[4,192,1024]{2,1,0:T(8,128)(2,1)} %bitcast.30), calls=%async_computation.1 | async-start | bytes 3145728 | tf_op jit(solution)/shard_map/all_to_all | solution.py:53
  104.2 1.7 collective-permute-done.12
  106.0 2.1 %add_add_fusion = f32[96,1664]{1,0:T(8,128)} fusion(bf16[96,1664]{1,0:T(8,128)(2,1)} %collective-permute-done.12, bf16[96,1664]{1,0:T(8,128)(2,1)} %collective-permute-done.11, bf16[96,1664]{1,0:T(8,128)(2,1)} %collective-permute-done.10, bf16[96,1664]{1,0:T(8,128)(2,1)S(1)} %get-tuple-element.26), kind=kLoop, calls=%fused_computation | loop fusion | flops 1118208 | bytes 1916928 | tf_op jit(solution)/shard_map/add | solution.py:381
  108.1 1.1 fusion.3
  109.2 0.3 collective-permute-start.13
  109.5 1.0 collective-permute-start.14
  110.5 2.5 %collective-permute-start.15 = (bf16[24,1664]{1,0:T(8,128)(2,1)S(1)}, bf16[24,1664]{1,0:T(8,128)(2,1)S(1)}, u32[]{:S(2)}, u32[]{:S(2)}) collective-permute-start(bf16[24,1664]{1,0:T(8,128)(2,1)S(1)} %get-tuple-element.32), channel_id=1, source_target_pairs={{0,48},{1,49},{2,50},{3,51},{4,52},{5,53},{6,54},{7,55},{8,56},{9,... | collective-permute-start | bytes 239624 | tf_op jit(solution)/shard_map/ppermute | solution.py:29
  113.0 15.4 %collective-permute-done.13 = bf16[24,1664]{1,0:T(8,128)(2,1)S(1)} collective-permute-done((bf16[24,1664]{1,0:T(8,128)(2,1)S(1)}, bf16[24,1664]{1,0:T(8,128)(2,1)S(1)}, u32[]{:S(2)}, u32[]{:S(2)}) %collective-permute-start.13) | collective-permute-done | bytes 79904 | tf_op jit(solution)/shard_map/ppermute | solution.py:29
  128.4 1.0 collective-permute-done.14
  129.4 4.4 %collective-permute-done.15 = bf16[24,1664]{1,0:T(8,128)(2,1)S(1)} collective-permute-done((bf16[24,1664]{1,0:T(8,128)(2,1)S(1)}, bf16[24,1664]{1,0:T(8,128)(2,1)S(1)}, u32[]{:S(2)}, u32[]{:S(2)}) %collective-permute-start.15) | collective-permute-done | bytes 79904 | tf_op jit(solution)/shard_map/ppermute | solution.py:29
  133.8 1.0 fusion.2.refs_1_
  134.8 4.3 %collective-permute-start.16 = (bf16[24,1664]{1,0:T(8,128)(2,1)S(1)}, bf16[24,1664]{1,0:T(8,128)(2,1)S(1)}, u32[]{:S(2)}, u32[]{:S(2)}) collective-permute-start(bf16[24,1664]{1,0:T(8,128)(2,1)S(1)} %fusion.2.refs_1_), channel_id=1, source_target_pairs={{0,64},{1,65},{2,66},{3,67},{4,68},{5,69},{6,70},{7,71},{8,72},{9,... | collective-permute-start | bytes 239624 | tf_op jit(solution)/shard_map/ppermute | solution.py:29
  139.1 6.0 %shard_map.101.refs_0_ = bf16[2,2,192,1024]{3,2,1,0:T(8,128)(2,1)S(1)} custom-call(s32[9]{0:T(128)S(1)} %stack.34.edge, bf16[2,2,192,1024]{3,2,1,0:T(8,128)(2,1)} %collective-permute-done.7.behind, bf16[2,2,192,1024]{3,2,1,0:T(8,128)(2,1)} %get-tuple-element.23.here, bf16[2,2,192,1024]{3,2,1,0:T(8,128)(2,1)} %collective-permute-done.8.ahead, ...), custom_call_target="tpu_custom_call" | custom-call | flops 1811939328 | bytes 7864320 | tf_op jit(solution)/shard_map/pallas_call | solution.py:324
  145.1 1.1 copy-done.1
  146.2 4.3 %all-to-all-start.2 = ((bf16[4,192,1024]{2,1,0:T(8,128)(2,1)}), bf16[4,192,1024]{2,1,0:T(8,128)(2,1)}, u32[]{:S(2)}, u32[]{:S(2)}) async-start(bf16[4,192,1024]{2,1,0:T(8,128)(2,1)} %bitcast.29), calls=%async_computation.2 | async-start | bytes 3145728 | tf_op jit(solution)/shard_map/all_to_all | solution.py:53
  150.6 1.4 copy-done.2
  152.3 3.7 %collective-permute-start.19 = (bf16[24,1664]{1,0:T(8,128)(2,1)S(1)}, bf16[24,1664]{1,0:T(8,128)(2,1)S(1)}, u32[]{:S(2)}, u32[]{:S(2)}) collective-permute-start(bf16[24,1664]{1,0:T(8,128)(2,1)S(1)} %shard_map.103), channel_id=1, source_target_pairs={{0,12},{1,13},{2,14},{3,15},{4,8},{5,9},{6,10},{7,11},{8,4},{9,5},... | collective-permute-start | bytes 239624 | tf_op jit(solution)/shard_map/ppermute | solution.py:29
  156.0 1.0 collective-permute-done.18
  157.0 0.8 collective-permute-done.19
  157.9 0.1 collective-permute-start.20
  158.0 2.1 %collective-permute-start.21 = (bf16[24,1664]{1,0:T(8,128)(2,1)S(1)}, bf16[24,1664]{1,0:T(8,128)(2,1)S(1)}, u32[]{:S(2)}, u32[]{:S(2)}) collective-permute-start(bf16[24,1664]{1,0:T(8,128)(2,1)S(1)} %multiply_convert_fusion.refs_0_), channel_id=1, source_target_pairs={{0,32},{1,33},{2,34},{3,35},{4,36},{5,37},{6,38},{7,39},{8,40},{9,... | collective-permute-start | bytes 239624 | tf_op jit(solution)/shard_map/ppermute | solution.py:29
  160.1 1.5 collective-permute-start.22
  161.6 0.1 collective-permute-done.20.refs_1_
  161.7 1.0 collective-permute-done.21.refs_2_
  162.7 2.6 %collective-permute-done.22.refs_3_ = bf16[24,1664]{1,0:T(8,128)(2,1)S(1)} collective-permute-done((bf16[24,1664]{1,0:T(8,128)(2,1)S(1)}, bf16[24,1664]{1,0:T(8,128)(2,1)S(1)}, u32[]{:S(2)}, u32[]{:S(2)}) %collective-permute-start.22) | collective-permute-done | bytes 79904 | tf_op jit(solution)/shard_map/ppermute | solution.py:29
  165.3 7.1 %collective-permute-start.23 = (bf16[4,24,1664]{2,1,0:T(8,128)(2,1)S(1)}, bf16[4,24,1664]{2,1,0:T(8,128)(2,1)S(1)}, u32[]{:S(2)}, u32[]{:S(2)}) collective-permute-start(bf16[4,24,1664]{2,1,0:T(8,128)(2,1)S(1)} %shard_map.104.own), channel_id=1, source_target_pairs={{0,2},{1,3},{2,0},{3,1},{4,6},{5,7},{6,4},{7,5},{8,10},{9,11},{10,... | collective-permute-start | bytes 958472 | tf_op jit(solution)/shard_map/ppermute | solution.py:29
  172.4 1.2 shard_map.99
  173.6 1.1 shard_map.105
  174.7 0.7 slice_reduce_fusion
  175.4 2.3 %shard_map.102 = bf16[2,192,2048]{2,1,0:T(8,128)(2,1)} custom-call(bf16[4,192,1024]{2,1,0:T(8,128)(2,1)} %all-to-all-done.2.source), custom_call_target="tpu_custom_call" | custom-call | bytes 3145728 | tf_op jit(solution)/shard_map/pallas_call | solution.py:144
  (38 shorter events, 0.7 us)
Async XLA Ops:
  0.7 1.4 copy-start
  2.1 5.5 %copy-start.10 = (f32[192]{0:T(256)S(1)}, f32[192]{0:T(256)}, u32[]{:S(2)}) copy-start(f32[192]{0:T(256)} %param.7) | copy-start | bytes 2308
  2.8 9.8 %collective-permute-start = (bf16[192,1024]{1,0:T(8,128)(2,1)S(1)}, bf16[192,1024]{1,0:T(8,128)(2,1)S(1)}, u32[]{:S(2)}, u32[]{:S(2)}) collective-permute-start(bf16[192,1024]{1,0:T(8,128)(2,1)S(1)} %get-tuple-element.19), channel_id=1, source_target_pairs={{0,128},{1,129},{2,130},{3,131},{4,132},{5,133},{6,134},{7,135},{8... | collective-permute-start | bytes 1179656 | tf_op jit(solution)/shard_map/ppermute | solution.py:29
  5.0 19.6 %collective-permute-start.1 = (bf16[192,1024]{1,0:T(8,128)(2,1)S(1)}, bf16[192,1024]{1,0:T(8,128)(2,1)S(1)}, u32[]{:S(2)}, u32[]{:S(2)}) collective-permute-start(bf16[192,1024]{1,0:T(8,128)(2,1)S(1)} %get-tuple-element.20), channel_id=1, source_target_pairs={{0,1},{1,0},{2,3},{3,2},{4,5},{5,4},{6,7},{7,6},{8,9},{9,8},{10,11... | collective-permute-start | bytes 1179656 | tf_op jit(solution)/shard_map/ppermute | solution.py:29
  7.6 19.0 %collective-permute-start.2 = (bf16[192,1024]{1,0:T(8,128)(2,1)S(1)}, bf16[192,1024]{1,0:T(8,128)(2,1)S(1)}, u32[]{:S(2)}, u32[]{:S(2)}) collective-permute-start(bf16[192,1024]{1,0:T(8,128)(2,1)S(1)} %get-tuple-element.21), channel_id=1, source_target_pairs={{0,129},{1,128},{2,131},{3,130},{4,133},{5,132},{6,135},{7,134},{8... | collective-permute-start | bytes 1179656 | tf_op jit(solution)/shard_map/ppermute | solution.py:29
  26.6 1.0 copy-start.8
  26.6 1.0 copy-start.9
  27.8 13.5 %copy-start.5 = (bf16[2,192,2048]{2,1,0:T(8,128)(2,1)S(1)}, bf16[2,192,2048]{2,1,0:T(8,128)(2,1)}, u32[]{:S(2)}) copy-start(bf16[2,192,2048]{2,1,0:T(8,128)(2,1)} %source.1) | copy-start | bytes 4718596
  27.8 8.5 %collective-permute-start.5 = (bf16[96,1664]{1,0:T(8,128)(2,1)S(1)}, bf16[96,1664]{1,0:T(8,128)(2,1)S(1)}, u32[]{:S(2)}, u32[]{:S(2)}) collective-permute-start(bf16[96,1664]{1,0:T(8,128)(2,1)S(1)} %dynamic-slice_bitcast_fusion), channel_id=1, source_target_pairs={{0,1},{1,0},{2,3},{3,2},{4,5},{5,4},{6,7},{7,6},{8,9},{9,8},{10,11... | collective-permute-start | bytes 958472 | tf_op jit(solution)/shard_map/ppermute | solution.py:29
  27.9 40.5 %collective-permute-start.3 = (bf16[2,2,192,1024]{3,2,1,0:T(8,128)(2,1)S(1)}, bf16[2,2,192,1024]{3,2,1,0:T(8,128)(2,1)}, u32[]{:S(2)}, u32[]{:S(2)}) collective-permute-start(bf16[2,2,192,1024]{3,2,1,0:T(8,128)(2,1)S(1)} %shard_map.93.refs_0_.here), channel_id=1, source_target_pairs={{0,4},{1,5},{2,6},{3,7},{4,8},{5,9},{6,10},{7,11},{8,12},{9,13},{1... | collective-permute-start | bytes 4718600 | tf_op jit(solution)/shard_map/ppermute | solution.py:29
  29.2 39.2 %collective-permute-start.4 = (bf16[2,2,192,1024]{3,2,1,0:T(8,128)(2,1)S(1)}, bf16[2,2,192,1024]{3,2,1,0:T(8,128)(2,1)}, u32[]{:S(2)}, u32[]{:S(2)}) collective-permute-start(bf16[2,2,192,1024]{3,2,1,0:T(8,128)(2,1)S(1)} %shard_map.93.refs_0_.here), channel_id=1, source_target_pairs={{0,124},{1,125},{2,126},{3,127},{4,0},{5,1},{6,2},{7,3},{8,4},{9,5... | collective-permute-start | bytes 4718600 | tf_op jit(solution)/shard_map/ppermute | solution.py:29
  36.3 4.3 %collective-permute-start.6 = (bf16[96,1664]{1,0:T(8,128)(2,1)S(1)}, bf16[96,1664]{1,0:T(8,128)(2,1)S(1)}, u32[]{:S(2)}, u32[]{:S(2)}) collective-permute-start(bf16[96,1664]{1,0:T(8,128)(2,1)S(1)} %collective-permute-done.5.straight), channel_id=1, source_target_pairs={{0,2},{1,3},{2,0},{3,1},{4,6},{5,7},{6,4},{7,5},{8,10},{9,11},{10,... | collective-permute-start | bytes 958472 | tf_op jit(solution)/shard_map/ppermute | solution.py:29
  41.7 1.1 copy-start.3
  42.8 25.6 %all-to-all-start = ((bf16[4,192,1024]{2,1,0:T(8,128)(2,1)}), bf16[4,192,1024]{2,1,0:T(8,128)(2,1)}, u32[]{:S(2)}, u32[]{:S(2)}) async-start(bf16[4,192,1024]{2,1,0:T(8,128)(2,1)} %copy-done.3), calls=%async_computation | async-start | bytes 3145728 | tf_op jit(solution)/shard_map/all_to_all | solution.py:53
  79.7 1.1 copy-start.6
  80.8 5.4 %collective-permute-start.9 = (f32[2,96,1664]{2,1,0:T(8,128)S(1)}, f32[2,96,1664]{2,1,0:T(8,128)S(1)}, u32[]{:S(2)}, u32[]{:S(2)}) collective-permute-start(f32[2,96,1664]{2,1,0:T(8,128)S(1)} %get-tuple-element.25), channel_id=1, source_target_pairs={{0,2},{1,3},{2,0},{3,1},{4,6},{5,7},{6,4},{7,5},{8,10},{9,11},{10,... | collective-permute-start | bytes 3833864 | tf_op jit(solution)/shard_map/ppermute | solution.py:29
  86.3 17.9 %collective-permute-start.10 = (bf16[96,1664]{1,0:T(8,128)(2,1)S(1)}, bf16[96,1664]{1,0:T(8,128)(2,1)}, u32[]{:S(2)}, u32[]{:S(2)}) collective-permute-start(bf16[96,1664]{1,0:T(8,128)(2,1)S(1)} %get-tuple-element.26), channel_id=1, source_target_pairs={{0,128},{1,129},{2,130},{3,131},{4,132},{5,133},{6,134},{7,135},{8... | collective-permute-start | bytes 958472 | tf_op jit(solution)/shard_map/ppermute | solution.py:29
  87.0 17.3 %collective-permute-start.11 = (bf16[96,1664]{1,0:T(8,128)(2,1)S(1)}, bf16[96,1664]{1,0:T(8,128)(2,1)}, u32[]{:S(2)}, u32[]{:S(2)}) collective-permute-start(bf16[96,1664]{1,0:T(8,128)(2,1)S(1)} %get-tuple-element.27), channel_id=1, source_target_pairs={{0,1},{1,0},{2,3},{3,2},{4,5},{5,4},{6,7},{7,6},{8,9},{9,8},{10,11... | collective-permute-start | bytes 958472 | tf_op jit(solution)/shard_map/ppermute | solution.py:29
  89.4 16.6 %collective-permute-start.12 = (bf16[96,1664]{1,0:T(8,128)(2,1)S(1)}, bf16[96,1664]{1,0:T(8,128)(2,1)}, u32[]{:S(2)}, u32[]{:S(2)}) collective-permute-start(bf16[96,1664]{1,0:T(8,128)(2,1)S(1)} %get-tuple-element.27), channel_id=1, source_target_pairs={{0,129},{1,128},{2,131},{3,130},{4,133},{5,132},{6,135},{7,134},{8... | collective-permute-start | bytes 958472 | tf_op jit(solution)/shard_map/ppermute | solution.py:29
  90.3 48.8 %collective-permute-start.7 = (bf16[2,2,192,1024]{3,2,1,0:T(8,128)(2,1)}, bf16[2,2,192,1024]{3,2,1,0:T(8,128)(2,1)}, u32[]{:S(2)}, u32[]{:S(2)}) collective-permute-start(bf16[2,2,192,1024]{3,2,1,0:T(8,128)(2,1)} %get-tuple-element.23.here), channel_id=1, source_target_pairs={{0,4},{1,5},{2,6},{3,7},{4,8},{5,9},{6,10},{7,11},{8,12},{9,13},{1... | collective-permute-start | bytes 4718600 | tf_op jit(solution)/shard_map/ppermute | solution.py:29
  90.3 48.8 %collective-permute-start.8 = (bf16[2,2,192,1024]{3,2,1,0:T(8,128)(2,1)}, bf16[2,2,192,1024]{3,2,1,0:T(8,128)(2,1)}, u32[]{:S(2)}, u32[]{:S(2)}) collective-permute-start(bf16[2,2,192,1024]{3,2,1,0:T(8,128)(2,1)} %get-tuple-element.23.here), channel_id=1, source_target_pairs={{0,124},{1,125},{2,126},{3,127},{4,0},{5,1},{6,2},{7,3},{8,4},{9,5... | collective-permute-start | bytes 4718600 | tf_op jit(solution)/shard_map/ppermute | solution.py:29
  95.7 1.4 copy-start.7
  99.5 1.1 copy-start.4
  100.7 38.4 %all-to-all-start.1 = ((bf16[4,192,1024]{2,1,0:T(8,128)(2,1)}), bf16[4,192,1024]{2,1,0:T(8,128)(2,1)S(1)}, u32[]{:S(2)}, u32[]{:S(2)}) async-start(bf16[4,192,1024]{2,1,0:T(8,128)(2,1)} %bitcast.30), calls=%async_computation.1 | async-start | bytes 3145728 | tf_op jit(solution)/shard_map/all_to_all | solution.py:53
  109.2 19.2 %collective-permute-start.13 = (bf16[24,1664]{1,0:T(8,128)(2,1)S(1)}, bf16[24,1664]{1,0:T(8,128)(2,1)S(1)}, u32[]{:S(2)}, u32[]{:S(2)}) collective-permute-start(bf16[24,1664]{1,0:T(8,128)(2,1)S(1)} %get-tuple-element.31), channel_id=1, source_target_pairs={{0,16},{1,17},{2,18},{3,19},{4,20},{5,21},{6,22},{7,23},{8,24},{9,... | collective-permute-start | bytes 239624 | tf_op jit(solution)/shard_map/ppermute | solution.py:29
  109.5 19.9 %collective-permute-start.14 = (bf16[24,1664]{1,0:T(8,128)(2,1)S(1)}, bf16[24,1664]{1,0:T(8,128)(2,1)S(1)}, u32[]{:S(2)}, u32[]{:S(2)}) collective-permute-start(bf16[24,1664]{1,0:T(8,128)(2,1)S(1)} %get-tuple-element.33), channel_id=1, source_target_pairs={{0,32},{1,33},{2,34},{3,35},{4,36},{5,37},{6,38},{7,39},{8,40},{9,... | collective-permute-start | bytes 239624 | tf_op jit(solution)/shard_map/ppermute | solution.py:29
  110.5 23.3 %collective-permute-start.15 = (bf16[24,1664]{1,0:T(8,128)(2,1)S(1)}, bf16[24,1664]{1,0:T(8,128)(2,1)S(1)}, u32[]{:S(2)}, u32[]{:S(2)}) collective-permute-start(bf16[24,1664]{1,0:T(8,128)(2,1)S(1)} %get-tuple-element.32), channel_id=1, source_target_pairs={{0,48},{1,49},{2,50},{3,51},{4,52},{5,53},{6,54},{7,55},{8,56},{9,... | collective-permute-start | bytes 239624 | tf_op jit(solution)/shard_map/ppermute | solution.py:29
  134.8 15.8 %collective-permute-start.16 = (bf16[24,1664]{1,0:T(8,128)(2,1)S(1)}, bf16[24,1664]{1,0:T(8,128)(2,1)S(1)}, u32[]{:S(2)}, u32[]{:S(2)}) collective-permute-start(bf16[24,1664]{1,0:T(8,128)(2,1)S(1)} %fusion.2.refs_1_), channel_id=1, source_target_pairs={{0,64},{1,65},{2,66},{3,67},{4,68},{5,69},{6,70},{7,71},{8,72},{9,... | collective-permute-start | bytes 239624 | tf_op jit(solution)/shard_map/ppermute | solution.py:29
  145.1 1.1 copy-start.1
  146.2 29.2 %all-to-all-start.2 = ((bf16[4,192,1024]{2,1,0:T(8,128)(2,1)}), bf16[4,192,1024]{2,1,0:T(8,128)(2,1)}, u32[]{:S(2)}, u32[]{:S(2)}) async-start(bf16[4,192,1024]{2,1,0:T(8,128)(2,1)} %bitcast.29), calls=%async_computation.2 | async-start | bytes 3145728 | tf_op jit(solution)/shard_map/all_to_all | solution.py:53
  150.6 1.4 copy-start.2
  152.1 3.9 %collective-permute-start.17 = (bf16[24,1664]{1,0:T(8,128)(2,1)S(1)}, bf16[24,1664]{1,0:T(8,128)(2,1)S(1)}, u32[]{:S(2)}, u32[]{:S(2)}) collective-permute-start(bf16[24,1664]{1,0:T(8,128)(2,1)S(1)} %shard_map.103), channel_id=1, source_target_pairs={{0,4},{1,5},{2,6},{3,7},{4,0},{5,1},{6,2},{7,3},{8,12},{9,13},{10,... | collective-permute-start | bytes 239624 | tf_op jit(solution)/shard_map/ppermute | solution.py:29
  152.2 4.9 %collective-permute-start.18 = (bf16[24,1664]{1,0:T(8,128)(2,1)S(1)}, bf16[24,1664]{1,0:T(8,128)(2,1)S(1)}, u32[]{:S(2)}, u32[]{:S(2)}) collective-permute-start(bf16[24,1664]{1,0:T(8,128)(2,1)S(1)} %shard_map.103), channel_id=1, source_target_pairs={{0,8},{1,9},{2,10},{3,11},{4,12},{5,13},{6,14},{7,15},{8,0},{9,1},... | collective-permute-start | bytes 239624 | tf_op jit(solution)/shard_map/ppermute | solution.py:29
  152.3 5.6 %collective-permute-start.19 = (bf16[24,1664]{1,0:T(8,128)(2,1)S(1)}, bf16[24,1664]{1,0:T(8,128)(2,1)S(1)}, u32[]{:S(2)}, u32[]{:S(2)}) collective-permute-start(bf16[24,1664]{1,0:T(8,128)(2,1)S(1)} %shard_map.103), channel_id=1, source_target_pairs={{0,12},{1,13},{2,14},{3,15},{4,8},{5,9},{6,10},{7,11},{8,4},{9,5},... | collective-permute-start | bytes 239624 | tf_op jit(solution)/shard_map/ppermute | solution.py:29
  157.9 3.8 %collective-permute-start.20 = (bf16[24,1664]{1,0:T(8,128)(2,1)S(1)}, bf16[24,1664]{1,0:T(8,128)(2,1)S(1)}, u32[]{:S(2)}, u32[]{:S(2)}) collective-permute-start(bf16[24,1664]{1,0:T(8,128)(2,1)S(1)} %multiply_convert_fusion.refs_0_), channel_id=1, source_target_pairs={{0,16},{1,17},{2,18},{3,19},{4,20},{5,21},{6,22},{7,23},{8,24},{9,... | collective-permute-start | bytes 239624 | tf_op jit(solution)/shard_map/ppermute | solution.py:29
  158.0 4.7 %collective-permute-start.21 = (bf16[24,1664]{1,0:T(8,128)(2,1)S(1)}, bf16[24,1664]{1,0:T(8,128)(2,1)S(1)}, u32[]{:S(2)}, u32[]{:S(2)}) collective-permute-start(bf16[24,1664]{1,0:T(8,128)(2,1)S(1)} %multiply_convert_fusion.refs_0_), channel_id=1, source_target_pairs={{0,32},{1,33},{2,34},{3,35},{4,36},{5,37},{6,38},{7,39},{8,40},{9,... | collective-permute-start | bytes 239624 | tf_op jit(solution)/shard_map/ppermute | solution.py:29
  160.1 5.2 %collective-permute-start.22 = (bf16[24,1664]{1,0:T(8,128)(2,1)S(1)}, bf16[24,1664]{1,0:T(8,128)(2,1)S(1)}, u32[]{:S(2)}, u32[]{:S(2)}) collective-permute-start(bf16[24,1664]{1,0:T(8,128)(2,1)S(1)} %multiply_convert_fusion.refs_0_), channel_id=1, source_target_pairs={{0,48},{1,49},{2,50},{3,51},{4,52},{5,53},{6,54},{7,55},{8,56},{9,... | collective-permute-start | bytes 239624 | tf_op jit(solution)/shard_map/ppermute | solution.py:29
  165.3 8.3 %collective-permute-start.23 = (bf16[4,24,1664]{2,1,0:T(8,128)(2,1)S(1)}, bf16[4,24,1664]{2,1,0:T(8,128)(2,1)S(1)}, u32[]{:S(2)}, u32[]{:S(2)}) collective-permute-start(bf16[4,24,1664]{2,1,0:T(8,128)(2,1)S(1)} %shard_map.104.own), channel_id=1, source_target_pairs={{0,2},{1,3},{2,0},{3,1},{4,6},{5,7},{6,4},{7,5},{8,10},{9,11},{10,... | collective-permute-start | bytes 958472 | tf_op jit(solution)/shard_map/ppermute | solution.py:29

commit v3 on v2

--- a/solution.py
+++ b/solution.py
@@ -11,7 +11,7 @@
 AXES = ("seq", "ch")
 CHUNKS = 1
 SIZE = 1024 // CHUNKS
-TILE = 512
+TILE = 1024
 ROOT = math.sqrt(2.0 / math.pi)
 CUBE = 0.044715
 
@@ -42,7 +42,7 @@
 
 
 def chips_on(step):
-    return lambda s, h: ((s & 64) | ((s + 2 * step) & 63), h)
+    return lambda s, h: ((s & 64) | ((s + (2 - 4 * (s & 1)) * step) & 63), h)
 
 
 def column_groups():
@@ -135,9 +135,10 @@
     return join(place, own, send(low, other_low), send(half, other_ch), send(both, other_both))
 
 
-def unpack_kernel(source, target):
+def unpack_kernel(source, target, token):
     target[0, :, 0:1024] = source[0]
     target[0, :, 1024:2048] = source[1]
+    token[...] = jnp.zeros((8, 128), F32)
 
 
 def unpack(pieces):
@@ -145,8 +146,14 @@
         unpack_kernel,
         grid=(2,),
         in_specs=[pl.BlockSpec((2, 192, 1024), lambda d: (d, 0, 0))],
-        out_specs=pl.BlockSpec((1, 192, 2048), lambda d: (d, 0, 0)),
-        out_shape=jax.ShapeDtypeStruct((2, 192, 2048), BF16),
+        out_specs=[
+            pl.BlockSpec((1, 192, 2048), lambda d: (d, 0, 0)),
+            pl.BlockSpec((8, 128), lambda d: (0, 0)),
+        ],
+        out_shape=[
+            jax.ShapeDtypeStruct((2, 192, 2048), BF16),
+            jax.ShapeDtypeStruct((8, 128), F32),
+        ],
         compiler_params=params(),
         cost_estimate=pl.CostEstimate(flops=0, bytes_accessed=16 * 192 * 1024, transcendentals=0),
     )(pieces[0])
@@ -200,11 +207,17 @@
     return ref[...].reshape(384, TILE)
 
 
-def masked(ref, keep):
-    return jnp.where(keep == 1, rows(ref), jnp.zeros((384, TILE), BF16))
-
-
-def middle_kernel(edge, behind, here, ahead, cot, weights, *refs):
+def neighbours(first, second, edge):
+    group, core = pl.program_id(0), edge[8]
+    first, second = rows(first), rows(second)
+    nothing = jnp.zeros((384, TILE), BF16)
+    behind = jnp.where(core == 0, first, second)
+    ahead = jnp.where(core == 0, second, first)
+    behind = jnp.where(edge[2 + group] == 1, behind, nothing)
+    return behind, jnp.where(edge[6 + group] == 1, ahead, nothing)
+
+
+def middle_kernel(edge, first, here, second, cot, weights, *refs):
     act_out, grad_pre, own, theirs, sums = refs
     group = pl.program_id(0)
 
@@ -213,9 +226,8 @@
         sums[...] = jnp.zeros((384, 1664), F32)
 
     center = rows(here)
-    field = jnp.concatenate(
-        [masked(behind, edge[2 + group]), center, masked(ahead, edge[6 + group])], axis=0
-    )
+    before, after = neighbours(first, second, edge)
+    field = jnp.concatenate([before, center, after], axis=0)
     bias = weights[:, 1536:1664].astype(F32)
     bias = bias[:, 0:1] + bias[:, 1:2] + bias[:, 2:3]
     pre = dot(weights[:, 0:1152], field) + bias
@@ -278,7 +290,14 @@
 
 
 def mix_kernel(edge, here, act, weights, *refs):
-    out = refs[-1]
+    out, taps = refs[-2:]
+
+    @pl.when((pl.program_id(0) == 0) & (pl.program_id(1) == 0))
+    def _():
+        for k in range(3):
+            tap = weights[:, 384 * (2 - k) : 384 * (3 - k)]
+            taps[:, 384 * k : 384 * (k + 1)] = tap.T
+
     result = rows(here).astype(F32) + dot(weights[:, 1152:1536], rows(act))
     out[...] = result.astype(BF16).reshape(out.shape)
 
@@ -292,9 +311,12 @@
             grid=(2, SIZE // TILE),
             in_specs=[plain, plain, whole(weights)]
             + [pl.BlockSpec(memory_space=pl.ANY)] * len(after),
-            out_specs=plain,
-        ),
-        out_shape=jax.ShapeDtypeStruct((2, 2, 192, SIZE), BF16),
+            out_specs=[plain, pl.BlockSpec((384, 1152), lambda g, i, edge: (0, 0))],
+        ),
+        out_shape=[
+            pltpu.HBM((2, 2, 192, SIZE), BF16),
+            jax.ShapeDtypeStruct((384, 1152), BF16),
+        ],
         compiler_params=params(),
         cost_estimate=pl.CostEstimate(
             flops=4 * 384 * 384 * SIZE, bytes_accessed=12 * 384 * SIZE, transcendentals=0
@@ -302,41 +324,35 @@
     )(edge, here, act, weights, *after)
 
 
-def back_kernel(edge, behind, here, ahead, cot, weights, *refs):
-    out, taps = refs[-2:]
-    group = pl.program_id(0)
-
-    @pl.when((group == 0) & (pl.program_id(1) == 0))
-    def _():
-        for k in range(3):
-            tap = weights[:, 384 * (2 - k) : 384 * (3 - k)]
-            taps[:, 384 * k : 384 * (k + 1)] = tap.T
-
-    field = jnp.concatenate(
-        [masked(behind, edge[2 + group]), rows(here), masked(ahead, edge[6 + group])], axis=0
-    )
+def back_kernel(edge, first, here, second, cot, taps, *refs):
+    out, token = refs[-2:]
+    token[...] = jnp.zeros((8, 128), F32)
+    before, after = neighbours(first, second, edge)
+    field = jnp.concatenate([before, rows(here), after], axis=0)
     result = (rows(cot).astype(F32) + dot(taps[...], field)).astype(BF16)
     out[...] = result.reshape(out.shape)
 
 
-def back(edge, behind, here, ahead, cot, weights, *after):
+def back(edge, behind, here, ahead, cot, taps, *after):
     plain, before, beyond = tile_specs()
     return pl.pallas_call(
         back_kernel,
         grid_spec=pltpu.PrefetchScalarGridSpec(
             num_scalar_prefetch=1,
             grid=(2, SIZE // TILE),
-            in_specs=[before, plain, beyond, plain, whole(weights)]
+            in_specs=[before, plain, beyond, plain, whole(taps)]
             + [pl.BlockSpec(memory_space=pl.ANY)] * len(after),
-            out_specs=plain,
-            scratch_shapes=[pltpu.VMEM((384, 1152), BF16)],
-        ),
-        out_shape=jax.ShapeDtypeStruct((2, 2, 192, SIZE), BF16),
+            out_specs=[plain, pl.BlockSpec((8, 128), lambda g, i, edge: (0, 0))],
+        ),
+        out_shape=[
+            pltpu.HBM((2, 2, 192, SIZE), BF16),
+            jax.ShapeDtypeStruct((8, 128), F32),
+        ],
         compiler_params=params(),
         cost_estimate=pl.CostEstimate(
             flops=12 * 384 * 384 * SIZE, bytes_accessed=20 * 384 * SIZE, transcendentals=0
         ),
-    )(edge, behind, here, ahead, cot, weights, *after)
+    )(edge, behind, here, ahead, cot, taps, *after)
 
 
 def round_kernel(total, *refs):
@@ -448,7 +464,15 @@
 def edges(chip, core):
     first, final = (chip == 0).astype(jnp.int32), (chip == 31).astype(jnp.int32)
     one, zero = jnp.int32(1), jnp.int32(0)
-    return jnp.stack([zero, 1 - first, 1 - first, one, final, one, one, 1 - final, core])
+    behind, ahead = jnp.stack([zero, 1 - first]), jnp.stack([final, one])
+    return jnp.concatenate(
+        [
+            jnp.where(core == 0, behind, ahead),
+            jnp.stack([1 - first, one]),
+            jnp.where(core == 0, ahead, behind),
+            jnp.stack([one, 1 - final, core]),
+        ]
+    )
 
 
 def per_device(inputs, convolution_weight, conv_bias, mix_weight, cotangent):
@@ -472,17 +496,19 @@
         return piece.reshape(4, 192, SIZE)
 
     mine = sum_in_column(*sums)
-    outs = [exchange(flat(mixed(edge, here[k], acts[k], weights))) for k in range(CHUNKS)]
+    out, taps = mixed(edge, here[0], acts[0], weights)
+    outs = [exchange(flat(out))]
     total = scatter_over_z(mine).astype(BF16)
     input_grads = [
-        back(edge, grad_sides[k][0], grads[k], grad_sides[k][1], cot[k], weights, *outs, total)
+        back(edge, grad_sides[k][0], grads[k], grad_sides[k][1], cot[k], taps, *outs, total)
         for k in range(CHUNKS)
     ]
-    input_parts = [exchange(flat(p)) for p in input_grads]
-    outputs, input_grad = unpack(outs), unpack(input_parts)
+    input_parts = [exchange(flat(p)) for p, _ in input_grads]
+    outputs, _ = unpack(outs)
+    input_grad, unpacked = unpack(input_parts)
     total = total.astype(F32) + send(total, flip(32)).astype(F32)
-    total = add_flips(rounded(total, *input_grads), 2, 4)
-    gathered = gather_over_z((total * factor).astype(BF16))
+    total = add_flips(rounded(total, *[token for _, token in input_grads]), 2, 4)
+    gathered = gather_over_z((total * factor).astype(BF16), unpacked)
     weight_grad, bias_grad, mix_grad = results(gathered)
     return outputs, input_grad, weight_grad, bias_grad, mix_grad
 

time: 178 us -> 176 us (0.989)
  waiting for transfers between devices: 72.4 us -> 84.2 us
  starting transfers between devices: 63.1 us -> 53.9 us
  local copies, waits for them, and re-layouts: 11.2 us -> 8.2 us
    ppermute x24, waiting for transfers between devices: 72.4 us -> 84.2 us  [send(): return lax.ppermute(block, AXES, route(target))]
    ppermute x24, starting transfers between devices: 50.9 us -> 42.4 us  [send(): return lax.ppermute(block, AXES, route(target))]
    unnamed x22, local copies, waits for them, and re-layouts: 9.19 us -> 7.27 us
  transfers between devices with their start and end apart: 27 -> 27, of which waited for: 17 -> 19; matrix products, arithmetic and copies ran while one was open for 3% -> 2% of each run, Pallas kernels for 7% -> 4%
where the time goes in v3:
time: 176 us; the launch traced here: 175 us
  waiting for transfers between devices  84.2 us (48%)
  starting transfers between devices  53.9 us (31%)
  Pallas kernels  25.5 us (14%)
  local copies, waits for them, and re-layouts  8.2 us (5%)
  other arithmetic  2.57 us (1%)
    ppermute x24, waiting for transfers between devices, send(): return lax.ppermute(block, AXES, route(target))  84.2 us
    ppermute x24, starting transfers between devices, send(): return lax.ppermute(block, AXES, route(target))  42.4 us
    all_to_all x3, starting transfers between devices, exchange(): return lax.all_to_all(block, AXES, 0, 0, axis_index_groups=column_groups())  11.5 us
    pallas_call x1, Pallas kernels, middle(): pl.pallas_call(middle_kernel, grid_spec=pltpu.PrefetchScalarGridSpec(num_...  10.5 us
    unnamed x22, local copies, waits for them, and re-layouts  7.27 us
    pallas_call x1, Pallas kernels, back(): pl.pallas_call(back_kernel, grid_spec=pltpu.PrefetchScalarGridSpec(num_sc...  5.83 us
  transfers between devices with their start and end apart: 27, of which 19 were waited for; matrix products, arithmetic and copies ran while one was open for 2% of the time, Pallas kernels for 4%

profile of v3, /device:TPU:1, one launch (start us, length us, event | category | flops | bytes accessed | tf_op | source)
XLA Modules:
  0.0 175.3 jit_solution(7619442199584598108)
XLA Ops:
  0.7 1.4 copy-done
  2.1 0.6 shard_map.92
  2.8 2.2 %collective-permute-start = (bf16[192,1024]{1,0:T(8,128)(2,1)S(1)}, bf16[192,1024]{1,0:T(8,128)(2,1)S(1)}, u32[]{:S(2)}, u32[]{:S(2)}) collective-permute-start(bf16[192,1024]{1,0:T(8,128)(2,1)S(1)} %get-tuple-element.26), channel_id=1, source_target_pairs={{0,128},{1,129},{2,130},{3,131},{4,132},{5,133},{6,134},{7,135},{8... | collective-permute-start | bytes 1179656 | tf_op jit(solution)/shard_map/ppermute | solution.py:29
  5.0 2.6 %collective-permute-start.1 = (bf16[192,1024]{1,0:T(8,128)(2,1)S(1)}, bf16[192,1024]{1,0:T(8,128)(2,1)S(1)}, u32[]{:S(2)}, u32[]{:S(2)}) collective-permute-start(bf16[192,1024]{1,0:T(8,128)(2,1)S(1)} %get-tuple-element.27), channel_id=1, source_target_pairs={{0,1},{1,0},{2,3},{3,2},{4,5},{5,4},{6,7},{7,6},{8,9},{9,8},{10,11... | collective-permute-start | bytes 1179656 | tf_op jit(solution)/shard_map/ppermute | solution.py:29
  7.6 0.1 copy.10.bias
  7.7 4.8 %collective-permute-done.low = bf16[192,1024]{1,0:T(8,128)(2,1)S(1)} collective-permute-done((bf16[192,1024]{1,0:T(8,128)(2,1)S(1)}, bf16[192,1024]{1,0:T(8,128)(2,1)S(1)}, u32[]{:S(2)}, u32[]{:S(2)}) %collective-permute-start) | collective-permute-done | bytes 393248 | tf_op jit(solution)/shard_map/ppermute | solution.py:29
  12.6 12.0 %collective-permute-done.1.half = bf16[192,1024]{1,0:T(8,128)(2,1)S(1)} collective-permute-done((bf16[192,1024]{1,0:T(8,128)(2,1)S(1)}, bf16[192,1024]{1,0:T(8,128)(2,1)S(1)}, u32[]{:S(2)}, u32[]{:S(2)}) %collective-permute-start.1) | collective-permute-done | bytes 393248 | tf_op jit(solution)/shard_map/ppermute | solution.py:29
  24.6 2.0 %collective-permute-done.2.both = bf16[192,1024]{1,0:T(8,128)(2,1)S(1)} collective-permute-done((bf16[192,1024]{1,0:T(8,128)(2,1)S(1)}, bf16[192,1024]{1,0:T(8,128)(2,1)S(1)}, u32[]{:S(2)}, u32[]{:S(2)}) %collective-permute-start.2) | collective-permute-done | bytes 393248 | tf_op jit(solution)/shard_map/ppermute | solution.py:29
  26.6 0.6 shard_map.93.refs_0_.here
  27.3 0.4 copy-done.7
  27.7 0.1 shard_map.94.own
  27.8 0.1 collective-permute-start.5
  27.9 7.8 %collective-permute-start.3 = (bf16[2,2,192,1024]{3,2,1,0:T(8,128)(2,1)S(1)}, bf16[2,2,192,1024]{3,2,1,0:T(8,128)(2,1)}, u32[]{:S(2)}, u32[]{:S(2)}) collective-permute-start(bf16[2,2,192,1024]{3,2,1,0:T(8,128)(2,1)S(1)} %shard_map.93.refs_0_.here), channel_id=1, source_target_pairs={{0,4},{1,5},{2,126},{3,127},{4,8},{5,9},{6,2},{7,3},{8,12},{9,13},... | collective-permute-start | bytes 4718600 | tf_op jit(solution)/shard_map/ppermute | solution.py:29
  35.8 0.5 collective-permute-done.5.straight
  36.3 3.1 %collective-permute-start.6 = (bf16[96,1664]{1,0:T(8,128)(2,1)S(1)}, bf16[96,1664]{1,0:T(8,128)(2,1)S(1)}, u32[]{:S(2)}, u32[]{:S(2)}) collective-permute-start(bf16[96,1664]{1,0:T(8,128)(2,1)S(1)} %collective-permute-done.5.straight), channel_id=1, source_target_pairs={{0,2},{1,3},{2,0},{3,1},{4,6},{5,7},{6,4},{7,5},{8,10},{9,11},{10,... | collective-permute-start | bytes 958472 | tf_op jit(solution)/shard_map/ppermute | solution.py:29
  39.4 1.2 collective-permute-done.6.crossed
  40.6 0.6 shard_map.95.refs_0_.weights
  41.3 0.4 shard_map.96
  41.7 1.1 copy-done.1
  42.8 4.3 %all-to-all-start = ((bf16[4,192,1024]{2,1,0:T(8,128)(2,1)}), bf16[4,192,1024]{2,1,0:T(8,128)(2,1)}, u32[]{:S(2)}, u32[]{:S(2)}) async-start(bf16[4,192,1024]{2,1,0:T(8,128)(2,1)} %copy-done.1), calls=%async_computation | async-start | bytes 3145728 | tf_op jit(solution)/shard_map/all_to_all | solution.py:53
  47.3 19.9 %collective-permute-done.3.first = bf16[2,2,192,1024]{3,2,1,0:T(8,128)(2,1)} collective-permute-done((bf16[2,2,192,1024]{3,2,1,0:T(8,128)(2,1)S(1)}, bf16[2,2,192,1024]{3,2,1,0:T(8,128)(2,1)}, u32[]{:S(2)}, u32[]{:S(2)}) %collective-permute-start.3) | collective-permute-done | bytes 1572896 | tf_op jit(solution)/shard_map/ppermute | solution.py:29
  67.2 5.7 %collective-permute-done.4.second = bf16[2,2,192,1024]{3,2,1,0:T(8,128)(2,1)} collective-permute-done((bf16[2,2,192,1024]{3,2,1,0:T(8,128)(2,1)S(1)}, bf16[2,2,192,1024]{3,2,1,0:T(8,128)(2,1)}, u32[]{:S(2)}, u32[]{:S(2)}) %collective-permute-start.4) | collective-permute-done | bytes 1572896 | tf_op jit(solution)/shard_map/ppermute | solution.py:29
  72.9 10.5 %shard_map.97 = (bf16[2,2,192,1024]{3,2,1,0:T(8,128)(2,1)S(1)}, bf16[2,2,192,1024]{3,2,1,0:T(8,128)(2,1)}, f32[2,96,1664]{2,1,0:T(8,128)S(1)}, f32[2,96,1664]{2,1,0:T(8,128)S(1)}) custom-call(s32[9]{0:T(128)S(1)} %concatenate.3.edge, bf16[2,2,192,1024]{3,2,1,0:T(8,128)(2,1)} %collective-permute-done.3.first, ...), custom_call_target="tpu_custom_call" | custom-call | flops 5435817984 | bytes 9437184 | tf_op jit(solution)/shard_map/pallas_call | solution.py:275
  83.4 1.1 copy-done.3
  84.6 3.0 %collective-permute-done.9.received = f32[2,96,1664]{2,1,0:T(8,128)S(1)} collective-permute-done((f32[2,96,1664]{2,1,0:T(8,128)S(1)}, f32[2,96,1664]{2,1,0:T(8,128)S(1)}, u32[]{:S(2)}, u32[]{:S(2)}) %collective-permute-start.9) | collective-permute-done | bytes 1277984 | tf_op jit(solution)/shard_map/ppermute | solution.py:29
  87.5 0.1 shard_map.100
  87.7 0.9 collective-permute-start.10
  88.5 2.5 %collective-permute-start.11 = (bf16[96,1664]{1,0:T(8,128)(2,1)S(1)}, bf16[96,1664]{1,0:T(8,128)(2,1)}, u32[]{:S(2)}, u32[]{:S(2)}) collective-permute-start(bf16[96,1664]{1,0:T(8,128)(2,1)S(1)} %get-tuple-element.37), channel_id=1, source_target_pairs={{0,1},{1,0},{2,3},{3,2},{4,5},{5,4},{6,7},{7,6},{8,9},{9,8},{10,11... | collective-permute-start | bytes 958472 | tf_op jit(solution)/shard_map/ppermute | solution.py:29
  91.0 0.6 collective-permute-start.12
  91.6 3.4 %collective-permute-start.7 = (bf16[2,2,192,1024]{3,2,1,0:T(8,128)(2,1)}, bf16[2,2,192,1024]{3,2,1,0:T(8,128)(2,1)}, u32[]{:S(2)}, u32[]{:S(2)}) collective-permute-start(bf16[2,2,192,1024]{3,2,1,0:T(8,128)(2,1)} %get-tuple-element.32.here), channel_id=1, source_target_pairs={{0,4},{1,5},{2,126},{3,127},{4,8},{5,9},{6,2},{7,3},{8,12},{9,13},... | collective-permute-start | bytes 4718600 | tf_op jit(solution)/shard_map/ppermute | solution.py:29
  95.0 1.4 copy-done.4
  96.4 3.1 %shard_map.98 = (bf16[2,2,192,1024]{3,2,1,0:T(8,128)(2,1)}, bf16[384,1152]{1,0:T(8,128)(2,1)S(1)}) custom-call(s32[9]{0:T(128)S(1)} %concatenate.3.edge, bf16[2,2,192,1024]{3,2,1,0:T(8,128)(2,1)S(1)} %shard_map.93.refs_0_.here, bf16[2,2,192,1024]{3,2,1,0:T(8,128)(2,1)S(1)} %copy-done.4, bf16[384,1664]{1,0:T(8,128)(2,1)S(1)} %shard_map.95.refs_0_.weights), custom_call_target="tpu_custom_call" | custom-call | flops 603979776 | bytes 4718592 | tf_op jit(solution)/shard_map/pallas_call | solution.py:307
  99.6 0.9 copy-done.5
  100.5 3.6 %all-to-all-start.1 = ((bf16[4,192,1024]{2,1,0:T(8,128)(2,1)}), bf16[4,192,1024]{2,1,0:T(8,128)(2,1)S(1)}, u32[]{:S(2)}, u32[]{:S(2)}) async-start(bf16[4,192,1024]{2,1,0:T(8,128)(2,1)} %bitcast.32), calls=%async_computation.1 | async-start | bytes 3145728 | tf_op jit(solution)/shard_map/all_to_all | solution.py:53
  104.1 1.6 collective-permute-done.11
  105.7 2.2 %collective-permute-done.12 = bf16[96,1664]{1,0:T(8,128)(2,1)} collective-permute-done((bf16[96,1664]{1,0:T(8,128)(2,1)S(1)}, bf16[96,1664]{1,0:T(8,128)(2,1)}, u32[]{:S(2)}, u32[]{:S(2)}) %collective-permute-start.12) | collective-permute-done | bytes 319520 | tf_op jit(solution)/shard_map/ppermute | solution.py:29
  107.8 1.3 add_add_fusion
  109.2 0.9 copy-done.9
  110.1 0.1 collective-permute-start.13
  110.2 0.1 collective-permute-start.14
  110.3 3.4 %collective-permute-start.15 = (bf16[24,1664]{1,0:T(8,128)(2,1)S(1)}, bf16[24,1664]{1,0:T(8,128)(2,1)S(1)}, u32[]{:S(2)}, u32[]{:S(2)}) collective-permute-start(bf16[24,1664]{1,0:T(8,128)(2,1)S(1)} %get-tuple-element.46), channel_id=1, source_target_pairs={{0,48},{1,49},{2,50},{3,51},{4,52},{5,53},{6,54},{7,55},{8,56},{9,... | collective-permute-start | bytes 239624 | tf_op jit(solution)/shard_map/ppermute | solution.py:29
  113.7 10.7 %collective-permute-done.13 = bf16[24,1664]{1,0:T(8,128)(2,1)S(1)} collective-permute-done((bf16[24,1664]{1,0:T(8,128)(2,1)S(1)}, bf16[24,1664]{1,0:T(8,128)(2,1)S(1)}, u32[]{:S(2)}, u32[]{:S(2)}) %collective-permute-start.13) | collective-permute-done | bytes 79904 | tf_op jit(solution)/shard_map/ppermute | solution.py:29
  124.4 1.1 collective-permute-done.14
  125.5 4.7 %collective-permute-done.15 = bf16[24,1664]{1,0:T(8,128)(2,1)S(1)} collective-permute-done((bf16[24,1664]{1,0:T(8,128)(2,1)S(1)}, bf16[24,1664]{1,0:T(8,128)(2,1)S(1)}, u32[]{:S(2)}, u32[]{:S(2)}) %collective-permute-start.15) | collective-permute-done | bytes 79904 | tf_op jit(solution)/shard_map/ppermute | solution.py:29
  130.2 1.0 fusion.2.refs_1_
  131.2 1.6 collective-permute-done.8.second
  132.8 5.8 %shard_map.101 = (bf16[2,2,192,1024]{3,2,1,0:T(8,128)(2,1)}, f32[8,128]{1,0:T(8,128)S(1)}) custom-call(s32[9]{0:T(128)S(1)} %concatenate.3.edge, bf16[2,2,192,1024]{3,2,1,0:T(8,128)(2,1)} %collective-permute-done.7.first, bf16[2,2,192,1024]{3,2,1,0:T(8,128)(2,1)} %get-tuple-element.32.here, bf16[2,2,192,1024]{3,2,1,0:T(8,128)(2,1)} %collective-permute-done.8.second, ...), custom_call_target="tpu_custom_call" | custom-call | flops 1811939328 | bytes 7864320 | tf_op jit(solution)/shard_map/pallas_call | solution.py:338
  138.7 3.6 %all-to-all-start.2 = ((bf16[4,192,1024]{2,1,0:T(8,128)(2,1)}), bf16[4,192,1024]{2,1,0:T(8,128)(2,1)S(1)}, u32[]{:S(2)}, u32[]{:S(2)}) async-start(bf16[4,192,1024]{2,1,0:T(8,128)(2,1)} %bitcast.33), calls=%async_computation.2 | async-start | bytes 3145728 | tf_op jit(solution)/shard_map/all_to_all | solution.py:53
  142.2 4.2 %collective-permute-start.16 = (bf16[24,1664]{1,0:T(8,128)(2,1)S(1)}, bf16[24,1664]{1,0:T(8,128)(2,1)S(1)}, u32[]{:S(2)}, u32[]{:S(2)}) collective-permute-start(bf16[24,1664]{1,0:T(8,128)(2,1)S(1)} %fusion.2.refs_1_), channel_id=1, source_target_pairs={{0,64},{1,65},{2,66},{3,67},{4,68},{5,69},{6,70},{7,71},{8,72},{9,... | collective-permute-start | bytes 239624 | tf_op jit(solution)/shard_map/ppermute | solution.py:29
  146.4 3.0 %collective-permute-done.16 = bf16[24,1664]{1,0:T(8,128)(2,1)S(1)} collective-permute-done((bf16[24,1664]{1,0:T(8,128)(2,1)S(1)}, bf16[24,1664]{1,0:T(8,128)(2,1)S(1)}, u32[]{:S(2)}, u32[]{:S(2)}) %collective-permute-start.16) | collective-permute-done | bytes 79904 | tf_op jit(solution)/shard_map/ppermute | solution.py:29
  149.5 0.1 collective-permute-start.17
  149.6 4.0 %collective-permute-start.18 = (bf16[24,1664]{1,0:T(8,128)(2,1)S(1)}, bf16[24,1664]{1,0:T(8,128)(2,1)S(1)}, u32[]{:S(2)}, u32[]{:S(2)}) collective-permute-start(bf16[24,1664]{1,0:T(8,128)(2,1)S(1)} %shard_map.103), channel_id=1, source_target_pairs={{0,8},{1,9},{2,10},{3,11},{4,12},{5,13},{6,14},{7,15},{8,0},{9,1},... | collective-permute-start | bytes 239624 | tf_op jit(solution)/shard_map/ppermute | solution.py:29
  153.7 3.4 %collective-permute-done.18 = bf16[24,1664]{1,0:T(8,128)(2,1)S(1)} collective-permute-done((bf16[24,1664]{1,0:T(8,128)(2,1)S(1)}, bf16[24,1664]{1,0:T(8,128)(2,1)S(1)}, u32[]{:S(2)}, u32[]{:S(2)}) %collective-permute-start.18) | collective-permute-done | bytes 79904 | tf_op jit(solution)/shard_map/ppermute | solution.py:29
  157.0 2.3 %collective-permute-done.19 = bf16[24,1664]{1,0:T(8,128)(2,1)S(1)} collective-permute-done((bf16[24,1664]{1,0:T(8,128)(2,1)S(1)}, bf16[24,1664]{1,0:T(8,128)(2,1)S(1)}, u32[]{:S(2)}, u32[]{:S(2)}) %collective-permute-start.19) | collective-permute-done | bytes 79904 | tf_op jit(solution)/shard_map/ppermute | solution.py:29
  159.4 1.2 collective-permute-start.20
  160.6 2.5 %collective-permute-start.21 = (bf16[24,1664]{1,0:T(8,128)(2,1)S(1)}, bf16[24,1664]{1,0:T(8,128)(2,1)S(1)}, u32[]{:S(2)}, u32[]{:S(2)}) collective-permute-start(bf16[24,1664]{1,0:T(8,128)(2,1)S(1)} %multiply_convert_fusion.refs_0_), channel_id=1, source_target_pairs={{0,32},{1,33},{2,34},{3,35},{4,36},{5,37},{6,38},{7,39},{8,40},{9,... | collective-permute-start | bytes 239624 | tf_op jit(solution)/shard_map/ppermute | solution.py:29
  163.1 0.4 collective-permute-start.22
  163.5 1.2 shard_map.102
  164.7 0.2 collective-permute-done.21.refs_2_
  164.9 4.2 %collective-permute-done.22.refs_3_ = bf16[24,1664]{1,0:T(8,128)(2,1)S(1)} collective-permute-done((bf16[24,1664]{1,0:T(8,128)(2,1)S(1)}, bf16[24,1664]{1,0:T(8,128)(2,1)S(1)}, u32[]{:S(2)}, u32[]{:S(2)}) %collective-permute-start.22) | collective-permute-done | bytes 79904 | tf_op jit(solution)/shard_map/ppermute | solution.py:29
  169.1 3.2 %collective-permute-start.23 = (bf16[4,24,1664]{2,1,0:T(8,128)(2,1)S(1)}, bf16[4,24,1664]{2,1,0:T(8,128)(2,1)S(1)}, u32[]{:S(2)}, u32[]{:S(2)}) collective-permute-start(bf16[4,24,1664]{2,1,0:T(8,128)(2,1)S(1)} %shard_map.104.own), channel_id=1, source_target_pairs={{0,2},{1,3},{2,0},{3,1},{4,6},{5,7},{6,4},{7,5},{8,10},{9,11},{10,... | collective-permute-start | bytes 958472 | tf_op jit(solution)/shard_map/ppermute | solution.py:29
  172.3 1.2 shard_map.99
  173.6 1.1 shard_map.105
  174.7 0.7 slice_reduce_fusion
  (38 shorter events, 0.6 us)
Async XLA Ops:
  0.7 1.4 copy-start
  2.1 5.5 %copy-start.10 = (f32[192]{0:T(256)S(1)}, f32[192]{0:T(256)}, u32[]{:S(2)}) copy-start(f32[192]{0:T(256)} %param.7) | copy-start | bytes 2308
  2.8 9.8 %collective-permute-start = (bf16[192,1024]{1,0:T(8,128)(2,1)S(1)}, bf16[192,1024]{1,0:T(8,128)(2,1)S(1)}, u32[]{:S(2)}, u32[]{:S(2)}) collective-permute-start(bf16[192,1024]{1,0:T(8,128)(2,1)S(1)} %get-tuple-element.26), channel_id=1, source_target_pairs={{0,128},{1,129},{2,130},{3,131},{4,132},{5,133},{6,134},{7,135},{8... | collective-permute-start | bytes 1179656 | tf_op jit(solution)/shard_map/ppermute | solution.py:29
  5.0 19.6 %collective-permute-start.1 = (bf16[192,1024]{1,0:T(8,128)(2,1)S(1)}, bf16[192,1024]{1,0:T(8,128)(2,1)S(1)}, u32[]{:S(2)}, u32[]{:S(2)}) collective-permute-start(bf16[192,1024]{1,0:T(8,128)(2,1)S(1)} %get-tuple-element.27), channel_id=1, source_target_pairs={{0,1},{1,0},{2,3},{3,2},{4,5},{5,4},{6,7},{7,6},{8,9},{9,8},{10,11... | collective-permute-start | bytes 1179656 | tf_op jit(solution)/shard_map/ppermute | solution.py:29
  7.6 19.0 %collective-permute-start.2 = (bf16[192,1024]{1,0:T(8,128)(2,1)S(1)}, bf16[192,1024]{1,0:T(8,128)(2,1)S(1)}, u32[]{:S(2)}, u32[]{:S(2)}) collective-permute-start(bf16[192,1024]{1,0:T(8,128)(2,1)S(1)} %get-tuple-element.28), channel_id=1, source_target_pairs={{0,129},{1,128},{2,131},{3,130},{4,133},{5,132},{6,135},{7,134},{8... | collective-permute-start | bytes 1179656 | tf_op jit(solution)/shard_map/ppermute | solution.py:29
  26.6 1.0 copy-start.7
  26.6 1.0 copy-start.8
  27.8 13.5 %copy-start.2 = (bf16[2,192,2048]{2,1,0:T(8,128)(2,1)S(1)}, bf16[2,192,2048]{2,1,0:T(8,128)(2,1)}, u32[]{:S(2)}) copy-start(bf16[2,192,2048]{2,1,0:T(8,128)(2,1)} %source.1) | copy-start | bytes 4718596
  27.8 8.5 %collective-permute-start.5 = (bf16[96,1664]{1,0:T(8,128)(2,1)S(1)}, bf16[96,1664]{1,0:T(8,128)(2,1)S(1)}, u32[]{:S(2)}, u32[]{:S(2)}) collective-permute-start(bf16[96,1664]{1,0:T(8,128)(2,1)S(1)} %dynamic-slice_bitcast_fusion), channel_id=1, source_target_pairs={{0,1},{1,0},{2,3},{3,2},{4,5},{5,4},{6,7},{7,6},{8,9},{9,8},{10,11... | collective-permute-start | bytes 958472 | tf_op jit(solution)/shard_map/ppermute | solution.py:29
  27.9 39.3 %collective-permute-start.3 = (bf16[2,2,192,1024]{3,2,1,0:T(8,128)(2,1)S(1)}, bf16[2,2,192,1024]{3,2,1,0:T(8,128)(2,1)}, u32[]{:S(2)}, u32[]{:S(2)}) collective-permute-start(bf16[2,2,192,1024]{3,2,1,0:T(8,128)(2,1)S(1)} %shard_map.93.refs_0_.here), channel_id=1, source_target_pairs={{0,4},{1,5},{2,126},{3,127},{4,8},{5,9},{6,2},{7,3},{8,12},{9,13},... | collective-permute-start | bytes 4718600 | tf_op jit(solution)/shard_map/ppermute | solution.py:29
  35.8 37.1 %collective-permute-start.4 = (bf16[2,2,192,1024]{3,2,1,0:T(8,128)(2,1)S(1)}, bf16[2,2,192,1024]{3,2,1,0:T(8,128)(2,1)}, u32[]{:S(2)}, u32[]{:S(2)}) collective-permute-start(bf16[2,2,192,1024]{3,2,1,0:T(8,128)(2,1)S(1)} %shard_map.93.refs_0_.here), channel_id=1, source_target_pairs={{0,124},{1,125},{2,6},{3,7},{4,0},{5,1},{6,10},{7,11},{8,4},{9,5},... | collective-permute-start | bytes 4718600 | tf_op jit(solution)/shard_map/ppermute | solution.py:29
  36.3 4.3 %collective-permute-start.6 = (bf16[96,1664]{1,0:T(8,128)(2,1)S(1)}, bf16[96,1664]{1,0:T(8,128)(2,1)S(1)}, u32[]{:S(2)}, u32[]{:S(2)}) collective-permute-start(bf16[96,1664]{1,0:T(8,128)(2,1)S(1)} %collective-permute-done.5.straight), channel_id=1, source_target_pairs={{0,2},{1,3},{2,0},{3,1},{4,6},{5,7},{6,4},{7,5},{8,10},{9,11},{10,... | collective-permute-start | bytes 958472 | tf_op jit(solution)/shard_map/ppermute | solution.py:29
  41.7 1.1 copy-start.1
  42.8 30.1 %all-to-all-start = ((bf16[4,192,1024]{2,1,0:T(8,128)(2,1)}), bf16[4,192,1024]{2,1,0:T(8,128)(2,1)}, u32[]{:S(2)}, u32[]{:S(2)}) async-start(bf16[4,192,1024]{2,1,0:T(8,128)(2,1)} %copy-done.1), calls=%async_computation | async-start | bytes 3145728 | tf_op jit(solution)/shard_map/all_to_all | solution.py:53
  83.4 1.1 copy-start.3
  84.6 3.0 %collective-permute-start.9 = (f32[2,96,1664]{2,1,0:T(8,128)S(1)}, f32[2,96,1664]{2,1,0:T(8,128)S(1)}, u32[]{:S(2)}, u32[]{:S(2)}) collective-permute-start(f32[2,96,1664]{2,1,0:T(8,128)S(1)} %get-tuple-element.35), channel_id=1, source_target_pairs={{0,2},{1,3},{2,0},{3,1},{4,6},{5,7},{6,4},{7,5},{8,10},{9,11},{10,... | collective-permute-start | bytes 3833864 | tf_op jit(solution)/shard_map/ppermute | solution.py:29
  87.7 16.4 %collective-permute-start.10 = (bf16[96,1664]{1,0:T(8,128)(2,1)S(1)}, bf16[96,1664]{1,0:T(8,128)(2,1)}, u32[]{:S(2)}, u32[]{:S(2)}) collective-permute-start(bf16[96,1664]{1,0:T(8,128)(2,1)S(1)} %get-tuple-element.36), channel_id=1, source_target_pairs={{0,128},{1,129},{2,130},{3,131},{4,132},{5,133},{6,134},{7,135},{8... | collective-permute-start | bytes 958472 | tf_op jit(solution)/shard_map/ppermute | solution.py:29
  88.5 17.2 %collective-permute-start.11 = (bf16[96,1664]{1,0:T(8,128)(2,1)S(1)}, bf16[96,1664]{1,0:T(8,128)(2,1)}, u32[]{:S(2)}, u32[]{:S(2)}) collective-permute-start(bf16[96,1664]{1,0:T(8,128)(2,1)S(1)} %get-tuple-element.37), channel_id=1, source_target_pairs={{0,1},{1,0},{2,3},{3,2},{4,5},{5,4},{6,7},{7,6},{8,9},{9,8},{10,11... | collective-permute-start | bytes 958472 | tf_op jit(solution)/shard_map/ppermute | solution.py:29
  91.0 16.8 %collective-permute-start.12 = (bf16[96,1664]{1,0:T(8,128)(2,1)S(1)}, bf16[96,1664]{1,0:T(8,128)(2,1)}, u32[]{:S(2)}, u32[]{:S(2)}) collective-permute-start(bf16[96,1664]{1,0:T(8,128)(2,1)S(1)} %get-tuple-element.37), channel_id=1, source_target_pairs={{0,129},{1,128},{2,131},{3,130},{4,133},{5,132},{6,135},{7,134},{8... | collective-permute-start | bytes 958472 | tf_op jit(solution)/shard_map/ppermute | solution.py:29
  91.6 39.6 %collective-permute-start.7 = (bf16[2,2,192,1024]{3,2,1,0:T(8,128)(2,1)}, bf16[2,2,192,1024]{3,2,1,0:T(8,128)(2,1)}, u32[]{:S(2)}, u32[]{:S(2)}) collective-permute-start(bf16[2,2,192,1024]{3,2,1,0:T(8,128)(2,1)} %get-tuple-element.32.here), channel_id=1, source_target_pairs={{0,4},{1,5},{2,126},{3,127},{4,8},{5,9},{6,2},{7,3},{8,12},{9,13},... | collective-permute-start | bytes 4718600 | tf_op jit(solution)/shard_map/ppermute | solution.py:29
  95.0 37.8 %collective-permute-start.8 = (bf16[2,2,192,1024]{3,2,1,0:T(8,128)(2,1)}, bf16[2,2,192,1024]{3,2,1,0:T(8,128)(2,1)}, u32[]{:S(2)}, u32[]{:S(2)}) collective-permute-start(bf16[2,2,192,1024]{3,2,1,0:T(8,128)(2,1)} %get-tuple-element.32.here), channel_id=1, source_target_pairs={{0,124},{1,125},{2,6},{3,7},{4,0},{5,1},{6,10},{7,11},{8,4},{9,5},... | collective-permute-start | bytes 4718600 | tf_op jit(solution)/shard_map/ppermute | solution.py:29
  95.0 1.4 copy-start.4
  99.6 0.9 copy-start.5
  100.5 30.7 %all-to-all-start.1 = ((bf16[4,192,1024]{2,1,0:T(8,128)(2,1)}), bf16[4,192,1024]{2,1,0:T(8,128)(2,1)S(1)}, u32[]{:S(2)}, u32[]{:S(2)}) async-start(bf16[4,192,1024]{2,1,0:T(8,128)(2,1)} %bitcast.32), calls=%async_computation.1 | async-start | bytes 3145728 | tf_op jit(solution)/shard_map/all_to_all | solution.py:53
  104.0 28.8 %copy-start.6 = (bf16[384,1152]{1,0:T(8,128)(2,1)S(1)}, bf16[384,1152]{1,0:T(8,128)(2,1)}, u32[]{:S(2)}) copy-start(bf16[384,1152]{1,0:T(8,128)(2,1)} %copy-done.5) | copy-start | bytes 2654212
  109.2 0.9 copy-start.9
  110.1 14.4 %collective-permute-start.13 = (bf16[24,1664]{1,0:T(8,128)(2,1)S(1)}, bf16[24,1664]{1,0:T(8,128)(2,1)S(1)}, u32[]{:S(2)}, u32[]{:S(2)}) collective-permute-start(bf16[24,1664]{1,0:T(8,128)(2,1)S(1)} %get-tuple-element.45), channel_id=1, source_target_pairs={{0,16},{1,17},{2,18},{3,19},{4,20},{5,21},{6,22},{7,23},{8,24},{9,... | collective-permute-start | bytes 239624 | tf_op jit(solution)/shard_map/ppermute | solution.py:29
  110.2 15.3 %collective-permute-start.14 = (bf16[24,1664]{1,0:T(8,128)(2,1)S(1)}, bf16[24,1664]{1,0:T(8,128)(2,1)S(1)}, u32[]{:S(2)}, u32[]{:S(2)}) collective-permute-start(bf16[24,1664]{1,0:T(8,128)(2,1)S(1)} %get-tuple-element.47), channel_id=1, source_target_pairs={{0,32},{1,33},{2,34},{3,35},{4,36},{5,37},{6,38},{7,39},{8,40},{9,... | collective-permute-start | bytes 239624 | tf_op jit(solution)/shard_map/ppermute | solution.py:29
  110.3 20.0 %collective-permute-start.15 = (bf16[24,1664]{1,0:T(8,128)(2,1)S(1)}, bf16[24,1664]{1,0:T(8,128)(2,1)S(1)}, u32[]{:S(2)}, u32[]{:S(2)}) collective-permute-start(bf16[24,1664]{1,0:T(8,128)(2,1)S(1)} %get-tuple-element.46), channel_id=1, source_target_pairs={{0,48},{1,49},{2,50},{3,51},{4,52},{5,53},{6,54},{7,55},{8,56},{9,... | collective-permute-start | bytes 239624 | tf_op jit(solution)/shard_map/ppermute | solution.py:29
  138.7 24.8 %all-to-all-start.2 = ((bf16[4,192,1024]{2,1,0:T(8,128)(2,1)}), bf16[4,192,1024]{2,1,0:T(8,128)(2,1)S(1)}, u32[]{:S(2)}, u32[]{:S(2)}) async-start(bf16[4,192,1024]{2,1,0:T(8,128)(2,1)} %bitcast.33), calls=%async_computation.2 | async-start | bytes 3145728 | tf_op jit(solution)/shard_map/all_to_all | solution.py:53
  142.2 7.3 %collective-permute-start.16 = (bf16[24,1664]{1,0:T(8,128)(2,1)S(1)}, bf16[24,1664]{1,0:T(8,128)(2,1)S(1)}, u32[]{:S(2)}, u32[]{:S(2)}) collective-permute-start(bf16[24,1664]{1,0:T(8,128)(2,1)S(1)} %fusion.2.refs_1_), channel_id=1, source_target_pairs={{0,64},{1,65},{2,66},{3,67},{4,68},{5,69},{6,70},{7,71},{8,72},{9,... | collective-permute-start | bytes 239624 | tf_op jit(solution)/shard_map/ppermute | solution.py:29
  149.5 4.1 %collective-permute-start.17 = (bf16[24,1664]{1,0:T(8,128)(2,1)S(1)}, bf16[24,1664]{1,0:T(8,128)(2,1)S(1)}, u32[]{:S(2)}, u32[]{:S(2)}) collective-permute-start(bf16[24,1664]{1,0:T(8,128)(2,1)S(1)} %shard_map.103), channel_id=1, source_target_pairs={{0,4},{1,5},{2,6},{3,7},{4,0},{5,1},{6,2},{7,3},{8,12},{9,13},{10,... | collective-permute-start | bytes 239624 | tf_op jit(solution)/shard_map/ppermute | solution.py:29
  149.6 7.4 %collective-permute-start.18 = (bf16[24,1664]{1,0:T(8,128)(2,1)S(1)}, bf16[24,1664]{1,0:T(8,128)(2,1)S(1)}, u32[]{:S(2)}, u32[]{:S(2)}) collective-permute-start(bf16[24,1664]{1,0:T(8,128)(2,1)S(1)} %shard_map.103), channel_id=1, source_target_pairs={{0,8},{1,9},{2,10},{3,11},{4,12},{5,13},{6,14},{7,15},{8,0},{9,1},... | collective-permute-start | bytes 239624 | tf_op jit(solution)/shard_map/ppermute | solution.py:29
  153.7 5.7 %collective-permute-start.19 = (bf16[24,1664]{1,0:T(8,128)(2,1)S(1)}, bf16[24,1664]{1,0:T(8,128)(2,1)S(1)}, u32[]{:S(2)}, u32[]{:S(2)}) collective-permute-start(bf16[24,1664]{1,0:T(8,128)(2,1)S(1)} %shard_map.103), channel_id=1, source_target_pairs={{0,12},{1,13},{2,14},{3,15},{4,8},{5,9},{6,10},{7,11},{8,4},{9,5},... | collective-permute-start | bytes 239624 | tf_op jit(solution)/shard_map/ppermute | solution.py:29
  159.4 5.3 %collective-permute-start.20 = (bf16[24,1664]{1,0:T(8,128)(2,1)S(1)}, bf16[24,1664]{1,0:T(8,128)(2,1)S(1)}, u32[]{:S(2)}, u32[]{:S(2)}) collective-permute-start(bf16[24,1664]{1,0:T(8,128)(2,1)S(1)} %multiply_convert_fusion.refs_0_), channel_id=1, source_target_pairs={{0,16},{1,17},{2,18},{3,19},{4,20},{5,21},{6,22},{7,23},{8,24},{9,... | collective-permute-start | bytes 239624 | tf_op jit(solution)/shard_map/ppermute | solution.py:29
  160.6 4.3 %collective-permute-start.21 = (bf16[24,1664]{1,0:T(8,128)(2,1)S(1)}, bf16[24,1664]{1,0:T(8,128)(2,1)S(1)}, u32[]{:S(2)}, u32[]{:S(2)}) collective-permute-start(bf16[24,1664]{1,0:T(8,128)(2,1)S(1)} %multiply_convert_fusion.refs_0_), channel_id=1, source_target_pairs={{0,32},{1,33},{2,34},{3,35},{4,36},{5,37},{6,38},{7,39},{8,40},{9,... | collective-permute-start | bytes 239624 | tf_op jit(solution)/shard_map/ppermute | solution.py:29
  163.1 6.0 %collective-permute-start.22 = (bf16[24,1664]{1,0:T(8,128)(2,1)S(1)}, bf16[24,1664]{1,0:T(8,128)(2,1)S(1)}, u32[]{:S(2)}, u32[]{:S(2)}) collective-permute-start(bf16[24,1664]{1,0:T(8,128)(2,1)S(1)} %multiply_convert_fusion.refs_0_), channel_id=1, source_target_pairs={{0,48},{1,49},{2,50},{3,51},{4,52},{5,53},{6,54},{7,55},{8,56},{9,... | collective-permute-start | bytes 239624 | tf_op jit(solution)/shard_map/ppermute | solution.py:29
  169.1 4.4 %collective-permute-start.23 = (bf16[4,24,1664]{2,1,0:T(8,128)(2,1)S(1)}, bf16[4,24,1664]{2,1,0:T(8,128)(2,1)S(1)}, u32[]{:S(2)}, u32[]{:S(2)}) collective-permute-start(bf16[4,24,1664]{2,1,0:T(8,128)(2,1)S(1)} %shard_map.104.own), channel_id=1, source_target_pairs={{0,2},{1,3},{2,0},{3,1},{4,6},{5,7},{6,4},{7,5},{8,10},{9,11},{10,... | collective-permute-start | bytes 958472 | tf_op jit(solution)/shard_map/ppermute | solution.py:29

commit v4 on v3

--- a/solution.py
+++ b/solution.py
@@ -389,8 +389,7 @@
     )(half.reshape(1), own, received)
 
 
-def sum_in_column(own, given):
-    own, theirs = add_cores(lax.axis_index("ch"), own, send(given, other_core))
+def sum_in_column(own, theirs):
     beside = send(own, other_low).astype(F32)
     across = send(theirs, other_ch).astype(F32)
     third = send(theirs, other_both).astype(F32)
@@ -495,12 +494,13 @@
     def flat(piece):
         return piece.reshape(4, 192, SIZE)
 
-    mine = sum_in_column(*sums)
-    out, taps = mixed(edge, here[0], acts[0], weights)
+    own, theirs = add_cores(lax.axis_index("ch"), sums[0], send(sums[1], other_core))
+    mine = sum_in_column(own, theirs)
+    out, taps = mixed(edge, here[0], acts[0], weights, mine)
     outs = [exchange(flat(out))]
     total = scatter_over_z(mine).astype(BF16)
     input_grads = [
-        back(edge, grad_sides[k][0], grads[k], grad_sides[k][1], cot[k], taps, *outs, total)
+        back(edge, grad_sides[k][0], grads[k], grad_sides[k][1], cot[k], taps, *outs)
         for k in range(CHUNKS)
     ]
     input_parts = [exchange(flat(p)) for p, _ in input_grads]

time: 176 us -> 174 us (0.989)
  starting transfers between devices: 53.9 us -> 57 us
  local copies, waits for them, and re-layouts: 8.2 us -> 5.47 us
    unnamed x22 -> x18, local copies, waits for them, and re-layouts: 7.27 us -> 3.86 us
    ppermute x24, starting transfers between devices: 42.4 us -> 45.4 us  [send(): return lax.ppermute(block, AXES, route(target))]
  transfers between devices with their start and end apart: 27 -> 27, of which waited for: 19 -> 19; matrix products, arithmetic and copies ran while one was open for 2% -> 1% of each run, Pallas kernels for 4% -> 7%
where the time goes in v4:
time: 174 us
  waiting for transfers between devices  83.6 us (48%)
  starting transfers between devices  57 us (33%)
  Pallas kernels  25.6 us (15%)
  local copies, waits for them, and re-layouts  5.47 us (3%)
    ppermute x24, waiting for transfers between devices, send(): return lax.ppermute(block, AXES, route(target))  82.8 us
    ppermute x24, starting transfers between devices, send(): return lax.ppermute(block, AXES, route(target))  45.4 us
    all_to_all x3, starting transfers between devices, exchange(): return lax.all_to_all(block, AXES, 0, 0, axis_index_groups=column_groups())  11.6 us
    pallas_call x1, Pallas kernels, middle(): pl.pallas_call(middle_kernel, grid_spec=pltpu.PrefetchScalarGridSpec(num_...  10.5 us
    pallas_call x1, Pallas kernels, back(): pl.pallas_call(back_kernel, grid_spec=pltpu.PrefetchScalarGridSpec(num_sc...  5.83 us
    unnamed x18, local copies, waits for them, and re-layouts  3.86 us
  transfers between devices with their start and end apart: 27, of which 19 were waited for; matrix products, arithmetic and copies ran while one was open for 1% of the time, Pallas kernels for 7%

profile of v4, /device:TPU:1, one launch (start us, length us, event | category | flops | bytes accessed | tf_op | source)
XLA Modules:
  0.0 173.9 jit_solution(6760018020851408280)
XLA Ops:
  0.7 1.4 copy-done
  2.1 0.6 shard_map.92
  2.8 2.2 %collective-permute-start = (bf16[192,1024]{1,0:T(8,128)(2,1)S(1)}, bf16[192,1024]{1,0:T(8,128)(2,1)S(1)}, u32[]{:S(2)}, u32[]{:S(2)}) collective-permute-start(bf16[192,1024]{1,0:T(8,128)(2,1)S(1)} %get-tuple-element.26), channel_id=1, source_target_pairs={{0,128},{1,129},{2,130},{3,131},{4,132},{5,133},{6,134},{7,135},{8... | collective-permute-start | bytes 1179656 | tf_op jit(solution)/shard_map/ppermute | solution.py:29
  5.0 2.6 %collective-permute-start.1 = (bf16[192,1024]{1,0:T(8,128)(2,1)S(1)}, bf16[192,1024]{1,0:T(8,128)(2,1)S(1)}, u32[]{:S(2)}, u32[]{:S(2)}) collective-permute-start(bf16[192,1024]{1,0:T(8,128)(2,1)S(1)} %get-tuple-element.27), channel_id=1, source_target_pairs={{0,1},{1,0},{2,3},{3,2},{4,5},{5,4},{6,7},{7,6},{8,9},{9,8},{10,11... | collective-permute-start | bytes 1179656 | tf_op jit(solution)/shard_map/ppermute | solution.py:29
  7.6 0.1 copy.10.bias
  7.7 4.8 %collective-permute-done.low = bf16[192,1024]{1,0:T(8,128)(2,1)S(1)} collective-permute-done((bf16[192,1024]{1,0:T(8,128)(2,1)S(1)}, bf16[192,1024]{1,0:T(8,128)(2,1)S(1)}, u32[]{:S(2)}, u32[]{:S(2)}) %collective-permute-start) | collective-permute-done | bytes 393248 | tf_op jit(solution)/shard_map/ppermute | solution.py:29
  12.6 12.0 %collective-permute-done.1.half = bf16[192,1024]{1,0:T(8,128)(2,1)S(1)} collective-permute-done((bf16[192,1024]{1,0:T(8,128)(2,1)S(1)}, bf16[192,1024]{1,0:T(8,128)(2,1)S(1)}, u32[]{:S(2)}, u32[]{:S(2)}) %collective-permute-start.1) | collective-permute-done | bytes 393248 | tf_op jit(solution)/shard_map/ppermute | solution.py:29
  24.6 2.0 %collective-permute-done.2.both = bf16[192,1024]{1,0:T(8,128)(2,1)S(1)} collective-permute-done((bf16[192,1024]{1,0:T(8,128)(2,1)S(1)}, bf16[192,1024]{1,0:T(8,128)(2,1)S(1)}, u32[]{:S(2)}, u32[]{:S(2)}) %collective-permute-start.2) | collective-permute-done | bytes 393248 | tf_op jit(solution)/shard_map/ppermute | solution.py:29
  26.6 0.6 shard_map.93.refs_0_.here
  27.3 0.4 copy-done.6
  27.7 0.1 shard_map.94.own
  27.8 0.1 collective-permute-start.5
  27.9 7.8 %collective-permute-start.3 = (bf16[2,2,192,1024]{3,2,1,0:T(8,128)(2,1)S(1)}, bf16[2,2,192,1024]{3,2,1,0:T(8,128)(2,1)}, u32[]{:S(2)}, u32[]{:S(2)}) collective-permute-start(bf16[2,2,192,1024]{3,2,1,0:T(8,128)(2,1)S(1)} %shard_map.93.refs_0_.here), channel_id=1, source_target_pairs={{0,4},{1,5},{2,126},{3,127},{4,8},{5,9},{6,2},{7,3},{8,12},{9,13},... | collective-permute-start | bytes 4718600 | tf_op jit(solution)/shard_map/ppermute | solution.py:29
  35.8 0.5 collective-permute-done.5.straight
  36.3 3.1 %collective-permute-start.6 = (bf16[96,1664]{1,0:T(8,128)(2,1)S(1)}, bf16[96,1664]{1,0:T(8,128)(2,1)S(1)}, u32[]{:S(2)}, u32[]{:S(2)}) collective-permute-start(bf16[96,1664]{1,0:T(8,128)(2,1)S(1)} %collective-permute-done.5.straight), channel_id=1, source_target_pairs={{0,2},{1,3},{2,0},{3,1},{4,6},{5,7},{6,4},{7,5},{8,10},{9,11},{10,... | collective-permute-start | bytes 958472 | tf_op jit(solution)/shard_map/ppermute | solution.py:29
  39.4 1.2 collective-permute-done.6.crossed
  40.6 0.6 shard_map.95.refs_0_.weights
  41.3 0.4 shard_map.96
  41.7 1.1 copy-done.1
  42.8 4.3 %all-to-all-start = ((bf16[4,192,1024]{2,1,0:T(8,128)(2,1)}), bf16[4,192,1024]{2,1,0:T(8,128)(2,1)}, u32[]{:S(2)}, u32[]{:S(2)}) async-start(bf16[4,192,1024]{2,1,0:T(8,128)(2,1)} %copy-done.1), calls=%async_computation | async-start | bytes 3145728 | tf_op jit(solution)/shard_map/all_to_all | solution.py:53
  47.2 0.1 broadcast_select_fusion
  47.3 0.1 concatenate.3.edge
  47.3 19.9 %collective-permute-done.3.first = bf16[2,2,192,1024]{3,2,1,0:T(8,128)(2,1)} collective-permute-done((bf16[2,2,192,1024]{3,2,1,0:T(8,128)(2,1)S(1)}, bf16[2,2,192,1024]{3,2,1,0:T(8,128)(2,1)}, u32[]{:S(2)}, u32[]{:S(2)}) %collective-permute-start.3) | collective-permute-done | bytes 1572896 | tf_op jit(solution)/shard_map/ppermute | solution.py:29
  67.2 5.7 %collective-permute-done.4.second = bf16[2,2,192,1024]{3,2,1,0:T(8,128)(2,1)} collective-permute-done((bf16[2,2,192,1024]{3,2,1,0:T(8,128)(2,1)S(1)}, bf16[2,2,192,1024]{3,2,1,0:T(8,128)(2,1)}, u32[]{:S(2)}, u32[]{:S(2)}) %collective-permute-start.4) | collective-permute-done | bytes 1572896 | tf_op jit(solution)/shard_map/ppermute | solution.py:29
  72.9 10.5 %shard_map.97 = (bf16[2,2,192,1024]{3,2,1,0:T(8,128)(2,1)S(1)}, bf16[2,2,192,1024]{3,2,1,0:T(8,128)(2,1)}, f32[2,96,1664]{2,1,0:T(8,128)S(1)}, f32[2,96,1664]{2,1,0:T(8,128)S(1)}) custom-call(s32[9]{0:T(128)S(1)} %concatenate.3.edge, bf16[2,2,192,1024]{3,2,1,0:T(8,128)(2,1)} %collective-permute-done.3.first, ...), custom_call_target="tpu_custom_call" | custom-call | flops 5435817984 | bytes 9437184 | tf_op jit(solution)/shard_map/pallas_call | solution.py:275
  83.4 3.0 %collective-permute-done.7.received = f32[2,96,1664]{2,1,0:T(8,128)S(1)} collective-permute-done((f32[2,96,1664]{2,1,0:T(8,128)S(1)}, f32[2,96,1664]{2,1,0:T(8,128)S(1)}, u32[]{:S(2)}, u32[]{:S(2)}) %collective-permute-start.7) | collective-permute-done | bytes 1277984 | tf_op jit(solution)/shard_map/ppermute | solution.py:29
  86.4 0.1 shard_map.98
  86.5 1.3 collective-permute-start.10
  87.8 1.6 collective-permute-start.8
  89.4 1.0 collective-permute-start.9
  90.5 3.4 %collective-permute-start.11 = (bf16[2,2,192,1024]{3,2,1,0:T(8,128)(2,1)}, bf16[2,2,192,1024]{3,2,1,0:T(8,128)(2,1)}, u32[]{:S(2)}, u32[]{:S(2)}) collective-permute-start(bf16[2,2,192,1024]{3,2,1,0:T(8,128)(2,1)} %get-tuple-element.36.here), channel_id=1, source_target_pairs={{0,4},{1,5},{2,126},{3,127},{4,8},{5,9},{6,2},{7,3},{8,12},{9,13},... | collective-permute-start | bytes 4718600 | tf_op jit(solution)/shard_map/ppermute | solution.py:29
  93.9 2.9 %collective-permute-done.10 = bf16[96,1664]{1,0:T(8,128)(2,1)S(1)} collective-permute-done((bf16[96,1664]{1,0:T(8,128)(2,1)S(1)}, bf16[96,1664]{1,0:T(8,128)(2,1)S(1)}, u32[]{:S(2)}, u32[]{:S(2)}) %collective-permute-start.10) | collective-permute-done | bytes 319520 | tf_op jit(solution)/shard_map/ppermute | solution.py:29
  96.8 0.1 collective-permute-done.8
  96.9 7.7 %collective-permute-done.9 = bf16[96,1664]{1,0:T(8,128)(2,1)S(1)} collective-permute-done((bf16[96,1664]{1,0:T(8,128)(2,1)S(1)}, bf16[96,1664]{1,0:T(8,128)(2,1)S(1)}, u32[]{:S(2)}, u32[]{:S(2)}) %collective-permute-start.9) | collective-permute-done | bytes 319520 | tf_op jit(solution)/shard_map/ppermute | solution.py:29
  104.6 0.2 add_add_fusion
  104.8 3.1 %shard_map.99 = (bf16[2,2,192,1024]{3,2,1,0:T(8,128)(2,1)}, bf16[384,1152]{1,0:T(8,128)(2,1)S(1)}) custom-call(s32[9]{0:T(128)S(1)} %concatenate.3.edge, bf16[2,2,192,1024]{3,2,1,0:T(8,128)(2,1)S(1)} %shard_map.93.refs_0_.here, bf16[2,2,192,1024]{3,2,1,0:T(8,128)(2,1)S(1)} %get-tuple-element.29.act, bf16[384,1664]{1,0:T(8,128)(2,1)S(1)} %shard_map.95.refs_0_.weights, ...), custom_call_target="tpu_custom_call" | custom-call | flops 603979776 | bytes 4718592 | tf_op jit(solution)/shard_map/pallas_call | solution.py:307
  108.0 0.9 copy-done.4
  108.9 3.7 %all-to-all-start.1 = ((bf16[4,192,1024]{2,1,0:T(8,128)(2,1)}), bf16[4,192,1024]{2,1,0:T(8,128)(2,1)S(1)}, u32[]{:S(2)}, u32[]{:S(2)}) async-start(bf16[4,192,1024]{2,1,0:T(8,128)(2,1)} %bitcast.34), calls=%async_computation.1 | async-start | bytes 3145728 | tf_op jit(solution)/shard_map/all_to_all | solution.py:53
  112.6 0.7 fusion.3
  113.3 0.2 collective-permute-start.14
  113.5 3.4 %collective-permute-start.15 = (bf16[24,1664]{1,0:T(8,128)(2,1)}, bf16[24,1664]{1,0:T(8,128)(2,1)S(1)}, u32[]{:S(2)}, u32[]{:S(2)}) collective-permute-start(bf16[24,1664]{1,0:T(8,128)(2,1)} %get-tuple-element.46), channel_id=1, source_target_pairs={{0,48},{1,49},{2,50},{3,51},{4,52},{5,53},{6,54},{7,55},{8,56},{9,... | collective-permute-start | bytes 239624 | tf_op jit(solution)/shard_map/ppermute | solution.py:29
  116.9 8.8 %collective-permute-done.11.first = bf16[2,2,192,1024]{3,2,1,0:T(8,128)(2,1)} collective-permute-done((bf16[2,2,192,1024]{3,2,1,0:T(8,128)(2,1)}, bf16[2,2,192,1024]{3,2,1,0:T(8,128)(2,1)}, u32[]{:S(2)}, u32[]{:S(2)}) %collective-permute-start.11) | collective-permute-done | bytes 1572896 | tf_op jit(solution)/shard_map/ppermute | solution.py:29
  125.7 6.0 %collective-permute-done.12.second = bf16[2,2,192,1024]{3,2,1,0:T(8,128)(2,1)} collective-permute-done((bf16[2,2,192,1024]{3,2,1,0:T(8,128)(2,1)}, bf16[2,2,192,1024]{3,2,1,0:T(8,128)(2,1)}, u32[]{:S(2)}, u32[]{:S(2)}) %collective-permute-start.12) | collective-permute-done | bytes 1572896 | tf_op jit(solution)/shard_map/ppermute | solution.py:29
  131.7 0.4 all-to-all-done.1.source.refs_0_
  132.1 5.8 %shard_map.101 = (bf16[2,2,192,1024]{3,2,1,0:T(8,128)(2,1)}, f32[8,128]{1,0:T(8,128)S(1)}) custom-call(s32[9]{0:T(128)S(1)} %concatenate.3.edge, bf16[2,2,192,1024]{3,2,1,0:T(8,128)(2,1)} %collective-permute-done.11.first, bf16[2,2,192,1024]{3,2,1,0:T(8,128)(2,1)} %get-tuple-element.36.here, bf16[2,2,192,1024]{3,2,1,0:T(8,128)(2,1)} %collective-permute-done.12.second, ...), custom_call_target="tpu_custom_call" | custom-call | flops 1811939328 | bytes 7864320 | tf_op jit(solution)/shard_map/pallas_call | solution.py:338
  137.9 3.6 %all-to-all-start.2 = ((bf16[4,192,1024]{2,1,0:T(8,128)(2,1)}), bf16[4,192,1024]{2,1,0:T(8,128)(2,1)S(1)}, u32[]{:S(2)}, u32[]{:S(2)}) async-start(bf16[4,192,1024]{2,1,0:T(8,128)(2,1)} %bitcast.33), calls=%async_computation.2 | async-start | bytes 3145728 | tf_op jit(solution)/shard_map/all_to_all | solution.py:53
  141.5 1.0 fusion.2
  142.5 3.5 %collective-permute-start.16 = (bf16[24,1664]{1,0:T(8,128)(2,1)S(1)}, bf16[24,1664]{1,0:T(8,128)(2,1)S(1)}, u32[]{:S(2)}, u32[]{:S(2)}) collective-permute-start(bf16[24,1664]{1,0:T(8,128)(2,1)S(1)} %fusion.2), channel_id=1, source_target_pairs={{0,64},{1,65},{2,66},{3,67},{4,68},{5,69},{6,70},{7,71},{8,72},{9,... | collective-permute-start | bytes 239624 | tf_op jit(solution)/shard_map/ppermute | solution.py:29
  146.0 3.9 %collective-permute-done.16 = bf16[24,1664]{1,0:T(8,128)(2,1)S(1)} collective-permute-done((bf16[24,1664]{1,0:T(8,128)(2,1)S(1)}, bf16[24,1664]{1,0:T(8,128)(2,1)S(1)}, u32[]{:S(2)}, u32[]{:S(2)}) %collective-permute-start.16) | collective-permute-done | bytes 79904 | tf_op jit(solution)/shard_map/ppermute | solution.py:29
  149.9 0.1 collective-permute-start.17
  150.0 0.3 collective-permute-start.18
  150.3 3.5 %collective-permute-start.19 = (bf16[24,1664]{1,0:T(8,128)(2,1)S(1)}, bf16[24,1664]{1,0:T(8,128)(2,1)S(1)}, u32[]{:S(2)}, u32[]{:S(2)}) collective-permute-start(bf16[24,1664]{1,0:T(8,128)(2,1)S(1)} %shard_map.103), channel_id=1, source_target_pairs={{0,12},{1,13},{2,14},{3,15},{4,8},{5,9},{6,10},{7,11},{8,4},{9,5},... | collective-permute-start | bytes 239624 | tf_op jit(solution)/shard_map/ppermute | solution.py:29
  153.9 1.0 collective-permute-done.18
  154.9 1.1 collective-permute-done.19
  156.1 0.1 collective-permute-start.20
  156.2 2.1 %collective-permute-start.21 = (bf16[24,1664]{1,0:T(8,128)(2,1)S(1)}, bf16[24,1664]{1,0:T(8,128)(2,1)S(1)}, u32[]{:S(2)}, u32[]{:S(2)}) collective-permute-start(bf16[24,1664]{1,0:T(8,128)(2,1)S(1)} %multiply_convert_fusion.refs_0_), channel_id=1, source_target_pairs={{0,32},{1,33},{2,34},{3,35},{4,36},{5,37},{6,38},{7,39},{8,40},{9,... | collective-permute-start | bytes 239624 | tf_op jit(solution)/shard_map/ppermute | solution.py:29
  158.3 1.4 collective-permute-start.22
  159.7 0.4 all-to-all-done.2.source
  160.1 1.2 shard_map.102
  161.3 2.0 %collective-permute-done.22.refs_3_ = bf16[24,1664]{1,0:T(8,128)(2,1)S(1)} collective-permute-done((bf16[24,1664]{1,0:T(8,128)(2,1)S(1)}, bf16[24,1664]{1,0:T(8,128)(2,1)S(1)}, u32[]{:S(2)}, u32[]{:S(2)}) %collective-permute-start.22) | collective-permute-done | bytes 79904 | tf_op jit(solution)/shard_map/ppermute | solution.py:29
  163.4 7.5 %collective-permute-start.23 = (bf16[4,24,1664]{2,1,0:T(8,128)(2,1)S(1)}, bf16[4,24,1664]{2,1,0:T(8,128)(2,1)S(1)}, u32[]{:S(2)}, u32[]{:S(2)}) collective-permute-start(bf16[4,24,1664]{2,1,0:T(8,128)(2,1)S(1)} %shard_map.104.own), channel_id=1, source_target_pairs={{0,2},{1,3},{2,0},{3,1},{4,6},{5,7},{6,4},{7,5},{8,10},{9,11},{10,... | collective-permute-start | bytes 958472 | tf_op jit(solution)/shard_map/ppermute | solution.py:29
  170.9 1.2 shard_map.100
  172.1 1.1 shard_map.105
  173.2 0.7 slice_reduce_fusion
  (34 shorter events, 0.4 us)
Async XLA Ops:
  0.7 1.4 copy-start
  2.1 5.5 %copy-start.8 = (f32[192]{0:T(256)S(1)}, f32[192]{0:T(256)}, u32[]{:S(2)}) copy-start(f32[192]{0:T(256)} %param.7) | copy-start | bytes 2308
  2.8 9.8 %collective-permute-start = (bf16[192,1024]{1,0:T(8,128)(2,1)S(1)}, bf16[192,1024]{1,0:T(8,128)(2,1)S(1)}, u32[]{:S(2)}, u32[]{:S(2)}) collective-permute-start(bf16[192,1024]{1,0:T(8,128)(2,1)S(1)} %get-tuple-element.26), channel_id=1, source_target_pairs={{0,128},{1,129},{2,130},{3,131},{4,132},{5,133},{6,134},{7,135},{8... | collective-permute-start | bytes 1179656 | tf_op jit(solution)/shard_map/ppermute | solution.py:29
  5.0 19.6 %collective-permute-start.1 = (bf16[192,1024]{1,0:T(8,128)(2,1)S(1)}, bf16[192,1024]{1,0:T(8,128)(2,1)S(1)}, u32[]{:S(2)}, u32[]{:S(2)}) collective-permute-start(bf16[192,1024]{1,0:T(8,128)(2,1)S(1)} %get-tuple-element.27), channel_id=1, source_target_pairs={{0,1},{1,0},{2,3},{3,2},{4,5},{5,4},{6,7},{7,6},{8,9},{9,8},{10,11... | collective-permute-start | bytes 1179656 | tf_op jit(solution)/shard_map/ppermute | solution.py:29
  7.6 19.0 %collective-permute-start.2 = (bf16[192,1024]{1,0:T(8,128)(2,1)S(1)}, bf16[192,1024]{1,0:T(8,128)(2,1)S(1)}, u32[]{:S(2)}, u32[]{:S(2)}) collective-permute-start(bf16[192,1024]{1,0:T(8,128)(2,1)S(1)} %get-tuple-element.28), channel_id=1, source_target_pairs={{0,129},{1,128},{2,131},{3,130},{4,133},{5,132},{6,135},{7,134},{8... | collective-permute-start | bytes 1179656 | tf_op jit(solution)/shard_map/ppermute | solution.py:29
  26.6 1.0 copy-start.6
  26.6 1.0 copy-start.7
  27.8 13.5 %copy-start.3 = (bf16[2,192,2048]{2,1,0:T(8,128)(2,1)S(1)}, bf16[2,192,2048]{2,1,0:T(8,128)(2,1)}, u32[]{:S(2)}) copy-start(bf16[2,192,2048]{2,1,0:T(8,128)(2,1)} %source.1) | copy-start | bytes 4718596
  27.8 8.5 %collective-permute-start.5 = (bf16[96,1664]{1,0:T(8,128)(2,1)S(1)}, bf16[96,1664]{1,0:T(8,128)(2,1)S(1)}, u32[]{:S(2)}, u32[]{:S(2)}) collective-permute-start(bf16[96,1664]{1,0:T(8,128)(2,1)S(1)} %dynamic-slice_bitcast_fusion), channel_id=1, source_target_pairs={{0,1},{1,0},{2,3},{3,2},{4,5},{5,4},{6,7},{7,6},{8,9},{9,8},{10,11... | collective-permute-start | bytes 958472 | tf_op jit(solution)/shard_map/ppermute | solution.py:29
  27.9 39.3 %collective-permute-start.3 = (bf16[2,2,192,1024]{3,2,1,0:T(8,128)(2,1)S(1)}, bf16[2,2,192,1024]{3,2,1,0:T(8,128)(2,1)}, u32[]{:S(2)}, u32[]{:S(2)}) collective-permute-start(bf16[2,2,192,1024]{3,2,1,0:T(8,128)(2,1)S(1)} %shard_map.93.refs_0_.here), channel_id=1, source_target_pairs={{0,4},{1,5},{2,126},{3,127},{4,8},{5,9},{6,2},{7,3},{8,12},{9,13},... | collective-permute-start | bytes 4718600 | tf_op jit(solution)/shard_map/ppermute | solution.py:29
  35.8 37.1 %collective-permute-start.4 = (bf16[2,2,192,1024]{3,2,1,0:T(8,128)(2,1)S(1)}, bf16[2,2,192,1024]{3,2,1,0:T(8,128)(2,1)}, u32[]{:S(2)}, u32[]{:S(2)}) collective-permute-start(bf16[2,2,192,1024]{3,2,1,0:T(8,128)(2,1)S(1)} %shard_map.93.refs_0_.here), channel_id=1, source_target_pairs={{0,124},{1,125},{2,6},{3,7},{4,0},{5,1},{6,10},{7,11},{8,4},{9,5},... | collective-permute-start | bytes 4718600 | tf_op jit(solution)/shard_map/ppermute | solution.py:29
  36.3 4.3 %collective-permute-start.6 = (bf16[96,1664]{1,0:T(8,128)(2,1)S(1)}, bf16[96,1664]{1,0:T(8,128)(2,1)S(1)}, u32[]{:S(2)}, u32[]{:S(2)}) collective-permute-start(bf16[96,1664]{1,0:T(8,128)(2,1)S(1)} %collective-permute-done.5.straight), channel_id=1, source_target_pairs={{0,2},{1,3},{2,0},{3,1},{4,6},{5,7},{6,4},{7,5},{8,10},{9,11},{10,... | collective-permute-start | bytes 958472 | tf_op jit(solution)/shard_map/ppermute | solution.py:29
  41.7 1.1 copy-start.1
  42.8 30.1 %all-to-all-start = ((bf16[4,192,1024]{2,1,0:T(8,128)(2,1)}), bf16[4,192,1024]{2,1,0:T(8,128)(2,1)}, u32[]{:S(2)}, u32[]{:S(2)}) async-start(bf16[4,192,1024]{2,1,0:T(8,128)(2,1)} %copy-done.1), calls=%async_computation | async-start | bytes 3145728 | tf_op jit(solution)/shard_map/all_to_all | solution.py:53
  83.4 3.0 %collective-permute-start.7 = (f32[2,96,1664]{2,1,0:T(8,128)S(1)}, f32[2,96,1664]{2,1,0:T(8,128)S(1)}, u32[]{:S(2)}, u32[]{:S(2)}) collective-permute-start(f32[2,96,1664]{2,1,0:T(8,128)S(1)} %get-tuple-element.31), channel_id=1, source_target_pairs={{0,2},{1,3},{2,0},{3,1},{4,6},{5,7},{6,4},{7,5},{8,10},{9,11},{10,... | collective-permute-start | bytes 3833864 | tf_op jit(solution)/shard_map/ppermute | solution.py:29
  86.5 10.3 %collective-permute-start.10 = (bf16[96,1664]{1,0:T(8,128)(2,1)S(1)}, bf16[96,1664]{1,0:T(8,128)(2,1)S(1)}, u32[]{:S(2)}, u32[]{:S(2)}) collective-permute-start(bf16[96,1664]{1,0:T(8,128)(2,1)S(1)} %get-tuple-element.33), channel_id=1, source_target_pairs={{0,129},{1,128},{2,131},{3,130},{4,133},{5,132},{6,135},{7,134},{8... | collective-permute-start | bytes 958472 | tf_op jit(solution)/shard_map/ppermute | solution.py:29
  87.8 9.1 %collective-permute-start.8 = (bf16[96,1664]{1,0:T(8,128)(2,1)S(1)}, bf16[96,1664]{1,0:T(8,128)(2,1)S(1)}, u32[]{:S(2)}, u32[]{:S(2)}) collective-permute-start(bf16[96,1664]{1,0:T(8,128)(2,1)S(1)} %get-tuple-element.32), channel_id=1, source_target_pairs={{0,128},{1,129},{2,130},{3,131},{4,132},{5,133},{6,134},{7,135},{8... | collective-permute-start | bytes 958472 | tf_op jit(solution)/shard_map/ppermute | solution.py:29
  89.4 15.2 %collective-permute-start.9 = (bf16[96,1664]{1,0:T(8,128)(2,1)S(1)}, bf16[96,1664]{1,0:T(8,128)(2,1)S(1)}, u32[]{:S(2)}, u32[]{:S(2)}) collective-permute-start(bf16[96,1664]{1,0:T(8,128)(2,1)S(1)} %get-tuple-element.33), channel_id=1, source_target_pairs={{0,1},{1,0},{2,3},{3,2},{4,5},{5,4},{6,7},{7,6},{8,9},{9,8},{10,11... | collective-permute-start | bytes 958472 | tf_op jit(solution)/shard_map/ppermute | solution.py:29
  90.5 35.2 %collective-permute-start.11 = (bf16[2,2,192,1024]{3,2,1,0:T(8,128)(2,1)}, bf16[2,2,192,1024]{3,2,1,0:T(8,128)(2,1)}, u32[]{:S(2)}, u32[]{:S(2)}) collective-permute-start(bf16[2,2,192,1024]{3,2,1,0:T(8,128)(2,1)} %get-tuple-element.36.here), channel_id=1, source_target_pairs={{0,4},{1,5},{2,126},{3,127},{4,8},{5,9},{6,2},{7,3},{8,12},{9,13},... | collective-permute-start | bytes 4718600 | tf_op jit(solution)/shard_map/ppermute | solution.py:29
  93.9 37.8 %collective-permute-start.12 = (bf16[2,2,192,1024]{3,2,1,0:T(8,128)(2,1)}, bf16[2,2,192,1024]{3,2,1,0:T(8,128)(2,1)}, u32[]{:S(2)}, u32[]{:S(2)}) collective-permute-start(bf16[2,2,192,1024]{3,2,1,0:T(8,128)(2,1)} %get-tuple-element.36.here), channel_id=1, source_target_pairs={{0,124},{1,125},{2,6},{3,7},{4,0},{5,1},{6,10},{7,11},{8,4},{9,5},... | collective-permute-start | bytes 4718600 | tf_op jit(solution)/shard_map/ppermute | solution.py:29
  104.8 7.8 %copy-start.2 = (f32[96,1664]{1,0:T(8,128)}, f32[96,1664]{1,0:T(8,128)S(1)}, u32[]{:S(2)}) copy-start(f32[96,1664]{1,0:T(8,128)S(1)} %add_add_fusion) | copy-start | bytes 1916932
  107.9 0.9 copy-start.4
  108.9 23.2 %copy-start.5 = (bf16[384,1152]{1,0:T(8,128)(2,1)S(1)}, bf16[384,1152]{1,0:T(8,128)(2,1)}, u32[]{:S(2)}) copy-start(bf16[384,1152]{1,0:T(8,128)(2,1)} %copy-done.4) | copy-start | bytes 2654212
  108.9 23.2 %all-to-all-start.1 = ((bf16[4,192,1024]{2,1,0:T(8,128)(2,1)}), bf16[4,192,1024]{2,1,0:T(8,128)(2,1)S(1)}, u32[]{:S(2)}, u32[]{:S(2)}) async-start(bf16[4,192,1024]{2,1,0:T(8,128)(2,1)} %bitcast.34), calls=%async_computation.1 | async-start | bytes 3145728 | tf_op jit(solution)/shard_map/all_to_all | solution.py:53
  113.3 28.2 %collective-permute-start.13 = (bf16[24,1664]{1,0:T(8,128)(2,1)}, bf16[24,1664]{1,0:T(8,128)(2,1)S(1)}, u32[]{:S(2)}, u32[]{:S(2)}) collective-permute-start(bf16[24,1664]{1,0:T(8,128)(2,1)} %get-tuple-element.45), channel_id=1, source_target_pairs={{0,16},{1,17},{2,18},{3,19},{4,20},{5,21},{6,22},{7,23},{8,24},{9,... | collective-permute-start | bytes 239624 | tf_op jit(solution)/shard_map/ppermute | solution.py:29
  113.3 28.2 %collective-permute-start.14 = (bf16[24,1664]{1,0:T(8,128)(2,1)}, bf16[24,1664]{1,0:T(8,128)(2,1)S(1)}, u32[]{:S(2)}, u32[]{:S(2)}) collective-permute-start(bf16[24,1664]{1,0:T(8,128)(2,1)} %get-tuple-element.47), channel_id=1, source_target_pairs={{0,32},{1,33},{2,34},{3,35},{4,36},{5,37},{6,38},{7,39},{8,40},{9,... | collective-permute-start | bytes 239624 | tf_op jit(solution)/shard_map/ppermute | solution.py:29
  113.5 28.1 %collective-permute-start.15 = (bf16[24,1664]{1,0:T(8,128)(2,1)}, bf16[24,1664]{1,0:T(8,128)(2,1)S(1)}, u32[]{:S(2)}, u32[]{:S(2)}) collective-permute-start(bf16[24,1664]{1,0:T(8,128)(2,1)} %get-tuple-element.46), channel_id=1, source_target_pairs={{0,48},{1,49},{2,50},{3,51},{4,52},{5,53},{6,54},{7,55},{8,56},{9,... | collective-permute-start | bytes 239624 | tf_op jit(solution)/shard_map/ppermute | solution.py:29
  137.9 22.2 %all-to-all-start.2 = ((bf16[4,192,1024]{2,1,0:T(8,128)(2,1)}), bf16[4,192,1024]{2,1,0:T(8,128)(2,1)S(1)}, u32[]{:S(2)}, u32[]{:S(2)}) async-start(bf16[4,192,1024]{2,1,0:T(8,128)(2,1)} %bitcast.33), calls=%async_computation.2 | async-start | bytes 3145728 | tf_op jit(solution)/shard_map/all_to_all | solution.py:53
  142.5 7.4 %collective-permute-start.16 = (bf16[24,1664]{1,0:T(8,128)(2,1)S(1)}, bf16[24,1664]{1,0:T(8,128)(2,1)S(1)}, u32[]{:S(2)}, u32[]{:S(2)}) collective-permute-start(bf16[24,1664]{1,0:T(8,128)(2,1)S(1)} %fusion.2), channel_id=1, source_target_pairs={{0,64},{1,65},{2,66},{3,67},{4,68},{5,69},{6,70},{7,71},{8,72},{9,... | collective-permute-start | bytes 239624 | tf_op jit(solution)/shard_map/ppermute | solution.py:29
  149.9 3.9 %collective-permute-start.17 = (bf16[24,1664]{1,0:T(8,128)(2,1)S(1)}, bf16[24,1664]{1,0:T(8,128)(2,1)S(1)}, u32[]{:S(2)}, u32[]{:S(2)}) collective-permute-start(bf16[24,1664]{1,0:T(8,128)(2,1)S(1)} %shard_map.103), channel_id=1, source_target_pairs={{0,4},{1,5},{2,6},{3,7},{4,0},{5,1},{6,2},{7,3},{8,12},{9,13},{10,... | collective-permute-start | bytes 239624 | tf_op jit(solution)/shard_map/ppermute | solution.py:29
  150.0 4.9 %collective-permute-start.18 = (bf16[24,1664]{1,0:T(8,128)(2,1)S(1)}, bf16[24,1664]{1,0:T(8,128)(2,1)S(1)}, u32[]{:S(2)}, u32[]{:S(2)}) collective-permute-start(bf16[24,1664]{1,0:T(8,128)(2,1)S(1)} %shard_map.103), channel_id=1, source_target_pairs={{0,8},{1,9},{2,10},{3,11},{4,12},{5,13},{6,14},{7,15},{8,0},{9,1},... | collective-permute-start | bytes 239624 | tf_op jit(solution)/shard_map/ppermute | solution.py:29
  150.3 5.7 %collective-permute-start.19 = (bf16[24,1664]{1,0:T(8,128)(2,1)S(1)}, bf16[24,1664]{1,0:T(8,128)(2,1)S(1)}, u32[]{:S(2)}, u32[]{:S(2)}) collective-permute-start(bf16[24,1664]{1,0:T(8,128)(2,1)S(1)} %shard_map.103), channel_id=1, source_target_pairs={{0,12},{1,13},{2,14},{3,15},{4,8},{5,9},{6,10},{7,11},{8,4},{9,5},... | collective-permute-start | bytes 239624 | tf_op jit(solution)/shard_map/ppermute | solution.py:29
  156.1 5.2 %collective-permute-start.20 = (bf16[24,1664]{1,0:T(8,128)(2,1)S(1)}, bf16[24,1664]{1,0:T(8,128)(2,1)S(1)}, u32[]{:S(2)}, u32[]{:S(2)}) collective-permute-start(bf16[24,1664]{1,0:T(8,128)(2,1)S(1)} %multiply_convert_fusion.refs_0_), channel_id=1, source_target_pairs={{0,16},{1,17},{2,18},{3,19},{4,20},{5,21},{6,22},{7,23},{8,24},{9,... | collective-permute-start | bytes 239624 | tf_op jit(solution)/shard_map/ppermute | solution.py:29
  156.2 5.1 %collective-permute-start.21 = (bf16[24,1664]{1,0:T(8,128)(2,1)S(1)}, bf16[24,1664]{1,0:T(8,128)(2,1)S(1)}, u32[]{:S(2)}, u32[]{:S(2)}) collective-permute-start(bf16[24,1664]{1,0:T(8,128)(2,1)S(1)} %multiply_convert_fusion.refs_0_), channel_id=1, source_target_pairs={{0,32},{1,33},{2,34},{3,35},{4,36},{5,37},{6,38},{7,39},{8,40},{9,... | collective-permute-start | bytes 239624 | tf_op jit(solution)/shard_map/ppermute | solution.py:29
  158.3 5.1 %collective-permute-start.22 = (bf16[24,1664]{1,0:T(8,128)(2,1)S(1)}, bf16[24,1664]{1,0:T(8,128)(2,1)S(1)}, u32[]{:S(2)}, u32[]{:S(2)}) collective-permute-start(bf16[24,1664]{1,0:T(8,128)(2,1)S(1)} %multiply_convert_fusion.refs_0_), channel_id=1, source_target_pairs={{0,48},{1,49},{2,50},{3,51},{4,52},{5,53},{6,54},{7,55},{8,56},{9,... | collective-permute-start | bytes 239624 | tf_op jit(solution)/shard_map/ppermute | solution.py:29
  163.4 8.8 %collective-permute-start.23 = (bf16[4,24,1664]{2,1,0:T(8,128)(2,1)S(1)}, bf16[4,24,1664]{2,1,0:T(8,128)(2,1)S(1)}, u32[]{:S(2)}, u32[]{:S(2)}) collective-permute-start(bf16[4,24,1664]{2,1,0:T(8,128)(2,1)S(1)} %shard_map.104.own), channel_id=1, source_target_pairs={{0,2},{1,3},{2,0},{3,1},{4,6},{5,7},{6,4},{7,5},{8,10},{9,11},{10,... | collective-permute-start | bytes 958472 | tf_op jit(solution)/shard_map/ppermute | solution.py:29
